TPU v7x, 512 devices: a whole 4x4x16 slice. The times are simulated.
512 devices in a mesh: row: 16 (over z), col: 32 (over y, x, core).
Axes of the slice: x: 4, y: 4, z: 16, core: 2. Of those that a mesh axis runs over, the one named last changes fastest.
Arguments:
- dosage_words: int32 [8192, 8192], P('row', 'col'), may hold values from 0 to 2730, as said below
- sample_weight: float32 [8192], P('row'), may hold values from 0.3 to 3
- variant_weight: float32 [49152], P('col'), may hold values from 0.7 to 12.6, as said below
- omega: bfloat16 [49152, 128], P('col'), may hold values from -6 to 6
Outputs:
- basis: float32 [8192, 128], P(('row', 'col'))
- right_basis: float32 [49152, 128], P('col')
- projection: float32 [49152, 128], P('col', 'row')
Inputs may be any that keep to these rules, and one draw needn't show every extreme that they name: `dosage_words`: each word holds 6 dosages of 0, 1 or 2 in two bits each, laid out as the first step says. `variant_weight`: positive weights of the variants.
All inputs are finite; a program needn't handle non-finite values.
Results may differ from a plain program's by a relative error of at most 0.024.
Values may be sent and summed in bfloat16 or wider, within the bound.
No kernel may reach another device: no remote copies, remote signals or barrier semaphores. Data moves between devices by JAX's collectives and lax.ppermute only.
A program may use at most 64 MiB of HBM per device.

v0:
```python
import math

import jax
import jax.numpy as jnp
from jax import lax
from jax.sharding import PartitionSpec as P

EPSILON = 1e-05
CONTRACT_ROWS = (((0,), (0,)), ((), ()))


def unpack(words):
    shifts = 2 * jnp.arange(6, dtype=jnp.int32)
    parts = jnp.bitwise_and(jnp.right_shift(words[None, :, :], shifts[:, None, None]), 3)
    return (
        jnp.transpose(parts, (1, 0, 2))
        .reshape(words.shape[0], 6 * words.shape[1])
        .astype(jnp.float32)
    )


def orthonormal(panel, gram_sum):
    lower = jnp.linalg.cholesky(gram_sum)
    identity = jnp.eye(gram_sum.shape[0], dtype=jnp.float32)
    inverse = lax.linalg.triangular_solve(lower, identity, left_side=True, lower=True)
    return jnp.dot(panel, inverse.T, precision=lax.Precision.HIGHEST)


def local_gram(panel):
    return jnp.dot(panel.T, panel, precision=lax.Precision.HIGHEST)


def per_device(dosage_words, sample_weight, variant_weight, omega):
    dosage = unpack(dosage_words)
    rows_local = dosage.shape[0]
    rows_all = rows_local * lax.axis_size("row")
    cols_all = dosage.shape[1] * lax.axis_size("col")
    totals, squares = lax.psum((jnp.sum(dosage, axis=0), jnp.sum(dosage * dosage, axis=0)), "row")
    column_mean = totals / rows_all
    column_scale = lax.rsqrt(squares / rows_all - column_mean * column_mean + EPSILON)
    matrix = (
        (dosage - column_mean) * column_scale * sample_weight[:, None] * variant_weight
    ).astype(jnp.bfloat16)

    def sketch(panel_in):
        tall_part = lax.psum_scatter(
            jnp.dot(matrix, panel_in, preferred_element_type=jnp.float32),
            "col",
            scatter_dimension=0,
            tiled=True,
        )
        gram_sum = lax.psum(local_gram(tall_part), ("row", "col"))
        return orthonormal(tall_part, gram_sum)

    def project(basis_half):
        return lax.dot_general(
            matrix,
            lax.all_gather(basis_half, "col", axis=0, tiled=True),
            CONTRACT_ROWS,
            preferred_element_type=jnp.float32,
        )

    first = sketch(omega).astype(jnp.bfloat16)
    partial_back = project(first)
    back = lax.psum(partial_back.astype(jnp.bfloat16), "row").astype(jnp.float32)
    wide_sum = lax.psum(local_gram(back).astype(jnp.bfloat16), "col").astype(jnp.float32)
    right_full = orthonormal(back, wide_sum)
    right = right_full.astype(jnp.bfloat16)
    second = sketch(right)
    projection = lax.psum_scatter(
        project(second.astype(jnp.bfloat16)).astype(jnp.bfloat16),
        "row",
        scatter_dimension=1,
        tiled=True,
    ).astype(jnp.float32)
    return (second * math.sqrt(rows_all), right_full * math.sqrt(cols_all), projection)


def solution(mesh):
    in_specs = (P("row", "col"), P("row"), P("col"), P("col", None))
    out_specs = (P(("row", "col"), None), P("col", None), P("col", "row"))
    return jax.shard_map(
        per_device, mesh=mesh, in_specs=in_specs, out_specs=out_specs, check_vma=False
    )
```

profile of v0, /device:TPU:2, one launch (start us, length us, event | category | flops | bytes accessed | tf_op | source)
XLA Modules:
  0.0 1600.8 jit_solution(2754105105404131142)
XLA Ops:
  7.2 0.0 copy-start
  7.2 0.0 copy-start.2
  7.2 0.0 copy-start.3
  7.2 0.0 reduce-scatter.4.cloned.1.call-start
  7.3 0.1 shift_right_arithmetic.29
  7.3 1.2 copy.13
  8.6 0.8 convert_reduce_fusion
  9.4 62.0 %all-reduce = (f32[1536]{0:T(1024)S(1)}, f32[1536]{0:T(1024)S(1)}) all-reduce(f32[1536]{0:T(1024)S(1)} %reduce_sum.25, f32[1536]{0:T(1024)S(1)} %reduce_sum.23), channel_id=1, replica_groups=mesh['row'=16,'col'=32] {'row'}, use_global_device_ids=true, to_apply=%region_3.0 | all-reduce | flops 3072 | bytes 24576 | tf_op jit(solution)/shard_map/psum | solution.py:38
  71.5 0.0 copy-done.2
  71.5 0.0 copy-done.3
  71.5 1.5 fusion.6
  73.0 0.0 copy-done
  73.0 1.3 fusion.25
  74.3 0.0 reduce-scatter.4.cloned.1.call-update
  74.3 0.0 all-reduce.5.cloned.1.call-start
  74.4 95.9 %reduce-scatter.4.cloned.1.call-done = f32[16,128]{1,0:T(8,128)} async-done(((f32[512,128]{1,0:T(8,128)}), f32[16,128]{1,0:T(8,128)}) %reduce-scatter.4.cloned.1.call-update) | async-done | bytes 8208 | tf_op jit(solution)/shard_map/reduce_scatter | solution.py:46
  170.2 1.7 fusion.26
  171.9 0.0 all-reduce.5.cloned.1.call-update
  172.0 0.0 all-reduce.7.cloned.1.call-start
  172.0 443.7 %all-reduce.5.cloned.1.call-done = f32[128,128]{0,1:T(8,128)} async-done(((f32[128,128]{0,1:T(8,128)}), f32[128,128]{0,1:T(8,128)}) %all-reduce.5.cloned.1.call-update) | async-done | bytes 65552 | tf_op jit(solution)/shard_map/psum | solution.py:52
  615.7 0.9 copy.15
  616.6 0.9 fusion.23
  617.5 11.7 cholesky.59
  629.2 0.6 compare_reduce_fusion.2
  629.9 0.7 fusion.15
  630.5 9.8 custom-call.7
  640.4 0.3 fusion.13
  640.7 0.9 convolution_convert_fusion.3
  641.5 24.3 %all_gather.6 = bf16[512,128]{1,0:T(8,128)(2,1)S(1)} all-gather(bf16[16,128]{1,0:T(8,128)(2,1)S(1)} %convolution_convert_fusion.3), channel_id=1, replica_groups=mesh['row'=16,'col'=32] {'col'}, dimensions={0}, use_global_device_ids=true | all-gather | bytes 135168 | tf_op jit(solution)/shard_map/all_gather | solution.py:58
  665.8 1.3 convolution_convert_fusion.1
  667.1 0.0 all-reduce.7.cloned.1.call-update
  667.2 0.0 reduce-scatter.6.cloned.1.call-start
  667.2 126.3 %all-reduce.7.cloned.1.call-done = bf16[1536,128]{1,0:T(8,128)(2,1)} async-done(((bf16[1536,128]{1,0:T(8,128)(2,1)}), bf16[1536,128]{1,0:T(8,128)(2,1)}) %all-reduce.7.cloned.1.call-update) | async-done | bytes 393232 | tf_op jit(solution)/shard_map/psum | solution.py:65
  793.6 1.5 convolution_convert_fusion.2
  795.0 119.0 %psum.46 = bf16[128,128]{0,1:T(8,128)(2,1)S(1)} all-reduce(bf16[128,128]{0,1:T(8,128)(2,1)S(1)} %convolution_convert_fusion.2), channel_id=1, replica_groups=mesh['row'=16,'col'=32] {'col'}, use_global_device_ids=true, to_apply=%region_9.12 | all-reduce | flops 16384 | bytes 65536 | tf_op jit(solution)/shard_map/psum | solution.py:66
  914.0 0.1 copy.17
  914.1 11.7 cholesky.70
  925.9 0.6 compare_reduce_fusion.1
  926.5 0.7 fusion.16
  927.2 9.8 custom-call.8
  937.0 0.3 fusion.11
  937.3 0.0 copy-done.1
  937.3 1.4 broadcast_multiply_fusion
  938.7 1.3 fusion.7
  940.0 0.0 reduce-scatter.6.cloned.1.call-update
  940.0 0.0 all-reduce.9.cloned.1.call-start
  940.1 96.7 %reduce-scatter.6.cloned.1.call-done = f32[16,128]{1,0:T(8,128)} async-done(((f32[512,128]{1,0:T(8,128)}), f32[16,128]{1,0:T(8,128)}) %reduce-scatter.6.cloned.1.call-update) | async-done | bytes 8208 | tf_op jit(solution)/shard_map/reduce_scatter | solution.py:46
  1036.8 1.7 fusion.27
  1038.4 0.0 all-reduce.9.cloned.1.call-update
  1038.5 0.3 reduce-scatter.8.cloned.1.call-start
  1038.7 442.6 %all-reduce.9.cloned.1.call-done = f32[128,128]{0,1:T(8,128)} async-done(((f32[128,128]{0,1:T(8,128)}), f32[128,128]{0,1:T(8,128)}) %all-reduce.9.cloned.1.call-update) | async-done | bytes 65552 | tf_op jit(solution)/shard_map/psum | solution.py:52
  1481.3 0.9 copy.19
  1482.3 0.9 fusion.19
  1483.1 11.7 cholesky.81
  1494.9 0.6 compare_reduce_fusion
  1495.5 0.7 fusion.17
  1496.2 9.8 custom-call.9
  1506.0 0.3 fusion.9
  1506.3 1.5 fusion.24
  1507.8 24.3 %all_gather.7 = bf16[512,128]{1,0:T(8,128)(2,1)S(1)} all-gather(bf16[16,128]{1,0:T(8,128)(2,1)S(1)} %get-tuple-element.9), channel_id=1, replica_groups=mesh['row'=16,'col'=32] {'col'}, dimensions={0}, use_global_device_ids=true | all-gather | bytes 135168 | tf_op jit(solution)/shard_map/all_gather | solution.py:58
  1532.1 1.4 convolution_convert_fusion
  1533.5 0.0 reduce-scatter.8.cloned.1.call-update
  1533.5 59.1 %reduce-scatter.8.cloned.1.call-done = bf16[1536,8]{0,1:T(8,128)(2,1)} async-done(((bf16[1536,128]{0,1:T(8,128)(2,1)}), bf16[1536,8]{0,1:T(8,128)(2,1)}) %reduce-scatter.8.cloned.1.call-update) | async-done | bytes 24592 | tf_op jit(solution)/shard_map/reduce_scatter | solution.py:70
  1592.6 1.4 convert_element_type.55
  (10 shorter events, 0.1 us)
Async XLA Ops:
  7.2 65.8 %copy-start = (bf16[1536,128]{1,0:T(8,128)(2,1)S(1)}, bf16[1536,128]{1,0:T(8,128)(2,1)}, u32[]{:S(2)}) copy-start(bf16[1536,128]{1,0:T(8,128)(2,1)} %param.10) | copy-start | bytes 1179652
  7.2 64.3 %copy-start.2 = (f32[1536]{0:T(1024)S(1)}, f32[1536]{0:T(1024)}, u32[]{:S(2)}) copy-start(f32[1536]{0:T(1024)} %param.9) | copy-start | bytes 18436
  7.2 64.3 %copy-start.3 = (f32[512]{0:T(512)S(1)}, f32[512]{0:T(512)}, u32[]{:S(2)}) copy-start(f32[512]{0:T(512)} %param.8) | copy-start | bytes 6148
  7.2 163.0 %reduce-scatter.4.cloned.1.call-start = ((), (), s32[]{:S(2)}) async-start(), calls=%async_computation.3 | async-start | bytes 270336 | tf_op jit(solution)/shard_map/reduce_scatter | solution.py:46
  74.3 541.4 %all-reduce.5.cloned.1.call-start = ((), (), s32[]{:S(2)}) async-start(), calls=%async_computation.4 | async-start | bytes 131072 | tf_op jit(solution)/shard_map/psum | solution.py:52
  172.0 621.6 %all-reduce.7.cloned.1.call-start = ((), (), s32[]{:S(2)}) async-start(), calls=%async_computation.5 | async-start | bytes 786432 | tf_op jit(solution)/shard_map/psum | solution.py:65
  667.2 369.6 %reduce-scatter.6.cloned.1.call-start = ((), (), s32[]{:S(2)}) async-start(), calls=%async_computation.6 | async-start | bytes 270336 | tf_op jit(solution)/shard_map/reduce_scatter | solution.py:46
  793.6 143.7 %copy-start.1 = (bf16[1536,128]{1,0:T(8,128)(2,1)S(1)}, bf16[1536,128]{1,0:T(8,128)(2,1)}, u32[]{:S(2)}) copy-start(bf16[1536,128]{1,0:T(8,128)(2,1)} %all-reduce.7.cloned.1.call-done) | copy-start | bytes 1179652
  940.0 541.3 %all-reduce.9.cloned.1.call-start = ((), (), s32[]{:S(2)}) async-start(), calls=%async_computation.7 | async-start | bytes 131072 | tf_op jit(solution)/shard_map/psum | solution.py:52
  1038.5 554.1 %reduce-scatter.8.cloned.1.call-start = ((), (), s32[]{:S(2)}) async-start(), calls=%async_computation.8 | async-start | bytes 417792 | tf_op jit(solution)/shard_map/reduce_scatter | solution.py:70
Sparse Core Ops, SparseCore 0:
  74.4 95.7 reduce-scatter.3
  176.3 439.3 all-reduce.4
  667.3 126.2 all-reduce.6
  940.1 96.5 reduce-scatter.5
  1042.0 439.2 all-reduce.8
  1533.6 58.9 reduce-scatter.7
where the time goes:
time: 1600 us
  waiting for transfers between devices  1260 us (79%)
  blocking collectives  230 us (14%)
  other arithmetic  74 us (5%)
    psum x2, waiting for transfers between devices, sketch(): gram_sum = lax.psum(local_gram(tall_part), ('row', 'col'))  886 us
    reduce_scatter x2, waiting for transfers between devices, sketch(): lax.psum_scatter(jnp.dot(matrix, panel_in, preferred_element_type=jnp.flo...  193 us
    psum x1, waiting for transfers between devices, per_device(): lax.psum(partial_back.astype(jnp.bfloat16), 'row').astype(jnp.float32)  126 us
    psum x1, blocking collectives, per_device(): lax.psum(local_gram(back).astype(jnp.bfloat16), 'col').astype(jnp.float32)  119 us
    psum x1, blocking collectives, per_device(): lax.psum((jnp.sum(dosage, axis=0), jnp.sum(dosage * dosage, axis=0)), 'row')  62 us
    reduce_scatter x1, waiting for transfers between devices, per_device(): lax.psum_scatter(project(second.astype(jnp.bfloat16)).astype(jnp.bfloat16...  59.1 us
    all_gather x2, blocking collectives, project(): lax.all_gather(basis_half, 'col', axis=0, tiled=True)  48.6 us
    another operation x9, other arithmetic, orthonormal(): lower = jnp.linalg.cholesky(gram_sum)  37.2 us
  transfers between devices with their start and end apart: 6, of which 6 were waited for; matrix products, arithmetic and copies ran while one was open for 0% of the time, Pallas kernels for 0%

commit v1 on v0

v1 whole, which is shorter than its diff:
```python
import math

import jax
import jax.numpy as jnp
from jax import lax
from jax.sharding import PartitionSpec as P

EPSILON = 1e-05
CONTRACT_ROWS = (((0,), (0,)), ((), ()))
HIGHEST = lax.Precision.HIGHEST
COL_CORE, COL_X, COL_Y = (1, 2), (2, 4), (8, 4)
ROW_LOW, ROW_HIGH = (1, 4), (4, 4)


def unpack(words):
    shifts = 2 * jnp.arange(6, dtype=jnp.int32)
    parts = jnp.bitwise_and(jnp.right_shift(words[None, :, :], shifts[:, None, None]), 3)
    return (
        jnp.transpose(parts, (1, 0, 2))
        .reshape(words.shape[0], 6 * words.shape[1])
        .astype(jnp.float32)
    )


def place(axis, group):
    stride, size = group
    return lax.rem(lax.div(lax.axis_index(axis), stride), size)


def shift(block, axis, group, steps):
    stride, size = group
    pairs = []
    for index in range(lax.axis_size(axis)):
        mine = (index // stride) % size
        pairs.append((index, index + ((mine + steps) % size - mine) * stride))
    return lax.ppermute(block, axis, pairs)


def group_scatter(panel, axis, group):
    size = group[1]
    mine = place(axis, group)
    blocks = panel.reshape((size, panel.shape[0] // size) + panel.shape[1:])

    def block_at(index):
        return lax.dynamic_index_in_dim(blocks, lax.rem(index, size), 0, keepdims=False)

    arrived = [shift(block_at(mine + k), axis, group, k) for k in range(1, size)]
    total = block_at(mine)
    for block in arrived:
        total = total + block
    return total


def group_gather(block, axis, group):
    size = group[1]
    mine = place(axis, group)
    ordered = [block] + [shift(block, axis, group, size - j) for j in range(1, size)]
    ring = jnp.concatenate(ordered + ordered[:-1], axis=0)
    start = lax.rem(size - mine, size) * block.shape[0]
    return lax.dynamic_slice_in_dim(ring, start, size * block.shape[0], 0)


def grouped_sum(panel, axis, groups):
    for group in groups:
        panel = group_scatter(panel, axis, group)
    for group in reversed(groups):
        panel = group_gather(panel, axis, group)
    return panel


def exchanged_scatter(panel, axis):
    size = lax.axis_size(axis)
    blocks = panel.reshape((size, panel.shape[0] // size) + panel.shape[1:])
    arrived = lax.all_to_all(blocks, axis, split_axis=0, concat_axis=0, tiled=True)
    return jnp.sum(arrived.astype(jnp.float32), axis=0)


def inverse_factor(gram_sum):
    lower = jnp.linalg.cholesky(gram_sum)
    identity = jnp.eye(gram_sum.shape[0], dtype=jnp.float32)
    return lax.linalg.triangular_solve(lower, identity, left_side=True, lower=True)


def apply_factor(panel, inverse):
    return lax.dot_general(panel, inverse, (((1,), (1,)), ((), ())), precision=HIGHEST)


def local_gram(panel):
    return lax.dot_general(panel, panel, CONTRACT_ROWS, precision=HIGHEST)


def per_device(dosage_words, sample_weight, variant_weight, omega):
    dosage = unpack(dosage_words)
    rows_local, cols_local = dosage.shape
    rows_all = rows_local * lax.axis_size("row")
    cols_all = cols_local * lax.axis_size("col")
    sums = jnp.stack([jnp.sum(dosage, axis=0), jnp.sum(dosage * dosage, axis=0)])
    totals, squares = jnp.sum(lax.all_gather(sums, "row"), axis=0)
    column_mean = totals / rows_all
    column_scale = lax.rsqrt(squares / rows_all - column_mean * column_mean + EPSILON)
    matrix = (
        (dosage - column_mean) * column_scale * sample_weight[:, None] * variant_weight
    ).astype(jnp.bfloat16)

    sketch_part = jnp.dot(matrix, omega, preferred_element_type=jnp.float32)
    sketch = lax.all_gather(exchanged_scatter(sketch_part, "col"), "col", axis=0, tiled=True)
    gram = grouped_sum(local_gram(sketch), "row", (ROW_LOW, ROW_HIGH))
    first = apply_factor(sketch, inverse_factor(gram)).astype(jnp.bfloat16)

    back_part = lax.dot_general(
        matrix, first, CONTRACT_ROWS, preferred_element_type=jnp.float32
    ).astype(jnp.bfloat16)
    back_rows = exchanged_scatter(back_part, "row").astype(jnp.bfloat16)
    back = lax.all_gather(back_rows, "row", axis=0, tiled=True)

    both = jnp.concatenate(
        [
            jnp.dot(matrix, back, preferred_element_type=jnp.float32),
            lax.dot_general(back, back, CONTRACT_ROWS, preferred_element_type=jnp.float32),
        ],
        axis=0,
    )
    both = grouped_sum(both, "col", (COL_CORE, COL_X, COL_Y))
    inverse = inverse_factor(both[rows_local:])
    right_full = apply_factor(back.astype(jnp.float32), inverse)
    product = apply_factor(both[:rows_local], inverse)

    gram = lax.all_gather(
        exchanged_scatter(local_gram(product), "row"), "row", axis=0, tiled=True
    )
    inverse = inverse_factor(gram)
    second = apply_factor(product, inverse)
    own = rows_local // lax.axis_size("col")
    second_own = lax.dynamic_slice_in_dim(second, lax.axis_index("col") * own, own, 0)

    projection_part = lax.dot_general(
        second.astype(jnp.bfloat16), matrix, CONTRACT_ROWS, preferred_element_type=jnp.float32
    ).astype(jnp.bfloat16)
    projection = exchanged_scatter(projection_part, "row").T
    return (second_own * math.sqrt(rows_all), right_full * math.sqrt(cols_all), projection)


def solution(mesh):
    in_specs = (P("row", "col"), P("row"), P("col"), P("col", None))
    out_specs = (P(("row", "col"), None), P("col", None), P("col", "row"))
    return jax.shard_map(
        per_device, mesh=mesh, in_specs=in_specs, out_specs=out_specs, check_vma=False
    )
```

time: 1600 us -> 425 us (0.27)
  the two profiles are of different devices: /device:TPU:2 before, /device:TPU:32 now
where the time goes in v1:
time: 425 us; the launch traced here: 423 us
  blocking collectives  134 us (32%)
  starting transfers between devices  115 us (27%)
  waiting for transfers between devices  77.1 us (18%)
  other arithmetic  72.9 us (17%)
  matrix products  11.9 us (3%)
  local copies, waits for them, and re-layouts  11.5 us (3%)
    ppermute x26, starting transfers between devices, shift(): return lax.ppermute(block, axis, pairs)  93 us
    all_to_all x3, waiting for transfers between devices, exchanged_scatter(): lax.all_to_all(blocks, axis, split_axis=0, concat_axis=0, tiled=True)  42.1 us
    another operation x9, other arithmetic, inverse_factor(): lower = jnp.linalg.cholesky(gram_sum)  37.2 us
    ppermute x26, waiting for transfers between devices, shift(): return lax.ppermute(block, axis, pairs)  34.9 us
    all_gather x1, blocking collectives, per_device(): totals, squares = jnp.sum(lax.all_gather(sums, 'row'), axis=0)  34.3 us
    another operation x6, other arithmetic, inverse_factor(): lax.linalg.triangular_solve(lower, identity, left_side=True, lower=True)  31.4 us
    all_gather x1, blocking collectives, per_device(): back = lax.all_gather(back_rows, 'row', axis=0, tiled=True)  28.4 us
    all_gather x1, blocking collectives, per_device(): lax.all_gather(exchanged_scatter(local_gram(product), 'row'), 'row', axis...  27.5 us
  transfers between devices with their start and end apart: 29, of which 18 were waited for; matrix products, arithmetic and copies ran while one was open for 1% of the time, Pallas kernels for 0%

profile of v1, /device:TPU:32, one launch (start us, length us, event | category | flops | bytes accessed | tf_op | source)
XLA Modules:
  0.0 423.5 jit_solution(7627273395620339934)
XLA Ops:
  0.7 1.3 copy.23
  1.9 0.8 convert_reduce_fusion
  2.8 34.3 %all-gather.1 = f32[16,2,1536]{2,1,0:T(2,128)S(1)} all-gather(f32[1,2,1536]{2,1,0:T(2,128)S(1)} %maximum_bitcast_fusion), channel_id=2, replica_groups=mesh['row'=16,'col'=32] {'row'}, dimensions={0}, use_global_device_ids=true | all-gather | bytes 208896 | tf_op jit(solution)/shard_map/all_gather | solution.py:98
  37.4 3.3 shift_right_arithmetic.38.clone
  40.6 5.0 %shift_right_arithmetic.46 = s32[32,16,1536]{2,1,0:T(8,128)} reshape(s32[512,6,256]{2,1,0:T(8,128)} %shift_right_arithmetic.38.clone) | data formatting | bytes 6291456 | tf_op jit(solution)/shard_map/shift_right_arithmetic | solution.py:17
  45.7 3.5 fusion.8
  49.2 7.3 %all-to-all-start = ((f32[32,16,128]{2,1,0:T(8,128)}), f32[32,16,128]{2,1,0:T(8,128)S(1)}, u32[]{:S(2)}, u32[]{:S(2)}) async-start(f32[32,16,128]{2,1,0:T(8,128)} %fusion.8), calls=%async_computation | async-start | bytes 524288 | tf_op jit(solution)/shard_map/all_to_all | solution.py:74
  56.6 8.9 %all-to-all-done = f32[32,16,128]{2,1,0:T(8,128)S(1)} async-done(((f32[32,16,128]{2,1,0:T(8,128)}), f32[32,16,128]{2,1,0:T(8,128)S(1)}, u32[]{:S(2)}, u32[]{:S(2)}) %all-to-all-start) | async-done | bytes 262176 | tf_op jit(solution)/shard_map/all_to_all | solution.py:74
  65.5 22.8 %all_gather.17 = f32[512,128]{1,0:T(8,128)S(1)} all-gather(f32[16,128]{1,0:T(8,128)S(1)} %reduce_sum.69), channel_id=1, replica_groups=mesh['row'=16,'col'=32] {'col'}, dimensions={0}, use_global_device_ids=true | all-gather | bytes 270336 | tf_op jit(solution)/shard_map/all_gather | solution.py:106
  89.0 2.9 collective-permute-start
  91.9 5.5 %collective-permute-start.1 = (f32[32,128]{1,0:T(8,128)S(1)}, f32[32,128]{1,0:T(8,128)S(1)}, u32[]{:S(2)}, u32[]{:S(2)}) collective-permute-start(f32[32,128]{1,0:T(8,128)S(1)} %get-tuple-element.16), channel_id=1, source_target_pairs={{0,64},{32,96},{64,0},{96,32},{128,192},{160,224},{192,128},{224,1... | collective-permute-start | bytes 49160 | tf_op jit(solution)/shard_map/ppermute | solution.py:36
  97.4 1.9 collective-permute-start.2
  99.4 3.6 collective-permute-done.2
  103.1 3.1 collective-permute-start.3
  106.2 9.6 %collective-permute-start.4 = (f32[8,128]{1,0:T(8,128)S(1)}, f32[8,128]{1,0:T(8,128)S(1)}, u32[]{:S(2)}, u32[]{:S(2)}) collective-permute-start(f32[8,128]{1,0:T(8,128)S(1)} %get-tuple-element.23), channel_id=1, source_target_pairs={{0,256},{32,288},{64,320},{96,352},{128,384},{160,416},{192,448},{... | collective-permute-start | bytes 12296 | tf_op jit(solution)/shard_map/ppermute | solution.py:36
  115.8 4.3 %collective-permute-start.5 = (f32[8,128]{1,0:T(8,128)S(1)}, f32[8,128]{1,0:T(8,128)S(1)}, u32[]{:S(2)}, u32[]{:S(2)}) collective-permute-start(f32[8,128]{1,0:T(8,128)S(1)} %get-tuple-element.22), channel_id=1, source_target_pairs={{0,384},{32,416},{64,448},{96,480},{128,0},{160,32},{192,64},{224,... | collective-permute-start | bytes 12296 | tf_op jit(solution)/shard_map/ppermute | solution.py:36
  120.4 4.8 %collective-permute-done.5 = f32[8,128]{1,0:T(8,128)S(1)} collective-permute-done((f32[8,128]{1,0:T(8,128)S(1)}, f32[8,128]{1,0:T(8,128)S(1)}, u32[]{:S(2)}, u32[]{:S(2)}) %collective-permute-start.5) | collective-permute-done | bytes 4128 | tf_op jit(solution)/shard_map/ppermute | solution.py:36
  125.2 4.3 %collective-permute-start.6 = (f32[8,128]{1,0:T(8,128)S(1)}, f32[8,128]{1,0:T(8,128)S(1)}, u32[]{:S(2)}, u32[]{:S(2)}) collective-permute-start(f32[8,128]{1,0:T(8,128)S(1)} %get-tuple-element.10), channel_id=1, source_target_pairs={{0,384},{32,416},{64,448},{96,480},{128,0},{160,32},{192,64},{224,... | collective-permute-start | bytes 12296 | tf_op jit(solution)/shard_map/ppermute | solution.py:36
  129.5 7.3 %collective-permute-start.7 = (f32[8,128]{1,0:T(8,128)S(1)}, f32[8,128]{1,0:T(8,128)S(1)}, u32[]{:S(2)}, u32[]{:S(2)}) collective-permute-start(f32[8,128]{1,0:T(8,128)S(1)} %get-tuple-element.10), channel_id=1, source_target_pairs={{0,256},{32,288},{64,320},{96,352},{128,384},{160,416},{192,448},{... | collective-permute-start | bytes 12296 | tf_op jit(solution)/shard_map/ppermute | solution.py:36
  136.8 3.1 collective-permute-start.8
  140.0 3.8 collective-permute-done.7
  143.7 2.6 collective-permute-done.8
  146.5 3.6 collective-permute-start.10
  150.1 1.9 collective-permute-start.11
  152.0 4.1 collective-permute-start.9
  156.1 1.5 fusion.6
  158.6 11.7 %cholesky.59 = f32[128,128]{1,0:T(8,128)S(1)} custom-call(f32[128,128]{1,0:T(8,128)S(1)} %fusion.31), custom_call_target="Cholesky" | custom-call | tf_op jit(solution)/shard_map/jit(cholesky)/cholesky | solution.py:79
  171.7 9.8 %custom-call.7 = f32[1,128,128]{1,2,0:T(8,128)S(1)} custom-call(f32[1,128,128]{2,1,0:T(8,128)S(1)} %fusion.21), custom_call_target="InvertDiagBlocksLowerTriangular" | custom-call | tf_op jit(solution)/shard_map/triangular_solve/custom-call.0 | solution.py:81
  182.2 1.3 convolution_convert_fusion.1
  183.5 8.7 %all-to-all-start.1 = ((bf16[16,96,128]{2,1,0:T(8,128)(2,1)}), bf16[16,96,128]{2,1,0:T(8,128)(2,1)S(1)}, u32[]{:S(2)}, u32[]{:S(2)}) async-start(bf16[16,96,128]{2,1,0:T(8,128)(2,1)} %bitcast.16), calls=%async_computation.1 | async-start | bytes 786432 | tf_op jit(solution)/shard_map/all_to_all | solution.py:74
  192.2 18.2 %all-to-all-done.1 = bf16[16,96,128]{2,1,0:T(8,128)(2,1)S(1)} async-done(((bf16[16,96,128]{2,1,0:T(8,128)(2,1)}), bf16[16,96,128]{2,1,0:T(8,128)(2,1)S(1)}, u32[]{:S(2)}, u32[]{:S(2)}) %all-to-all-start.1) | async-done | bytes 393248 | tf_op jit(solution)/shard_map/all_to_all | solution.py:74
  210.5 28.4 %all_gather.18 = bf16[1536,128]{1,0:T(8,128)(2,1)S(1)} all-gather(bf16[96,128]{1,0:T(8,128)(2,1)S(1)} %reduce_sum.70), channel_id=1, replica_groups=mesh['row'=16,'col'=32] {'row'}, dimensions={0}, use_global_device_ids=true | all-gather | bytes 417792 | tf_op jit(solution)/shard_map/all_gather | solution.py:114
  239.8 1.9 collective-permute-start.12
  241.8 1.3 collective-permute-done.12
  243.2 2.8 collective-permute-start.13
  246.0 4.6 %collective-permute-start.14 = (f32[80,128]{1,0:T(8,128)S(1)}, f32[80,128]{1,0:T(8,128)S(1)}, u32[]{:S(2)}, u32[]{:S(2)}) collective-permute-start(f32[80,128]{1,0:T(8,128)S(1)} %get-tuple-element.13), channel_id=1, source_target_pairs={{0,4},{1,5},{2,6},{3,7},{4,0},{5,1},{6,2},{7,3},{8,12},{9,13},{10,... | collective-permute-start | bytes 122888 | tf_op jit(solution)/shard_map/ppermute | solution.py:36
  250.6 2.5 collective-permute-start.15
  253.4 3.1 collective-permute-done.15
  256.7 2.2 collective-permute-start.16
  259.0 4.2 collective-permute-start.17
  263.3 3.4 collective-permute-start.18
  266.8 2.6 collective-permute-done.18
  269.4 4.6 %collective-permute-start.19 = (f32[20,128]{0,1:T(8,128)S(1)}, f32[20,128]{0,1:T(8,128)S(1)}, u32[]{:S(2)}, u32[]{:S(2)}) collective-permute-start(f32[20,128]{0,1:T(8,128)S(1)} %fusion.29), channel_id=1, source_target_pairs={{0,24},{1,25},{2,26},{3,27},{4,28},{5,29},{6,30},{7,31},{8,0},{9,1... | collective-permute-start | bytes 30728 | tf_op jit(solution)/shard_map/ppermute | solution.py:36
  274.1 2.8 collective-permute-start.20
  276.9 1.9 collective-permute-start.21
  278.8 2.9 collective-permute-done.20
  281.7 2.5 collective-permute-done.21
  284.5 3.7 collective-permute-start.22
  288.2 2.7 collective-permute-start.23
  290.9 2.0 collective-permute-start.24
  292.9 2.9 collective-permute-done.23
  295.8 2.4 collective-permute-done.24
  298.6 2.1 collective-permute-start.25
  300.8 1.2 collective-permute-done.25
  302.4 11.7 %cholesky.70 = f32[128,128]{1,0:T(8,128)S(1)} custom-call(f32[128,128]{1,0:T(8,128)S(1)} %fusion.27), custom_call_target="Cholesky" | custom-call | tf_op jit(solution)/shard_map/jit(cholesky)/cholesky | solution.py:79
  315.4 9.8 %custom-call.8 = f32[1,128,128]{1,2,0:T(8,128)S(1)} custom-call(f32[1,128,128]{2,1,0:T(8,128)S(1)} %fusion.22), custom_call_target="InvertDiagBlocksLowerTriangular" | custom-call | tf_op jit(solution)/shard_map/triangular_solve/custom-call.0 | solution.py:81
  326.7 20.7 %all_to_all.20 = f32[16,8,128]{2,1,0:T(8,128)S(1)} all-to-all(f32[16,8,128]{2,1,0:T(8,128)S(1)} %convolution_bitcast_fusion), channel_id=1, replica_groups=mesh['row'=16,'col'=32] {'row'}, dimensions={0} | all-to-all | bytes 131072 | tf_op jit(solution)/shard_map/all_to_all | solution.py:74
  347.5 27.5 %all_gather.19 = f32[128,128]{1,0:T(8,128)S(1)} all-gather(f32[8,128]{1,0:T(8,128)S(1)} %reduce_sum.71), channel_id=1, replica_groups=mesh['row'=16,'col'=32] {'row'}, dimensions={0}, use_global_device_ids=true | all-gather | bytes 69632 | tf_op jit(solution)/shard_map/all_gather | solution.py:128
  375.1 11.7 %cholesky.81 = f32[128,128]{1,0:T(8,128)S(1)} custom-call(f32[128,128]{1,0:T(8,128)S(1)} %fusion.25), custom_call_target="Cholesky" | custom-call | tf_op jit(solution)/shard_map/jit(cholesky)/cholesky | solution.py:79
  388.2 9.8 %custom-call.9 = f32[1,128,128]{1,2,0:T(8,128)S(1)} custom-call(f32[1,128,128]{2,1,0:T(8,128)S(1)} %fusion.23), custom_call_target="InvertDiagBlocksLowerTriangular" | custom-call | tf_op jit(solution)/shard_map/triangular_solve/custom-call.0 | solution.py:81
  398.7 1.4 fusion.7
  400.1 5.6 %all-to-all-start.3 = ((bf16[16,8,1536]{2,1,0:T(8,128)(2,1)}), bf16[16,8,1536]{2,1,0:T(8,128)(2,1)S(1)}, u32[]{:S(2)}, u32[]{:S(2)}) async-start(bf16[16,8,1536]{2,1,0:T(8,128)(2,1)} %fusion.7), calls=%async_computation.3 | async-start | bytes 786432 | tf_op jit(solution)/shard_map/all_to_all | solution.py:74
  405.7 1.4 convolution_multiply_fusion
  407.7 15.1 %all-to-all-done.3 = bf16[16,8,1536]{2,1,0:T(8,128)(2,1)S(1)} async-done(((bf16[16,8,1536]{2,1,0:T(8,128)(2,1)}), bf16[16,8,1536]{2,1,0:T(8,128)(2,1)S(1)}, u32[]{:S(2)}, u32[]{:S(2)}) %all-to-all-start.3) | async-done | bytes 393248 | tf_op jit(solution)/shard_map/all_to_all | solution.py:74
  (91 shorter events, 13.3 us)
Async XLA Ops:
  0.6 45.1 %copy-start = (bf16[1536,128]{1,0:T(8,128)(2,1)S(1)}, bf16[1536,128]{1,0:T(8,128)(2,1)}, u32[]{:S(2)}) copy-start(bf16[1536,128]{1,0:T(8,128)(2,1)} %param.10) | copy-start | bytes 1179652
  40.6 5.0 %copy-start.2 = (f32[512]{0:T(512)S(1)}, f32[512]{0:T(512)}, u32[]{:S(2)}) copy-start(f32[512]{0:T(512)} %param.8) | copy-start | bytes 6148
  40.6 5.1 %copy-start.1 = (f32[1536]{0:T(1024)S(1)}, f32[1536]{0:T(1024)}, u32[]{:S(2)}) copy-start(f32[1536]{0:T(1024)} %param.9) | copy-start | bytes 18436
  49.2 16.2 %all-to-all-start = ((f32[32,16,128]{2,1,0:T(8,128)}), f32[32,16,128]{2,1,0:T(8,128)S(1)}, u32[]{:S(2)}, u32[]{:S(2)}) async-start(f32[32,16,128]{2,1,0:T(8,128)} %fusion.8), calls=%async_computation | async-start | bytes 524288 | tf_op jit(solution)/shard_map/all_to_all | solution.py:74
  89.0 10.4 %collective-permute-start = (f32[32,128]{1,0:T(8,128)S(1)}, f32[32,128]{1,0:T(8,128)S(1)}, u32[]{:S(2)}, u32[]{:S(2)}) collective-permute-start(f32[32,128]{1,0:T(8,128)S(1)} %get-tuple-element.14), channel_id=1, source_target_pairs={{0,32},{32,64},{64,96},{96,0},{128,160},{160,192},{192,224},{224,1... | collective-permute-start | bytes 49160 | tf_op jit(solution)/shard_map/ppermute | solution.py:36
  91.9 7.5 %collective-permute-start.1 = (f32[32,128]{1,0:T(8,128)S(1)}, f32[32,128]{1,0:T(8,128)S(1)}, u32[]{:S(2)}, u32[]{:S(2)}) collective-permute-start(f32[32,128]{1,0:T(8,128)S(1)} %get-tuple-element.16), channel_id=1, source_target_pairs={{0,64},{32,96},{64,0},{96,32},{128,192},{160,224},{192,128},{224,1... | collective-permute-start | bytes 49160 | tf_op jit(solution)/shard_map/ppermute | solution.py:36
  97.4 5.6 %collective-permute-start.2 = (f32[32,128]{1,0:T(8,128)S(1)}, f32[32,128]{1,0:T(8,128)S(1)}, u32[]{:S(2)}, u32[]{:S(2)}) collective-permute-start(f32[32,128]{1,0:T(8,128)S(1)} %get-tuple-element.15), channel_id=1, source_target_pairs={{0,96},{32,0},{64,32},{96,64},{128,224},{160,128},{192,160},{224,1... | collective-permute-start | bytes 49160 | tf_op jit(solution)/shard_map/ppermute | solution.py:36
  103.1 17.0 %collective-permute-start.3 = (f32[8,128]{1,0:T(8,128)S(1)}, f32[8,128]{1,0:T(8,128)S(1)}, u32[]{:S(2)}, u32[]{:S(2)}) collective-permute-start(f32[8,128]{1,0:T(8,128)S(1)} %get-tuple-element.21), channel_id=1, source_target_pairs={{0,128},{32,160},{64,192},{96,224},{128,256},{160,288},{192,320},{... | collective-permute-start | bytes 12296 | tf_op jit(solution)/shard_map/ppermute | solution.py:36
  106.2 14.2 %collective-permute-start.4 = (f32[8,128]{1,0:T(8,128)S(1)}, f32[8,128]{1,0:T(8,128)S(1)}, u32[]{:S(2)}, u32[]{:S(2)}) collective-permute-start(f32[8,128]{1,0:T(8,128)S(1)} %get-tuple-element.23), channel_id=1, source_target_pairs={{0,256},{32,288},{64,320},{96,352},{128,384},{160,416},{192,448},{... | collective-permute-start | bytes 12296 | tf_op jit(solution)/shard_map/ppermute | solution.py:36
  115.8 9.4 %collective-permute-start.5 = (f32[8,128]{1,0:T(8,128)S(1)}, f32[8,128]{1,0:T(8,128)S(1)}, u32[]{:S(2)}, u32[]{:S(2)}) collective-permute-start(f32[8,128]{1,0:T(8,128)S(1)} %get-tuple-element.22), channel_id=1, source_target_pairs={{0,384},{32,416},{64,448},{96,480},{128,0},{160,32},{192,64},{224,... | collective-permute-start | bytes 12296 | tf_op jit(solution)/shard_map/ppermute | solution.py:36
  125.2 14.7 %collective-permute-start.6 = (f32[8,128]{1,0:T(8,128)S(1)}, f32[8,128]{1,0:T(8,128)S(1)}, u32[]{:S(2)}, u32[]{:S(2)}) collective-permute-start(f32[8,128]{1,0:T(8,128)S(1)} %get-tuple-element.10), channel_id=1, source_target_pairs={{0,384},{32,416},{64,448},{96,480},{128,0},{160,32},{192,64},{224,... | collective-permute-start | bytes 12296 | tf_op jit(solution)/shard_map/ppermute | solution.py:36
  129.5 14.2 %collective-permute-start.7 = (f32[8,128]{1,0:T(8,128)S(1)}, f32[8,128]{1,0:T(8,128)S(1)}, u32[]{:S(2)}, u32[]{:S(2)}) collective-permute-start(f32[8,128]{1,0:T(8,128)S(1)} %get-tuple-element.10), channel_id=1, source_target_pairs={{0,256},{32,288},{64,320},{96,352},{128,384},{160,416},{192,448},{... | collective-permute-start | bytes 12296 | tf_op jit(solution)/shard_map/ppermute | solution.py:36
  136.8 9.5 %collective-permute-start.8 = (f32[8,128]{1,0:T(8,128)S(1)}, f32[8,128]{1,0:T(8,128)S(1)}, u32[]{:S(2)}, u32[]{:S(2)}) collective-permute-start(f32[8,128]{1,0:T(8,128)S(1)} %get-tuple-element.10), channel_id=1, source_target_pairs={{0,128},{32,160},{64,192},{96,224},{128,256},{160,288},{192,320},{... | collective-permute-start | bytes 12296 | tf_op jit(solution)/shard_map/ppermute | solution.py:36
  146.5 11.2 %collective-permute-start.10 = (f32[32,128]{0,1:T(8,128)S(1)}, f32[32,128]{0,1:T(8,128)S(1)}, u32[]{:S(2)}, u32[]{:S(2)}) collective-permute-start(f32[32,128]{0,1:T(8,128)S(1)} %copy.33), channel_id=1, source_target_pairs={{0,64},{32,96},{64,0},{96,32},{128,192},{160,224},{192,128},{224,1... | collective-permute-start | bytes 49160 | tf_op jit(solution)/shard_map/ppermute | solution.py:36
  150.1 7.6 %collective-permute-start.11 = (f32[32,128]{0,1:T(8,128)S(1)}, f32[32,128]{0,1:T(8,128)S(1)}, u32[]{:S(2)}, u32[]{:S(2)}) collective-permute-start(f32[32,128]{0,1:T(8,128)S(1)} %copy.33), channel_id=1, source_target_pairs={{0,32},{32,64},{64,96},{96,0},{128,160},{160,192},{192,224},{224,1... | collective-permute-start | bytes 49160 | tf_op jit(solution)/shard_map/ppermute | solution.py:36
  152.0 6.2 %collective-permute-start.9 = (f32[32,128]{0,1:T(8,128)S(1)}, f32[32,128]{0,1:T(8,128)S(1)}, u32[]{:S(2)}, u32[]{:S(2)}) collective-permute-start(f32[32,128]{0,1:T(8,128)S(1)} %copy.33), channel_id=1, source_target_pairs={{0,96},{32,0},{64,32},{96,64},{128,224},{160,128},{192,160},{224,1... | collective-permute-start | bytes 49160 | tf_op jit(solution)/shard_map/ppermute | solution.py:36
  183.5 26.9 %all-to-all-start.1 = ((bf16[16,96,128]{2,1,0:T(8,128)(2,1)}), bf16[16,96,128]{2,1,0:T(8,128)(2,1)S(1)}, u32[]{:S(2)}, u32[]{:S(2)}) async-start(bf16[16,96,128]{2,1,0:T(8,128)(2,1)} %bitcast.16), calls=%async_computation.1 | async-start | bytes 786432 | tf_op jit(solution)/shard_map/all_to_all | solution.py:74
  239.8 3.3 collective-permute-start.12
  243.2 9.9 %collective-permute-start.13 = (f32[80,128]{1,0:T(8,128)S(1)}, f32[80,128]{1,0:T(8,128)S(1)}, u32[]{:S(2)}, u32[]{:S(2)}) collective-permute-start(f32[80,128]{1,0:T(8,128)S(1)} %get-tuple-element.11), channel_id=1, source_target_pairs={{0,2},{1,3},{2,4},{3,5},{4,6},{5,7},{6,0},{7,1},{8,10},{9,11},{10,... | collective-permute-start | bytes 122888 | tf_op jit(solution)/shard_map/ppermute | solution.py:36
  246.0 7.4 %collective-permute-start.14 = (f32[80,128]{1,0:T(8,128)S(1)}, f32[80,128]{1,0:T(8,128)S(1)}, u32[]{:S(2)}, u32[]{:S(2)}) collective-permute-start(f32[80,128]{1,0:T(8,128)S(1)} %get-tuple-element.13), channel_id=1, source_target_pairs={{0,4},{1,5},{2,6},{3,7},{4,0},{5,1},{6,2},{7,3},{8,12},{9,13},{10,... | collective-permute-start | bytes 122888 | tf_op jit(solution)/shard_map/ppermute | solution.py:36
  250.6 5.9 %collective-permute-start.15 = (f32[80,128]{1,0:T(8,128)S(1)}, f32[80,128]{1,0:T(8,128)S(1)}, u32[]{:S(2)}, u32[]{:S(2)}) collective-permute-start(f32[80,128]{1,0:T(8,128)S(1)} %get-tuple-element.12), channel_id=1, source_target_pairs={{0,6},{1,7},{2,0},{3,1},{4,2},{5,3},{6,4},{7,5},{8,14},{9,15},{10,... | collective-permute-start | bytes 122888 | tf_op jit(solution)/shard_map/ppermute | solution.py:36
  256.7 10.1 %collective-permute-start.16 = (f32[20,128]{0,1:T(8,128)S(1)}, f32[20,128]{0,1:T(8,128)S(1)}, u32[]{:S(2)}, u32[]{:S(2)}) collective-permute-start(f32[20,128]{0,1:T(8,128)S(1)} %bitcast.143), channel_id=1, source_target_pairs={{0,8},{1,9},{2,10},{3,11},{4,12},{5,13},{6,14},{7,15},{8,16},{9,17... | collective-permute-start | bytes 30728 | tf_op jit(solution)/shard_map/ppermute | solution.py:36
  259.0 7.8 %collective-permute-start.17 = (f32[20,128]{0,1:T(8,128)S(1)}, f32[20,128]{0,1:T(8,128)S(1)}, u32[]{:S(2)}, u32[]{:S(2)}) collective-permute-start(f32[20,128]{0,1:T(8,128)S(1)} %bitcast.144), channel_id=1, source_target_pairs={{0,16},{1,17},{2,18},{3,19},{4,20},{5,21},{6,22},{7,23},{8,24},{9,... | collective-permute-start | bytes 30728 | tf_op jit(solution)/shard_map/ppermute | solution.py:36
  263.3 6.2 %collective-permute-start.18 = (f32[20,128]{0,1:T(8,128)S(1)}, f32[20,128]{0,1:T(8,128)S(1)}, u32[]{:S(2)}, u32[]{:S(2)}) collective-permute-start(f32[20,128]{0,1:T(8,128)S(1)} %bitcast.145), channel_id=1, source_target_pairs={{0,24},{1,25},{2,26},{3,27},{4,28},{5,29},{6,30},{7,31},{8,0},{9,1... | collective-permute-start | bytes 30728 | tf_op jit(solution)/shard_map/ppermute | solution.py:36
  269.4 9.4 %collective-permute-start.19 = (f32[20,128]{0,1:T(8,128)S(1)}, f32[20,128]{0,1:T(8,128)S(1)}, u32[]{:S(2)}, u32[]{:S(2)}) collective-permute-start(f32[20,128]{0,1:T(8,128)S(1)} %fusion.29), channel_id=1, source_target_pairs={{0,24},{1,25},{2,26},{3,27},{4,28},{5,29},{6,30},{7,31},{8,0},{9,1... | collective-permute-start | bytes 30728 | tf_op jit(solution)/shard_map/ppermute | solution.py:36
  274.1 7.7 %collective-permute-start.20 = (f32[20,128]{0,1:T(8,128)S(1)}, f32[20,128]{0,1:T(8,128)S(1)}, u32[]{:S(2)}, u32[]{:S(2)}) collective-permute-start(f32[20,128]{0,1:T(8,128)S(1)} %fusion.29), channel_id=1, source_target_pairs={{0,16},{1,17},{2,18},{3,19},{4,20},{5,21},{6,22},{7,23},{8,24},{9,... | collective-permute-start | bytes 30728 | tf_op jit(solution)/shard_map/ppermute | solution.py:36
  276.9 7.4 %collective-permute-start.21 = (f32[20,128]{0,1:T(8,128)S(1)}, f32[20,128]{0,1:T(8,128)S(1)}, u32[]{:S(2)}, u32[]{:S(2)}) collective-permute-start(f32[20,128]{0,1:T(8,128)S(1)} %fusion.29), channel_id=1, source_target_pairs={{0,8},{1,9},{2,10},{3,11},{4,12},{5,13},{6,14},{7,15},{8,16},{9,17... | collective-permute-start | bytes 30728 | tf_op jit(solution)/shard_map/ppermute | solution.py:36
  284.5 8.4 %collective-permute-start.22 = (f32[80,128]{0,1:T(8,128)S(1)}, f32[80,128]{0,1:T(8,128)S(1)}, u32[]{:S(2)}, u32[]{:S(2)}) collective-permute-start(f32[80,128]{0,1:T(8,128)S(1)} %constant_dynamic-slice_fusion.1), channel_id=1, source_target_pairs={{0,6},{1,7},{2,0},{3,1},{4,2},{5,3},{6,4},{7,5},{8,14},{9,15},{10,... | collective-permute-start | bytes 122888 | tf_op jit(solution)/shard_map/ppermute | solution.py:36
  288.2 7.7 %collective-permute-start.23 = (f32[80,128]{0,1:T(8,128)S(1)}, f32[80,128]{0,1:T(8,128)S(1)}, u32[]{:S(2)}, u32[]{:S(2)}) collective-permute-start(f32[80,128]{0,1:T(8,128)S(1)} %constant_dynamic-slice_fusion.1), channel_id=1, source_target_pairs={{0,4},{1,5},{2,6},{3,7},{4,0},{5,1},{6,2},{7,3},{8,12},{9,13},{10,... | collective-permute-start | bytes 122888 | tf_op jit(solution)/shard_map/ppermute | solution.py:36
  290.9 7.4 %collective-permute-start.24 = (f32[80,128]{0,1:T(8,128)S(1)}, f32[80,128]{0,1:T(8,128)S(1)}, u32[]{:S(2)}, u32[]{:S(2)}) collective-permute-start(f32[80,128]{0,1:T(8,128)S(1)} %constant_dynamic-slice_fusion.1), channel_id=1, source_target_pairs={{0,2},{1,3},{2,4},{3,5},{4,6},{5,7},{6,0},{7,1},{8,10},{9,11},{10,... | collective-permute-start | bytes 122888 | tf_op jit(solution)/shard_map/ppermute | solution.py:36
  298.6 3.3 collective-permute-start.25
  400.1 22.7 %all-to-all-start.3 = ((bf16[16,8,1536]{2,1,0:T(8,128)(2,1)}), bf16[16,8,1536]{2,1,0:T(8,128)(2,1)S(1)}, u32[]{:S(2)}, u32[]{:S(2)}) async-start(bf16[16,8,1536]{2,1,0:T(8,128)(2,1)} %fusion.7), calls=%async_computation.3 | async-start | bytes 786432 | tf_op jit(solution)/shard_map/all_to_all | solution.py:74

commit v2 on v1

v2 whole, which is shorter than its diff:
```python
import math

import jax
import jax.numpy as jnp
from jax import lax
from jax.experimental import pallas as pl
from jax.experimental.pallas import tpu as pltpu
from jax.sharding import PartitionSpec as P

EPSILON = 1e-05
PLACES = 6
CONTRACT_ROWS = (((0,), (0,)), ((), ()))
HIGHEST = lax.Precision.HIGHEST
VMEM_LIMIT = 32 * 1024 * 1024
BLOCK = 8


def exchange(blocks, axis):
    return lax.all_to_all(blocks, axis, split_axis=0, concat_axis=0, tiled=True)


def exchanged_scatter(panel, axis):
    size = lax.axis_size(axis)
    blocks = panel.reshape((size, panel.shape[0] // size) + panel.shape[1:])
    return jnp.sum(exchange(blocks, axis).astype(jnp.float32), axis=0)


def exchanged_gather(block, axis):
    size = lax.axis_size(axis)
    gathered = exchange(jnp.broadcast_to(block[None], (size,) + block.shape), axis)
    return gathered.reshape((size * block.shape[0],) + block.shape[1:])


def doubled_sum(panel, axis):
    size = lax.axis_size(axis)
    distance = 1
    while distance < size:
        pairs = [(index, index ^ distance) for index in range(size)]
        panel = panel + lax.ppermute(panel, axis, pairs)
        distance *= 2
    return panel


def pack(gram):
    return jnp.concatenate(
        [
            gram[0:32],
            jnp.concatenate([gram[96:128, 96:128], gram[32:64, 32:128]], axis=1),
            jnp.concatenate([gram[80:96, 64:128], gram[64:80, 64:128]], axis=1),
        ],
        axis=0,
    )


def unpack_upper(packed):
    zeros = jnp.zeros((32, 128), jnp.float32)
    return jnp.concatenate(
        [
            packed[0:32],
            jnp.concatenate([zeros[:, :32], packed[32:64, 32:128]], axis=1),
            jnp.concatenate([zeros[:16, :64], packed[64:80, 64:128]], axis=1),
            jnp.concatenate([zeros[:16, :64], packed[64:80, 0:64]], axis=1),
            jnp.concatenate([zeros[:, :96], packed[32:64, 0:32]], axis=1),
        ],
        axis=0,
    )


def symmetric(upper):
    rows = lax.broadcasted_iota(jnp.int32, upper.shape, 0)
    columns = lax.broadcasted_iota(jnp.int32, upper.shape, 1)
    return jnp.where(rows <= columns, upper, upper.T)


def inverse_factor_kernel(gram_ref, inverse_ref, work):
    size = gram_ref.shape[0]
    shape = (BLOCK, size)
    work[...] = gram_ref[...]
    lane = lax.broadcasted_iota(jnp.int32, shape, 1)
    sublane = lax.broadcasted_iota(jnp.int32, shape, 0)
    all_lanes = lax.broadcasted_iota(jnp.int32, (size, size), 1)

    def spread(rows):
        out = rows[0]
        for index in range(1, BLOCK):
            out = jnp.where(sublane == index, rows[index], out)
        return out

    def step(at, carry):
        base = pl.multiple_of(at * BLOCK, BLOCK)
        rows = work[pl.ds(base, BLOCK), :]
        turned = pltpu.roll(rows, lax.rem(size - base, size), 1)
        columns = [jnp.broadcast_to(turned[:, j : j + 1], shape) for j in range(BLOCK)]
        entry = {
            (i, j): jnp.broadcast_to(columns[i][j : j + 1, :], shape)
            for j in range(BLOCK)
            for i in range(j, BLOCK)
        }
        within = jnp.logical_and(lane >= base, lane < base + BLOCK)
        start = jnp.where(within, (lane - base == sublane).astype(jnp.float32), rows)
        done, pivots, reciprocals = [], [], []
        for j in range(BLOCK):
            pivots.append(entry[j, j])
            reciprocal = 1.0 / entry[j, j]
            reciprocals.append(reciprocal)
            factors = {i: entry[i, j] * reciprocal for i in range(j + 1, BLOCK)}
            for i in range(j + 1, BLOCK):
                for k in range(j + 1, i + 1):
                    entry[i, k] = entry[i, k] - factors[i] * entry[k, j]
            for i in range(j + 1, BLOCK):
                entry[i, j] = factors[i]
        for i in range(BLOCK):
            row = jnp.broadcast_to(start[i : i + 1, :], shape)
            for j in range(i):
                row = row - entry[i, j] * done[j]
            done.append(row)
        block = spread(done)
        inverse_ref[pl.ds(base, BLOCK), :] = jnp.where(
            lane < base + BLOCK, block, 0.0
        ) * lax.rsqrt(spread(pivots))
        factor = jnp.where(lane >= base + BLOCK, block * spread(reciprocals), 0.0)
        update = lax.dot_general(
            factor, block, CONTRACT_ROWS, precision=HIGHEST, preferred_element_type=jnp.float32
        )
        inside = jnp.logical_and(all_lanes >= base, all_lanes < base + BLOCK)
        work[...] = jnp.where(inside, 0.0, work[...]) - update
        return carry

    lax.fori_loop(0, size // BLOCK, step, 0)


def inverse_factor(gram_sum):
    vmem = pl.BlockSpec(memory_space=pltpu.VMEM)
    return pl.pallas_call(
        inverse_factor_kernel,
        out_shape=jax.ShapeDtypeStruct(gram_sum.shape, jnp.float32),
        in_specs=[vmem],
        out_specs=vmem,
        scratch_shapes=[pltpu.VMEM(gram_sum.shape, jnp.float32)],
        compiler_params=pltpu.CompilerParams(vmem_limit_bytes=VMEM_LIMIT),
        cost_estimate=pl.CostEstimate(
            flops=4 * 10**9, bytes_accessed=3 * 10**7, transcendentals=0
        ),
        name="inverse_factor",
    )(gram_sum)


def standardize_kernel(words_ref, weight_ref, mean_ref, scale_ref, matrix_ref):
    rows, width = words_ref.shape
    step = 64

    def chunk(at, carry):
        span = pl.ds(pl.multiple_of(at * step, step), step)
        words = words_ref[span, :]
        weight = jnp.broadcast_to(weight_ref[span, :], (step, width))
        for place in range(PLACES):
            across = slice(place * width, (place + 1) * width)
            dosage = jnp.bitwise_and(jnp.right_shift(words, 2 * place), 3).astype(jnp.float32)
            value = (dosage - mean_ref[:, across]) * scale_ref[:, across] * weight
            matrix_ref[span, across] = value.astype(jnp.bfloat16)
        return carry

    lax.fori_loop(0, rows // step, chunk, 0)


def standardize(words, sample_weight, column_mean, column_scale):
    rows, width = words.shape
    vmem = pl.BlockSpec(memory_space=pltpu.VMEM)
    return pl.pallas_call(
        standardize_kernel,
        out_shape=jax.ShapeDtypeStruct((rows, PLACES * width), jnp.bfloat16),
        in_specs=[vmem] * 4,
        out_specs=vmem,
        compiler_params=pltpu.CompilerParams(vmem_limit_bytes=VMEM_LIMIT),
        cost_estimate=pl.CostEstimate(
            flops=10**7, bytes_accessed=4 * 10**6, transcendentals=0
        ),
        name="standardize",
    )(words, sample_weight[:, None], column_mean[None, :], column_scale[None, :])


def apply_factor(panel, inverse):
    return lax.dot_general(panel, inverse, (((1,), (1,)), ((), ())), precision=HIGHEST)


def local_gram(panel):
    return lax.dot_general(panel, panel, CONTRACT_ROWS, precision=HIGHEST)


def per_device(dosage_words, sample_weight, variant_weight, omega):
    rows_local, width = dosage_words.shape
    rows_all = rows_local * lax.axis_size("row")
    cols_all = PLACES * width * lax.axis_size("col")
    dosage = [
        jnp.bitwise_and(jnp.right_shift(dosage_words, 2 * place), 3).astype(jnp.float32)
        for place in range(PLACES)
    ]
    sums = jnp.concatenate(
        [jnp.sum(part, axis=0) for part in dosage]
        + [jnp.sum(part * part, axis=0) for part in dosage]
    )
    totals, squares = doubled_sum(sums.reshape(-1, 128), "row").reshape(2, PLACES * width)
    column_mean = totals / rows_all
    column_scale = lax.rsqrt(squares / rows_all - column_mean * column_mean + EPSILON)
    matrix = standardize(
        dosage_words, sample_weight, column_mean, column_scale * variant_weight
    )

    sketch_part = jnp.dot(matrix, omega, preferred_element_type=jnp.float32)
    sketch = exchanged_gather(exchanged_scatter(sketch_part, "col"), "col")
    gram = unpack_upper(doubled_sum(pack(local_gram(sketch)), "row"))
    first = apply_factor(sketch, inverse_factor(gram)).astype(jnp.bfloat16)

    back_part = lax.dot_general(
        matrix, first, CONTRACT_ROWS, preferred_element_type=jnp.float32
    ).astype(jnp.bfloat16)
    back = exchanged_gather(exchanged_scatter(back_part, "row").astype(jnp.bfloat16), "row")

    both = jnp.concatenate(
        [
            jnp.dot(matrix, back, preferred_element_type=jnp.float32),
            lax.dot_general(back, back, CONTRACT_ROWS, preferred_element_type=jnp.float32),
        ],
        axis=0,
    )
    both = exchanged_gather(exchanged_scatter(both, "col"), "col")
    product = both[:rows_local]

    gathered = exchanged_gather(pack(local_gram(product))[None], "row")
    inverse = inverse_factor(both[rows_local:])
    right_full = apply_factor(back.astype(jnp.float32), inverse)
    product = apply_factor(product, inverse)
    gram = symmetric(unpack_upper(jnp.sum(gathered, axis=0)))
    gram = apply_factor(jnp.dot(inverse, gram, precision=HIGHEST), inverse)
    second = apply_factor(product, inverse_factor(gram))
    own = rows_local // lax.axis_size("col")
    second_own = lax.dynamic_slice_in_dim(second, lax.axis_index("col") * own, own, 0)

    projection_part = lax.dot_general(
        second.astype(jnp.bfloat16), matrix, CONTRACT_ROWS, preferred_element_type=jnp.float32
    ).astype(jnp.bfloat16)
    projection = exchanged_scatter(projection_part, "row").T
    return (second_own * math.sqrt(rows_all), right_full * math.sqrt(cols_all), projection)


def solution(mesh):
    in_specs = (P("row", "col"), P("row"), P("col"), P("col", None))
    out_specs = (P(("row", "col"), None), P("col", None), P("col", "row"))
    return jax.shard_map(
        per_device, mesh=mesh, in_specs=in_specs, out_specs=out_specs, check_vma=False
    )
```

time: 425 us -> 294 us (0.69)
  the two profiles are of different devices: /device:TPU:32 before, /device:TPU:2 now
where the time goes in v2:
time: 294 us; the launch traced here: 293 us
  blocking collectives  113 us (38%)
  starting transfers between devices  69.3 us (24%)
  waiting for transfers between devices  68.2 us (23%)
  Pallas kernels  25.2 us (9%)
  matrix products  8.05 us (3%)
  local copies, waits for them, and re-layouts  4.43 us (2%)
  other arithmetic  4.18 us (1%)
    all_to_all x6, blocking collectives, exchange(): return lax.all_to_all(blocks, axis, split_axis=0, concat_axis=0, tiled=True)  113 us
    ppermute x8, starting transfers between devices, doubled_sum(): panel = panel + lax.ppermute(panel, axis, pairs)  56.7 us
    all_to_all x2, waiting for transfers between devices, exchange(): return lax.all_to_all(blocks, axis, split_axis=0, concat_axis=0, tiled=True)  48.6 us
    pallas_call x3, Pallas kernels, inverse_factor(): pl.pallas_call(inverse_factor_kernel, out_shape=jax.ShapeDtypeStruct(gram...  24.5 us
    ppermute x8, waiting for transfers between devices, doubled_sum(): panel = panel + lax.ppermute(panel, axis, pairs)  19.5 us
    all_to_all x2, starting transfers between devices, exchange(): return lax.all_to_all(blocks, axis, split_axis=0, concat_axis=0, tiled=True)  12.6 us
  transfers between devices with their start and end apart: 10, of which 10 were waited for; matrix products, arithmetic and copies ran while one was open for 1% of the time, Pallas kernels for 3%

profile of v2, /device:TPU:2, one launch (start us, length us, event | category | flops | bytes accessed | tf_op | source)
XLA Modules:
  0.0 293.1 jit_solution(8736943743477895384)
XLA Ops:
  0.6 1.7 multiply_reduce_fusion
  2.4 3.8 %collective-permute-start = (f32[24,128]{1,0:T(8,128)S(1)}, f32[24,128]{1,0:T(8,128)S(1)}, u32[]{:S(2)}, u32[]{:S(2)}) collective-permute-start(f32[24,128]{1,0:T(8,128)S(1)} %concatenate.91), channel_id=1, source_target_pairs={{0,32},{32,0},{64,96},{96,64},{128,160},{160,128},{192,224},{224,1... | collective-permute-start | bytes 36872 | tf_op jit(solution)/shard_map/ppermute | solution.py:39
  6.3 1.8 collective-permute-done
  8.0 5.2 %collective-permute-start.1 = (f32[24,128]{1,0:T(8,128)S(1)}, f32[24,128]{1,0:T(8,128)S(1)}, u32[]{:S(2)}, u32[]{:S(2)}) collective-permute-start(f32[24,128]{1,0:T(8,128)S(1)} %add.52), channel_id=1, source_target_pairs={{0,64},{32,96},{64,0},{96,32},{128,192},{160,224},{192,128},{224,1... | collective-permute-start | bytes 36872 | tf_op jit(solution)/shard_map/ppermute | solution.py:39
  13.2 1.7 collective-permute-done.1
  14.9 9.1 %collective-permute-start.2 = (f32[24,128]{1,0:T(8,128)S(1)}, f32[24,128]{1,0:T(8,128)S(1)}, u32[]{:S(2)}, u32[]{:S(2)}) collective-permute-start(f32[24,128]{1,0:T(8,128)S(1)} %add.53), channel_id=1, source_target_pairs={{0,128},{32,160},{64,192},{96,224},{128,0},{160,32},{192,64},{224,... | collective-permute-start | bytes 36872 | tf_op jit(solution)/shard_map/ppermute | solution.py:39
  23.9 1.7 collective-permute-done.2
  25.6 14.1 %collective-permute-start.3 = (f32[24,128]{1,0:T(8,128)S(1)}, f32[24,128]{1,0:T(8,128)S(1)}, u32[]{:S(2)}, u32[]{:S(2)}) collective-permute-start(f32[24,128]{1,0:T(8,128)S(1)} %add.54), channel_id=1, source_target_pairs={{0,256},{32,288},{64,320},{96,352},{128,384},{160,416},{192,448},{... | collective-permute-start | bytes 36872 | tf_op jit(solution)/shard_map/ppermute | solution.py:39
  39.7 0.8 copy.15.weight_ref
  40.5 0.8 collective-permute-done.3
  41.4 0.7 fusion.11
  42.1 1.0 copy-done.1
  43.1 0.7 standardize.1
  43.9 0.6 fusion.17
  44.5 15.1 %all_to_all.40 = f32[32,16,128]{2,1,0:T(8,128)S(1)} all-to-all(f32[32,16,128]{2,1,0:T(8,128)S(1)} %bitcast.62), channel_id=1, replica_groups=mesh['row'=16,'col'=32] {'col'}, dimensions={0} | all-to-all | bytes 524288 | tf_op jit(solution)/shard_map/all_to_all | solution.py:19
  59.7 12.5 %all_to_all.41 = f32[32,16,128]{2,1,0:T(8,128)S(1)} all-to-all(f32[32,16,128]{2,1,0:T(8,128)S(1)} %broadcast_in_dim.14), channel_id=1, replica_groups=mesh['row'=16,'col'=32] {'col'}, dimensions={0} | all-to-all | bytes 524288 | tf_op jit(solution)/shard_map/all_to_all | solution.py:19
  72.1 0.6 convolution_bitcast_fusion.1
  72.7 0.1 fusion.14
  72.9 0.1 maximum_maximum_fusion
  73.0 2.9 collective-permute-start.4
  75.9 3.0 %collective-permute-done.4 = f32[80,128]{1,0:T(8,128)S(1)} collective-permute-done((f32[80,128]{1,0:T(8,128)S(1)}, f32[80,128]{1,0:T(8,128)S(1)}, u32[]{:S(2)}, u32[]{:S(2)}) %collective-permute-start.4) | collective-permute-done | bytes 40992 | tf_op jit(solution)/shard_map/ppermute | solution.py:39
  78.9 0.1 fusion.42
  79.0 3.5 %collective-permute-start.5 = (f32[80,128]{1,0:T(8,128)S(1)}, f32[80,128]{1,0:T(8,128)S(1)}, u32[]{:S(2)}, u32[]{:S(2)}) collective-permute-start(f32[80,128]{1,0:T(8,128)S(1)} %fusion.42), channel_id=1, source_target_pairs={{0,64},{32,96},{64,0},{96,32},{128,192},{160,224},{192,128},{224,1... | collective-permute-start | bytes 122888 | tf_op jit(solution)/shard_map/ppermute | solution.py:39
  82.5 3.3 %collective-permute-done.5 = f32[80,128]{1,0:T(8,128)S(1)} collective-permute-done((f32[80,128]{1,0:T(8,128)S(1)}, f32[80,128]{1,0:T(8,128)S(1)}, u32[]{:S(2)}, u32[]{:S(2)}) %collective-permute-start.5) | collective-permute-done | bytes 40992 | tf_op jit(solution)/shard_map/ppermute | solution.py:39
  85.8 6.8 %collective-permute-start.6 = (f32[80,128]{1,0:T(8,128)S(1)}, f32[80,128]{1,0:T(8,128)S(1)}, u32[]{:S(2)}, u32[]{:S(2)}) collective-permute-start(f32[80,128]{1,0:T(8,128)S(1)} %add.60), channel_id=1, source_target_pairs={{0,128},{32,160},{64,192},{96,224},{128,0},{160,32},{192,64},{224,... | collective-permute-start | bytes 122888 | tf_op jit(solution)/shard_map/ppermute | solution.py:39
  92.5 4.2 %collective-permute-done.6 = f32[80,128]{1,0:T(8,128)S(1)} collective-permute-done((f32[80,128]{1,0:T(8,128)S(1)}, f32[80,128]{1,0:T(8,128)S(1)}, u32[]{:S(2)}, u32[]{:S(2)}) %collective-permute-start.6) | collective-permute-done | bytes 40992 | tf_op jit(solution)/shard_map/ppermute | solution.py:39
  96.8 11.4 %collective-permute-start.7 = (f32[80,128]{1,0:T(8,128)S(1)}, f32[80,128]{1,0:T(8,128)S(1)}, u32[]{:S(2)}, u32[]{:S(2)}) collective-permute-start(f32[80,128]{1,0:T(8,128)S(1)} %add.61), channel_id=1, source_target_pairs={{0,256},{32,288},{64,320},{96,352},{128,384},{160,416},{192,448},{... | collective-permute-start | bytes 122888 | tf_op jit(solution)/shard_map/ppermute | solution.py:39
  108.2 3.2 %collective-permute-done.7 = f32[80,128]{1,0:T(8,128)S(1)} collective-permute-done((f32[80,128]{1,0:T(8,128)S(1)}, f32[80,128]{1,0:T(8,128)S(1)}, u32[]{:S(2)}, u32[]{:S(2)}) %collective-permute-start.7) | collective-permute-done | bytes 40992 | tf_op jit(solution)/shard_map/ppermute | solution.py:39
  111.5 0.1 constant_dynamic-update-slice_fusion.3
  111.6 0.1 constant_dynamic-update-slice_fusion.2
  111.7 0.1 constant_dynamic-update-slice_fusion.1
  111.7 0.1 constant_dynamic-update-slice_fusion.gram_ref
  111.8 8.2 %inverse_factor.3 = f32[128,128]{1,0:T(8,128)S(1)} custom-call(f32[128,128]{1,0:T(8,128)S(1)} %constant_dynamic-update-slice_fusion.gram_ref), custom_call_target="tpu_custom_call" | custom-call | flops 4000000000 | bytes 30000000 | tf_op jit(solution)/shard_map/inverse_factor/pallas_call | solution.py:134
  120.0 0.4 convolution_convert_fusion.2
  120.4 0.6 convolution_convert_fusion.1
  121.0 30.5 %all_to_all.42 = bf16[16,96,128]{2,1,0:T(8,128)(2,1)S(1)} all-to-all(bf16[16,96,128]{2,1,0:T(8,128)(2,1)S(1)} %bitcast.61), channel_id=1, replica_groups=mesh['row'=16,'col'=32] {'row'}, dimensions={0} | all-to-all | bytes 786432 | tf_op jit(solution)/shard_map/all_to_all | solution.py:19
  151.6 26.9 %all_to_all.43 = bf16[16,96,128]{2,1,0:T(8,128)(2,1)S(1)} all-to-all(bf16[16,96,128]{2,1,0:T(8,128)(2,1)S(1)} %broadcast_in_dim.15), channel_id=1, replica_groups=mesh['row'=16,'col'=32] {'row'}, dimensions={0} | all-to-all | bytes 786432 | tf_op jit(solution)/shard_map/all_to_all | solution.py:19
  178.5 0.6 fusion.18
  179.1 0.3 convolution_bitcast_fusion
  179.5 14.1 %all_to_all.44 = f32[32,20,128]{2,1,0:T(8,128)S(1)} all-to-all(f32[32,20,128]{2,1,0:T(8,128)S(1)} %reshape.76), channel_id=1, replica_groups=mesh['row'=16,'col'=32] {'col'}, dimensions={0} | all-to-all | bytes 655360 | tf_op jit(solution)/shard_map/all_to_all | solution.py:19
  193.6 13.8 %all_to_all.45 = f32[32,20,128]{2,1,0:T(8,128)S(1)} all-to-all(f32[32,20,128]{2,1,0:T(8,128)S(1)} %broadcast_in_dim.16), channel_id=1, replica_groups=mesh['row'=16,'col'=32] {'col'}, dimensions={0} | all-to-all | bytes 655360 | tf_op jit(solution)/shard_map/all_to_all | solution.py:19
  207.4 0.6 fusion.1
  208.0 0.1 fusion.13
  208.2 0.1 maximum_maximum_fusion.1
  208.3 0.9 broadcast_in_dim.17
  209.2 6.6 %all-to-all-start.6 = ((f32[16,1,80,128]{3,2,1,0:T(8,128)}), f32[16,1,80,128]{3,2,1,0:T(8,128)S(1)}, u32[]{:S(2)}, u32[]{:S(2)}) async-start(f32[16,1,80,128]{3,2,1,0:T(8,128)} %broadcast_in_dim.17), calls=%async_computation.6 | async-start | bytes 1310720 | tf_op jit(solution)/shard_map/all_to_all | solution.py:19
  215.8 8.2 %inverse_factor.4 = f32[128,128]{1,0:T(8,128)S(1)} custom-call(f32[128,128]{1,0:T(8,128)S(1)} %slice.101.gram_ref), custom_call_target="tpu_custom_call" | custom-call | flops 4000000000 | bytes 30000000 | tf_op jit(solution)/shard_map/inverse_factor/pallas_call | solution.py:134
  224.0 1.1 fusion.3
  225.0 26.4 %all-to-all-done.6 = f32[16,1,80,128]{3,2,1,0:T(8,128)S(1)} async-done(((f32[16,1,80,128]{3,2,1,0:T(8,128)}), f32[16,1,80,128]{3,2,1,0:T(8,128)S(1)}, u32[]{:S(2)}, u32[]{:S(2)}) %all-to-all-start.6) | async-done | bytes 655392 | tf_op jit(solution)/shard_map/all_to_all | solution.py:19
  251.6 0.1 constant_dynamic-update-slice_fusion.8
  251.7 0.1 constant_dynamic-update-slice_fusion.7
  251.8 0.1 constant_dynamic-update-slice_fusion.6
  251.8 0.1 constant_dynamic-update-slice_fusion.5
  251.9 0.1 copy.16
  252.0 0.2 fusion.6
  252.2 0.3 fusion.19.gram_ref
  252.5 8.2 %inverse_factor.5 = f32[128,128]{1,0:T(8,128)S(1)} custom-call(f32[128,128]{1,0:T(8,128)S(1)} %fusion.19.gram_ref), custom_call_target="tpu_custom_call" | custom-call | flops 4000000000 | bytes 30000000 | tf_op jit(solution)/shard_map/inverse_factor/pallas_call | solution.py:134
  260.7 0.4 fusion.20
  261.1 1.1 fusion
  262.2 6.0 %all-to-all-start.7 = ((bf16[16,8,1536]{2,1,0:T(8,128)(2,1)}), bf16[16,8,1536]{2,1,0:T(8,128)(2,1)S(1)}, u32[]{:S(2)}, u32[]{:S(2)}) async-start(bf16[16,8,1536]{2,1,0:T(8,128)(2,1)} %fusion), calls=%async_computation.7 | async-start | bytes 786432 | tf_op jit(solution)/shard_map/all_to_all | solution.py:19
  268.2 1.4 convolution_multiply_fusion
  269.6 0.6 dynamic-slice_multiply_fusion
  270.2 22.2 %all-to-all-done.7 = bf16[16,8,1536]{2,1,0:T(8,128)(2,1)S(1)} async-done(((bf16[16,8,1536]{2,1,0:T(8,128)(2,1)}), bf16[16,8,1536]{2,1,0:T(8,128)(2,1)S(1)}, u32[]{:S(2)}, u32[]{:S(2)}) %all-to-all-start.7) | async-done | bytes 393248 | tf_op jit(solution)/shard_map/all_to_all | solution.py:19
  292.4 0.7 convert_reduce_fusion
  (41 shorter events, 1.1 us)
Async XLA Ops:
  0.6 43.3 %copy-start = (bf16[1536,128]{1,0:T(8,128)(2,1)S(1)}, bf16[1536,128]{1,0:T(8,128)(2,1)}, u32[]{:S(2)}) copy-start(bf16[1536,128]{1,0:T(8,128)(2,1)} %param.7) | copy-start | bytes 1179652
  2.4 5.6 %collective-permute-start = (f32[24,128]{1,0:T(8,128)S(1)}, f32[24,128]{1,0:T(8,128)S(1)}, u32[]{:S(2)}, u32[]{:S(2)}) collective-permute-start(f32[24,128]{1,0:T(8,128)S(1)} %concatenate.91), channel_id=1, source_target_pairs={{0,32},{32,0},{64,96},{96,64},{128,160},{160,128},{192,224},{224,1... | collective-permute-start | bytes 36872 | tf_op jit(solution)/shard_map/ppermute | solution.py:39
  8.0 6.8 %collective-permute-start.1 = (f32[24,128]{1,0:T(8,128)S(1)}, f32[24,128]{1,0:T(8,128)S(1)}, u32[]{:S(2)}, u32[]{:S(2)}) collective-permute-start(f32[24,128]{1,0:T(8,128)S(1)} %add.52), channel_id=1, source_target_pairs={{0,64},{32,96},{64,0},{96,32},{128,192},{160,224},{192,128},{224,1... | collective-permute-start | bytes 36872 | tf_op jit(solution)/shard_map/ppermute | solution.py:39
  14.9 10.8 %collective-permute-start.2 = (f32[24,128]{1,0:T(8,128)S(1)}, f32[24,128]{1,0:T(8,128)S(1)}, u32[]{:S(2)}, u32[]{:S(2)}) collective-permute-start(f32[24,128]{1,0:T(8,128)S(1)} %add.53), channel_id=1, source_target_pairs={{0,128},{32,160},{64,192},{96,224},{128,0},{160,32},{192,64},{224,... | collective-permute-start | bytes 36872 | tf_op jit(solution)/shard_map/ppermute | solution.py:39
  25.6 15.8 %collective-permute-start.3 = (f32[24,128]{1,0:T(8,128)S(1)}, f32[24,128]{1,0:T(8,128)S(1)}, u32[]{:S(2)}, u32[]{:S(2)}) collective-permute-start(f32[24,128]{1,0:T(8,128)S(1)} %add.54), channel_id=1, source_target_pairs={{0,256},{32,288},{64,320},{96,352},{128,384},{160,416},{192,448},{... | collective-permute-start | bytes 36872 | tf_op jit(solution)/shard_map/ppermute | solution.py:39
  42.1 1.0 copy-start.1
  73.0 5.9 %collective-permute-start.4 = (f32[80,128]{1,0:T(8,128)S(1)}, f32[80,128]{1,0:T(8,128)S(1)}, u32[]{:S(2)}, u32[]{:S(2)}) collective-permute-start(f32[80,128]{1,0:T(8,128)S(1)} %maximum_maximum_fusion), channel_id=1, source_target_pairs={{0,32},{32,0},{64,96},{96,64},{128,160},{160,128},{192,224},{224,1... | collective-permute-start | bytes 122888 | tf_op jit(solution)/shard_map/ppermute | solution.py:39
  79.0 6.8 %collective-permute-start.5 = (f32[80,128]{1,0:T(8,128)S(1)}, f32[80,128]{1,0:T(8,128)S(1)}, u32[]{:S(2)}, u32[]{:S(2)}) collective-permute-start(f32[80,128]{1,0:T(8,128)S(1)} %fusion.42), channel_id=1, source_target_pairs={{0,64},{32,96},{64,0},{96,32},{128,192},{160,224},{192,128},{224,1... | collective-permute-start | bytes 122888 | tf_op jit(solution)/shard_map/ppermute | solution.py:39
  85.8 11.0 %collective-permute-start.6 = (f32[80,128]{1,0:T(8,128)S(1)}, f32[80,128]{1,0:T(8,128)S(1)}, u32[]{:S(2)}, u32[]{:S(2)}) collective-permute-start(f32[80,128]{1,0:T(8,128)S(1)} %add.60), channel_id=1, source_target_pairs={{0,128},{32,160},{64,192},{96,224},{128,0},{160,32},{192,64},{224,... | collective-permute-start | bytes 122888 | tf_op jit(solution)/shard_map/ppermute | solution.py:39
  96.8 14.6 %collective-permute-start.7 = (f32[80,128]{1,0:T(8,128)S(1)}, f32[80,128]{1,0:T(8,128)S(1)}, u32[]{:S(2)}, u32[]{:S(2)}) collective-permute-start(f32[80,128]{1,0:T(8,128)S(1)} %add.61), channel_id=1, source_target_pairs={{0,256},{32,288},{64,320},{96,352},{128,384},{160,416},{192,448},{... | collective-permute-start | bytes 122888 | tf_op jit(solution)/shard_map/ppermute | solution.py:39
  209.2 42.2 %all-to-all-start.6 = ((f32[16,1,80,128]{3,2,1,0:T(8,128)}), f32[16,1,80,128]{3,2,1,0:T(8,128)S(1)}, u32[]{:S(2)}, u32[]{:S(2)}) async-start(f32[16,1,80,128]{3,2,1,0:T(8,128)} %broadcast_in_dim.17), calls=%async_computation.6 | async-start | bytes 1310720 | tf_op jit(solution)/shard_map/all_to_all | solution.py:19
  252.5 8.2 %copy-start.2 = (f32[512,128]{1,0:T(8,128)S(1)}, f32[512,128]{1,0:T(8,128)}, u32[]{:S(2)}) copy-start(f32[512,128]{1,0:T(8,128)} %fusion.3) | copy-start | bytes 786436
  262.2 30.2 %all-to-all-start.7 = ((bf16[16,8,1536]{2,1,0:T(8,128)(2,1)}), bf16[16,8,1536]{2,1,0:T(8,128)(2,1)S(1)}, u32[]{:S(2)}, u32[]{:S(2)}) async-start(bf16[16,8,1536]{2,1,0:T(8,128)(2,1)} %fusion), calls=%async_computation.7 | async-start | bytes 786432 | tf_op jit(solution)/shard_map/all_to_all | solution.py:19

commit v3 on v2

--- a/solution.py
+++ b/solution.py
@@ -9,6 +9,7 @@
 
 EPSILON = 1e-05
 PLACES = 6
+RANK = 128
 CONTRACT_ROWS = (((0,), (0,)), ((), ()))
 HIGHEST = lax.Precision.HIGHEST
 VMEM_LIMIT = 32 * 1024 * 1024
@@ -19,26 +20,18 @@
     return lax.all_to_all(blocks, axis, split_axis=0, concat_axis=0, tiled=True)
 
 
-def exchanged_scatter(panel, axis):
-    size = lax.axis_size(axis)
-    blocks = panel.reshape((size, panel.shape[0] // size) + panel.shape[1:])
-    return jnp.sum(exchange(blocks, axis).astype(jnp.float32), axis=0)
-
-
 def exchanged_gather(block, axis):
     size = lax.axis_size(axis)
-    gathered = exchange(jnp.broadcast_to(block[None], (size,) + block.shape), axis)
-    return gathered.reshape((size * block.shape[0],) + block.shape[1:])
-
-
-def doubled_sum(panel, axis):
-    size = lax.axis_size(axis)
-    distance = 1
-    while distance < size:
-        pairs = [(index, index ^ distance) for index in range(size)]
-        panel = panel + lax.ppermute(panel, axis, pairs)
-        distance *= 2
-    return panel
+    return exchange(jnp.broadcast_to(block[None], (size,) + block.shape), axis)
+
+
+def halves(values, count):
+    terms = []
+    for index in range(count):
+        term = lax.reduce_precision(values, exponent_bits=8, mantissa_bits=7)
+        values = values - term
+        terms.append(term.astype(jnp.bfloat16))
+    return terms
 
 
 def pack(gram):
@@ -183,6 +176,10 @@
     return lax.dot_general(panel, inverse, (((1,), (1,)), ((), ())), precision=HIGHEST)
 
 
+def congruent(gram, factor):
+    return apply_factor(jnp.dot(factor, gram, precision=HIGHEST), factor)
+
+
 def local_gram(panel):
     return lax.dot_general(panel, panel, CONTRACT_ROWS, precision=HIGHEST)
 
@@ -199,47 +196,96 @@
         [jnp.sum(part, axis=0) for part in dosage]
         + [jnp.sum(part * part, axis=0) for part in dosage]
     )
-    totals, squares = doubled_sum(sums.reshape(-1, 128), "row").reshape(2, PLACES * width)
+    sums = jnp.sum(exchanged_gather(sums.reshape(-1, 128), "row"), axis=0)
+    totals, squares = sums.reshape(2, PLACES * width)
     column_mean = totals / rows_all
     column_scale = lax.rsqrt(squares / rows_all - column_mean * column_mean + EPSILON)
     matrix = standardize(
         dosage_words, sample_weight, column_mean, column_scale * variant_weight
     )
+    n_row, n_col = lax.axis_size("row"), lax.axis_size("col")
+    col = lax.axis_index("col")
+    own, part = rows_local // n_col, RANK // n_col
+    chunk = PLACES * width // n_row
 
     sketch_part = jnp.dot(matrix, omega, preferred_element_type=jnp.float32)
-    sketch = exchanged_gather(exchanged_scatter(sketch_part, "col"), "col")
-    gram = unpack_upper(doubled_sum(pack(local_gram(sketch)), "row"))
-    first = apply_factor(sketch, inverse_factor(gram)).astype(jnp.bfloat16)
-
-    back_part = lax.dot_general(
-        matrix, first, CONTRACT_ROWS, preferred_element_type=jnp.float32
-    ).astype(jnp.bfloat16)
-    back = exchanged_gather(exchanged_scatter(back_part, "row").astype(jnp.bfloat16), "row")
-
-    both = jnp.concatenate(
-        [
-            jnp.dot(matrix, back, preferred_element_type=jnp.float32),
-            lax.dot_general(back, back, CONTRACT_ROWS, preferred_element_type=jnp.float32),
-        ],
-        axis=0,
-    )
-    both = exchanged_gather(exchanged_scatter(both, "col"), "col")
-    product = both[:rows_local]
-
-    gathered = exchanged_gather(pack(local_gram(product))[None], "row")
-    inverse = inverse_factor(both[rows_local:])
-    right_full = apply_factor(back.astype(jnp.float32), inverse)
-    product = apply_factor(product, inverse)
-    gram = symmetric(unpack_upper(jnp.sum(gathered, axis=0)))
-    gram = apply_factor(jnp.dot(inverse, gram, precision=HIGHEST), inverse)
+    sketch_own = jnp.sum(exchange(sketch_part.reshape(n_col, own, RANK), "col"), axis=0)
+    sketch = exchanged_gather(sketch_own, "col").reshape(rows_local, RANK)
+
+    gram_share = lax.dynamic_slice_in_dim(local_gram(sketch), col * part, part, 0)
+    sketch_terms = jnp.concatenate(halves(sketch, 2), axis=1)
+    back_terms = lax.dot_general(
+        matrix, sketch_terms, CONTRACT_ROWS, preferred_element_type=jnp.float32
+    )
+    back_part = (back_terms[:, :RANK] + back_terms[:, RANK:]).astype(jnp.bfloat16)
+    share_terms = jnp.concatenate(
+        halves(gram_share, 3) + [jnp.zeros((part, RANK), jnp.bfloat16)], axis=0
+    )
+    arrived = exchange(
+        jnp.concatenate(
+            [
+                back_part.reshape(n_row, chunk, RANK),
+                jnp.broadcast_to(share_terms[None], (n_row,) + share_terms.shape),
+            ],
+            axis=1,
+        ),
+        "row",
+    )
+    arrived = jnp.sum(arrived.astype(jnp.float32), axis=0)
+    back_own = arrived[:chunk].astype(jnp.bfloat16)
+    gram_share = jnp.sum(arrived[chunk:].reshape(4, part, RANK), axis=0)
+    back = exchanged_gather(back_own, "row").reshape(n_row * chunk, RANK)
+
+    product_part = jnp.dot(matrix, back, preferred_element_type=jnp.float32)
+    back_gram = lax.dot_general(back, back, CONTRACT_ROWS, preferred_element_type=jnp.float32)
+    back_gram = lax.optimization_barrier(back_gram)
+    arrived = exchange(
+        jnp.concatenate(
+            [
+                product_part.reshape(n_col, own, RANK),
+                back_gram.reshape(n_col, part, RANK),
+                jnp.broadcast_to(gram_share[None], (n_col, part, RANK)),
+            ],
+            axis=1,
+        ),
+        "col",
+    )
+    summed = jnp.sum(arrived[:, : own + part], axis=0)
+    sketch_factor = inverse_factor(arrived[:, own + part :].reshape(RANK, RANK))
+    gathered = exchanged_gather(
+        jnp.concatenate([summed, jnp.zeros((part, RANK), jnp.float32)], axis=0), "col"
+    )
+    gathered, sketch_factor = lax.optimization_barrier((gathered, sketch_factor))
+    product = gathered[:, :own].reshape(rows_local, RANK)
+    back_gram = gathered[:, own : own + part].reshape(RANK, RANK)
+
+    packed = pack(local_gram(product))
+    half = packed.shape[0] // 2
+    core = lax.rem(col, 2)
+    gathered = exchanged_gather(
+        lax.dynamic_slice_in_dim(packed, core * half, half, 0), "row"
+    )
+    back_factor = inverse_factor(congruent(back_gram, sketch_factor))
+    factor = jnp.dot(back_factor, sketch_factor, precision=HIGHEST)
+    right_full = apply_factor(back.astype(jnp.float32), factor)
+    product = apply_factor(product, factor)
+    gathered, product = lax.optimization_barrier((gathered, product))
+    packed = jnp.sum(gathered, axis=0)
+    other = lax.ppermute(packed, "col", [(index, index ^ 1) for index in range(n_col)])
+    packed = jnp.where(
+        core == 0,
+        jnp.concatenate([packed, other], axis=0),
+        jnp.concatenate([other, packed], axis=0),
+    )
+    gram = congruent(symmetric(unpack_upper(packed)), factor)
     second = apply_factor(product, inverse_factor(gram))
-    own = rows_local // lax.axis_size("col")
-    second_own = lax.dynamic_slice_in_dim(second, lax.axis_index("col") * own, own, 0)
+    second_own = lax.dynamic_slice_in_dim(second, col * own, own, 0)
 
     projection_part = lax.dot_general(
         second.astype(jnp.bfloat16), matrix, CONTRACT_ROWS, preferred_element_type=jnp.float32
     ).astype(jnp.bfloat16)
-    projection = exchanged_scatter(projection_part, "row").T
+    arrived = exchange(projection_part.reshape(n_row, RANK // n_row, -1), "row")
+    projection = jnp.sum(arrived.astype(jnp.float32), axis=0).T
     return (second_own * math.sqrt(rows_all), right_full * math.sqrt(cols_all), projection)
 
 

time: 294 us -> 234 us (0.80)
  blocking collectives: 113 us -> 60.8 us
  starting transfers between devices: 69.3 us -> 44.6 us
  waiting for transfers between devices: 68.2 us -> 84.3 us
    ppermute x8 -> x1, starting transfers between devices: 56.7 us -> 1.92 us  [per_device(): lax.ppermute(packed, 'col', [(index, index ^ 1) for index in range(n_col)])]
    all_to_all x6 -> x3, blocking collectives: 113 us -> 60.8 us  [exchange(): return lax.all_to_all(blocks, axis, split_axis=0, concat_axis=0, tiled=True)]
    all_to_all x2 -> x6, waiting for transfers between devices: 48.6 us -> 83.1 us  [exchange(): return lax.all_to_all(blocks, axis, split_axis=0, concat_axis=0, tiled=True)]
    all_to_all x2 -> x6, starting transfers between devices: 12.6 us -> 42.7 us  [exchange(): return lax.all_to_all(blocks, axis, split_axis=0, concat_axis=0, tiled=True)]
    ppermute x8 -> x1, waiting for transfers between devices: 19.5 us -> 1.15 us  [per_device(): lax.ppermute(packed, 'col', [(index, index ^ 1) for index in range(n_col)])]
  transfers between devices with their start and end apart: 10 -> 7, of which waited for: 10 -> 7; matrix products, arithmetic and copies ran while one was open for 1% -> 2% of each run, Pallas kernels for 3% -> 7%
where the time goes in v3:
time: 234 us; the launch traced here: 233 us
  waiting for transfers between devices  84.3 us (36%)
  blocking collectives  60.8 us (26%)
  starting transfers between devices  44.6 us (19%)
  Pallas kernels  25.2 us (11%)
  matrix products  7.66 us (3%)
  local copies, waits for them, and re-layouts  5.81 us (2%)
  other arithmetic  3.64 us (2%)
    all_to_all x6, waiting for transfers between devices, exchange(): return lax.all_to_all(blocks, axis, split_axis=0, concat_axis=0, tiled=True)  83.1 us
    all_to_all x3, blocking collectives, exchange(): return lax.all_to_all(blocks, axis, split_axis=0, concat_axis=0, tiled=True)  60.8 us
    all_to_all x6, starting transfers between devices, exchange(): return lax.all_to_all(blocks, axis, split_axis=0, concat_axis=0, tiled=True)  42.7 us
    pallas_call x3, Pallas kernels, inverse_factor(): pl.pallas_call(inverse_factor_kernel, out_shape=jax.ShapeDtypeStruct(gram...  24.5 us
  transfers between devices with their start and end apart: 7, of which 7 were waited for; matrix products, arithmetic and copies ran while one was open for 2% of the time, Pallas kernels for 7%

profile of v3, /device:TPU:2, one launch (start us, length us, event | category | flops | bytes accessed | tf_op | source)
XLA Modules:
  0.0 233.1 jit_solution(13234516891029177546)
XLA Ops:
  0.6 0.0 copy-start
  0.7 1.7 multiply_reduce_fusion
  2.4 0.1 concatenate.85
  2.5 0.7 broadcast_in_dim.21
  3.2 15.2 %all-to-all-start = ((f32[16,24,128]{2,1,0:T(8,128)}), f32[16,24,128]{2,1,0:T(8,128)S(1)}, u32[]{:S(2)}, u32[]{:S(2)}) async-start(f32[16,24,128]{2,1,0:T(8,128)} %broadcast_in_dim.21), calls=%async_computation | async-start | bytes 393216 | tf_op jit(solution)/shard_map/all_to_all | solution.py:20
  18.4 0.8 copy.19.weight_ref
  19.2 15.6 %all-to-all-done = f32[16,24,128]{2,1,0:T(8,128)S(1)} async-done(((f32[16,24,128]{2,1,0:T(8,128)}), f32[16,24,128]{2,1,0:T(8,128)S(1)}, u32[]{:S(2)}, u32[]{:S(2)}) %all-to-all-start) | async-done | bytes 196640 | tf_op jit(solution)/shard_map/all_to_all | solution.py:20
  34.9 0.7 standardize.1
  35.7 0.6 fusion.26
  36.2 15.1 %all_to_all.45 = f32[32,16,128]{2,1,0:T(8,128)S(1)} all-to-all(f32[32,16,128]{2,1,0:T(8,128)S(1)} %bitcast.81), channel_id=1, replica_groups=mesh['row'=16,'col'=32] {'col'}, dimensions={0} | all-to-all | bytes 524288 | tf_op jit(solution)/shard_map/all_to_all | solution.py:20
  51.4 0.7 broadcast_in_dim.23
  52.1 5.0 %all-to-all-start.2 = ((f32[32,16,128]{2,1,0:T(8,128)}), f32[32,16,128]{2,1,0:T(8,128)S(1)}, u32[]{:S(2)}, u32[]{:S(2)}) async-start(f32[32,16,128]{2,1,0:T(8,128)} %broadcast_in_dim.23), calls=%async_computation.2 | async-start | bytes 524288 | tf_op jit(solution)/shard_map/all_to_all | solution.py:20
  57.1 0.1 pad.22.clone
  57.2 7.7 %all-to-all-done.2 = f32[32,16,128]{2,1,0:T(8,128)S(1)} async-done(((f32[32,16,128]{2,1,0:T(8,128)}), f32[32,16,128]{2,1,0:T(8,128)S(1)}, u32[]{:S(2)}, u32[]{:S(2)}) %all-to-all-start.2) | async-done | bytes 262176 | tf_op jit(solution)/shard_map/all_to_all | solution.py:20
  64.9 0.6 fusion.4
  65.6 0.1 fusion.1
  65.7 0.6 convolution_bitcast_fusion.2
  66.3 0.1 maximum_maximum_fusion
  66.4 32.1 %all_to_all.46 = bf16[16,112,128]{2,1,0:T(8,128)(2,1)S(1)} all-to-all(bf16[16,112,128]{2,1,0:T(8,128)(2,1)S(1)} %pad_maximum_fusion), channel_id=1, replica_groups=mesh['row'=16,'col'=32] {'row'}, dimensions={0} | all-to-all | bytes 917504 | tf_op jit(solution)/shard_map/all_to_all | solution.py:20
  98.5 0.1 convert_reduce_fusion
  98.6 0.8 broadcast_in_dim.26
  99.4 5.8 %all-to-all-start.4 = ((bf16[16,96,128]{2,1,0:T(8,128)(2,1)}), bf16[16,96,128]{2,1,0:T(8,128)(2,1)S(1)}, u32[]{:S(2)}, u32[]{:S(2)}) async-start(bf16[16,96,128]{2,1,0:T(8,128)(2,1)} %broadcast_in_dim.26), calls=%async_computation.4 | async-start | bytes 786432 | tf_op jit(solution)/shard_map/all_to_all | solution.py:20
  105.2 24.2 %all-to-all-done.4 = bf16[16,96,128]{2,1,0:T(8,128)(2,1)S(1)} async-done(((bf16[16,96,128]{2,1,0:T(8,128)(2,1)}), bf16[16,96,128]{2,1,0:T(8,128)(2,1)S(1)}, u32[]{:S(2)}, u32[]{:S(2)}) %all-to-all-start.4) | async-done | bytes 393248 | tf_op jit(solution)/shard_map/all_to_all | solution.py:20
  129.4 0.3 convolution_bitcast_fusion.1
  129.7 0.6 fusion.27
  130.4 13.6 %all_to_all.47 = f32[32,24,128]{2,1,0:T(8,128)S(1)} all-to-all(f32[32,24,128]{2,1,0:T(8,128)S(1)} %pad_maximum_fusion.1), channel_id=1, replica_groups=mesh['row'=16,'col'=32] {'col'}, dimensions={0} | all-to-all | bytes 786432 | tf_op jit(solution)/shard_map/all_to_all | solution.py:20
  144.0 0.8 broadcast_in_dim.28
  144.8 5.0 %all-to-all-start.6 = ((f32[32,24,128]{2,1,0:T(8,128)}), f32[32,24,128]{2,1,0:T(8,128)S(1)}, u32[]{:S(2)}, u32[]{:S(2)}) async-start(f32[32,24,128]{2,1,0:T(8,128)} %broadcast_in_dim.28), calls=%async_computation.6 | async-start | bytes 786432 | tf_op jit(solution)/shard_map/all_to_all | solution.py:20
  149.8 8.2 %inverse_factor.3 = f32[128,128]{1,0:T(8,128)S(1)} custom-call(f32[128,128]{1,0:T(8,128)S(1)} %bitcast.76), custom_call_target="tpu_custom_call" | custom-call | flops 4000000000 | bytes 30000000 | tf_op jit(solution)/shard_map/inverse_factor/pallas_call | solution.py:127
  157.9 1.0 all-to-all-done.6
  159.0 0.1 copy.20
  159.0 0.6 convolution_bitcast_fusion
  159.7 0.1 slice.86
  159.7 0.1 slice.85
  159.8 0.1 fusion.24
  159.9 0.2 copy.21
  160.1 0.1 fusion.11
  160.2 0.7 broadcast_in_dim.29
  160.9 5.7 %all-to-all-start.7 = ((f32[16,40,128]{2,1,0:T(8,128)}), f32[16,40,128]{2,1,0:T(8,128)S(1)}, u32[]{:S(2)}, u32[]{:S(2)}) async-start(f32[16,40,128]{2,1,0:T(8,128)} %broadcast_in_dim.29), calls=%async_computation.7 | async-start | bytes 655360 | tf_op jit(solution)/shard_map/all_to_all | solution.py:20
  166.7 0.2 fusion.28
  166.9 0.3 fusion.29.gram_ref
  167.1 8.2 %inverse_factor.4 = f32[128,128]{1,0:T(8,128)S(1)} custom-call(f32[128,128]{1,0:T(8,128)S(1)} %fusion.29.gram_ref), custom_call_target="tpu_custom_call" | custom-call | flops 4000000000 | bytes 30000000 | tf_op jit(solution)/shard_map/inverse_factor/pallas_call | solution.py:127
  175.3 0.2 fusion.30
  175.5 0.4 fusion.31
  175.9 12.3 %all-to-all-done.7 = f32[16,40,128]{2,1,0:T(8,128)S(1)} async-done(((f32[16,40,128]{2,1,0:T(8,128)}), f32[16,40,128]{2,1,0:T(8,128)S(1)}, u32[]{:S(2)}, u32[]{:S(2)}) %all-to-all-start.7) | async-done | bytes 327712 | tf_op jit(solution)/shard_map/all_to_all | solution.py:20
  188.2 1.9 collective-permute-start
  190.2 1.1 collective-permute-done
  191.3 0.1 slice.90
  191.4 0.1 fusion.25
  191.5 0.1 pad_dynamic-update-slice_fusion.1
  191.6 0.1 constant_dynamic-update-slice_fusion.1
  191.6 0.1 constant_dynamic-update-slice_fusion
  191.7 0.1 pad_dynamic-update-slice_fusion
  191.8 0.1 copy.22
  191.9 0.2 fusion.9
  192.1 0.3 fusion.32.gram_ref
  192.4 8.2 %inverse_factor.5 = f32[128,128]{1,0:T(8,128)S(1)} custom-call(f32[128,128]{1,0:T(8,128)S(1)} %fusion.32.gram_ref), custom_call_target="tpu_custom_call" | custom-call | flops 4000000000 | bytes 30000000 | tf_op jit(solution)/shard_map/inverse_factor/pallas_call | solution.py:127
  200.5 0.4 fusion.33
  200.9 1.1 fusion
  202.1 6.0 %all-to-all-start.8 = ((bf16[16,8,1536]{2,1,0:T(8,128)(2,1)}), bf16[16,8,1536]{2,1,0:T(8,128)(2,1)S(1)}, u32[]{:S(2)}, u32[]{:S(2)}) async-start(bf16[16,8,1536]{2,1,0:T(8,128)(2,1)} %fusion), calls=%async_computation.8 | async-start | bytes 786432 | tf_op jit(solution)/shard_map/all_to_all | solution.py:20
  208.1 1.4 convolution_multiply_fusion
  209.5 0.6 dynamic-slice_multiply_fusion
  210.1 22.3 %all-to-all-done.8 = bf16[16,8,1536]{2,1,0:T(8,128)(2,1)S(1)} async-done(((bf16[16,8,1536]{2,1,0:T(8,128)(2,1)}), bf16[16,8,1536]{2,1,0:T(8,128)(2,1)S(1)}, u32[]{:S(2)}, u32[]{:S(2)}) %all-to-all-start.8) | async-done | bytes 393248 | tf_op jit(solution)/shard_map/all_to_all | solution.py:20
  232.4 0.7 convert_reduce_fusion.1
  (31 shorter events, 0.4 us)
Async XLA Ops:
  0.6 35.0 %copy-start = (bf16[1536,128]{1,0:T(8,128)(2,1)S(1)}, bf16[1536,128]{1,0:T(8,128)(2,1)}, u32[]{:S(2)}) copy-start(bf16[1536,128]{1,0:T(8,128)(2,1)} %param.7) | copy-start | bytes 1179652
  0.6 34.3 %copy-start.1 = (s32[512,256]{1,0:T(8,128)S(1)}, s32[512,256]{1,0:T(8,128)}, u32[]{:S(2)}) copy-start(s32[512,256]{1,0:T(8,128)} %words_ref.1) | copy-start | bytes 1572868
  0.7 34.2 %copy-start.2 = (f32[1536]{0:T(1024)S(1)}, f32[1536]{0:T(1024)}, u32[]{:S(2)}) copy-start(f32[1536]{0:T(1024)} %param.6) | copy-start | bytes 18436
  3.2 31.6 %all-to-all-start = ((f32[16,24,128]{2,1,0:T(8,128)}), f32[16,24,128]{2,1,0:T(8,128)S(1)}, u32[]{:S(2)}, u32[]{:S(2)}) async-start(f32[16,24,128]{2,1,0:T(8,128)} %broadcast_in_dim.21), calls=%async_computation | async-start | bytes 393216 | tf_op jit(solution)/shard_map/all_to_all | solution.py:20
  52.1 12.8 %all-to-all-start.2 = ((f32[32,16,128]{2,1,0:T(8,128)}), f32[32,16,128]{2,1,0:T(8,128)S(1)}, u32[]{:S(2)}, u32[]{:S(2)}) async-start(f32[32,16,128]{2,1,0:T(8,128)} %broadcast_in_dim.23), calls=%async_computation.2 | async-start | bytes 524288 | tf_op jit(solution)/shard_map/all_to_all | solution.py:20
  99.4 30.0 %all-to-all-start.4 = ((bf16[16,96,128]{2,1,0:T(8,128)(2,1)}), bf16[16,96,128]{2,1,0:T(8,128)(2,1)S(1)}, u32[]{:S(2)}, u32[]{:S(2)}) async-start(bf16[16,96,128]{2,1,0:T(8,128)(2,1)} %broadcast_in_dim.26), calls=%async_computation.4 | async-start | bytes 786432 | tf_op jit(solution)/shard_map/all_to_all | solution.py:20
  144.8 14.2 %all-to-all-start.6 = ((f32[32,24,128]{2,1,0:T(8,128)}), f32[32,24,128]{2,1,0:T(8,128)S(1)}, u32[]{:S(2)}, u32[]{:S(2)}) async-start(f32[32,24,128]{2,1,0:T(8,128)} %broadcast_in_dim.28), calls=%async_computation.6 | async-start | bytes 786432 | tf_op jit(solution)/shard_map/all_to_all | solution.py:20
  160.9 27.3 %all-to-all-start.7 = ((f32[16,40,128]{2,1,0:T(8,128)}), f32[16,40,128]{2,1,0:T(8,128)S(1)}, u32[]{:S(2)}, u32[]{:S(2)}) async-start(f32[16,40,128]{2,1,0:T(8,128)} %broadcast_in_dim.29), calls=%async_computation.7 | async-start | bytes 655360 | tf_op jit(solution)/shard_map/all_to_all | solution.py:20
  188.2 3.1 %collective-permute-start = (f32[40,128]{1,0:T(8,128)S(1)}, f32[40,128]{1,0:T(8,128)S(1)}, u32[]{:S(2)}, u32[]{:S(2)}) collective-permute-start(f32[40,128]{1,0:T(8,128)S(1)} %reduce_sum.188), channel_id=1, source_target_pairs={{0,1},{1,0},{2,3},{3,2},{4,5},{5,4},{6,7},{7,6},{8,9},{9,8},{10,11... | collective-permute-start | bytes 61448 | tf_op jit(solution)/shard_map/ppermute | solution.py:274
  202.1 30.3 %all-to-all-start.8 = ((bf16[16,8,1536]{2,1,0:T(8,128)(2,1)}), bf16[16,8,1536]{2,1,0:T(8,128)(2,1)S(1)}, u32[]{:S(2)}, u32[]{:S(2)}) async-start(bf16[16,8,1536]{2,1,0:T(8,128)(2,1)} %fusion), calls=%async_computation.8 | async-start | bytes 786432 | tf_op jit(solution)/shard_map/all_to_all | solution.py:20

commit v4 on v3

--- a/solution.py
+++ b/solution.py
@@ -10,6 +10,8 @@
 EPSILON = 1e-05
 PLACES = 6
 RANK = 128
+COUNT_ROWS = 16
+PACKED_ROWS = 80
 CONTRACT_ROWS = (((0,), (0,)), ((), ()))
 HIGHEST = lax.Precision.HIGHEST
 VMEM_LIMIT = 32 * 1024 * 1024
@@ -18,11 +20,6 @@
 
 def exchange(blocks, axis):
     return lax.all_to_all(blocks, axis, split_axis=0, concat_axis=0, tiled=True)
-
-
-def exchanged_gather(block, axis):
-    size = lax.axis_size(axis)
-    return exchange(jnp.broadcast_to(block[None], (size,) + block.shape), axis)
 
 
 def halves(values, count):
@@ -123,23 +120,71 @@
 
 
 def inverse_factor(gram_sum):
+    return call(
+        inverse_factor_kernel,
+        "inverse_factor",
+        jax.ShapeDtypeStruct(gram_sum.shape, jnp.float32),
+        (gram_sum,),
+        scratch=[pltpu.VMEM(gram_sum.shape, jnp.float32)],
+        flops=4 * 10**9,
+        moved=3 * 10**7,
+    )
+
+
+def call(kernel, name, shapes, operands, scratch=(), flops=10**7, moved=4 * 10**6):
     vmem = pl.BlockSpec(memory_space=pltpu.VMEM)
+    smem = pl.BlockSpec(memory_space=pltpu.SMEM)
     return pl.pallas_call(
-        inverse_factor_kernel,
-        out_shape=jax.ShapeDtypeStruct(gram_sum.shape, jnp.float32),
-        in_specs=[vmem],
-        out_specs=vmem,
-        scratch_shapes=[pltpu.VMEM(gram_sum.shape, jnp.float32)],
+        kernel,
+        out_shape=shapes,
+        in_specs=[smem if operand.ndim == 1 else vmem for operand in operands],
+        out_specs=jax.tree.map(lambda _: vmem, shapes),
+        scratch_shapes=scratch,
         compiler_params=pltpu.CompilerParams(vmem_limit_bytes=VMEM_LIMIT),
-        cost_estimate=pl.CostEstimate(
-            flops=4 * 10**9, bytes_accessed=3 * 10**7, transcendentals=0
-        ),
-        name="inverse_factor",
-    )(gram_sum)
-
-
-def standardize_kernel(words_ref, weight_ref, mean_ref, scale_ref, matrix_ref):
+        cost_estimate=pl.CostEstimate(flops=flops, bytes_accessed=moved, transcendentals=0),
+        name=name,
+    )(*operands)
+
+
+def count_kernel(words_ref, spread_ref):
     rows, width = words_ref.shape
+    step = 64
+
+    def chunk(at, totals):
+        words = words_ref[pl.ds(pl.multiple_of(at * step, step), step), :]
+        bits = [
+            jnp.bitwise_and(jnp.right_shift(words, 2 * place + bit), 1)
+            for bit in range(2)
+            for place in range(PLACES)
+        ]
+        return tuple(
+            total + jnp.sum(bit.reshape(step // 8, 8, width), axis=0)
+            for total, bit in zip(totals, bits)
+        )
+
+    zeros = jnp.zeros((8, width), jnp.int32)
+    totals = lax.fori_loop(0, rows // step, chunk, (zeros,) * (2 * PLACES))
+    shape = (COUNT_ROWS, width)
+    sublane = lax.broadcasted_iota(jnp.int32, shape, 0)
+    out = jnp.zeros(shape, jnp.float32)
+    for index, total in enumerate(totals):
+        count = jnp.sum(total.astype(jnp.float32), axis=0, keepdims=True) - rows / 2
+        out = jnp.where(sublane == index, jnp.broadcast_to(count, shape), out)
+    out = out.astype(jnp.bfloat16)
+    for index in range(spread_ref.shape[0]):
+        spread_ref[index] = out
+
+
+def standardize_kernel(counts_ref, words_ref, weight_ref, variant_ref, matrix_ref):
+    rows, width = words_ref.shape
+    rows_all = rows * counts_ref.shape[0]
+    counts = counts_ref[0].astype(jnp.float32)
+    for index in range(1, counts_ref.shape[0]):
+        counts = counts + counts_ref[index].astype(jnp.float32)
+    counts = counts + rows_all / 2
+    ones, twos = counts[:PLACES], counts[PLACES : 2 * PLACES]
+    mean = (ones + 2 * twos) / rows_all
+    scale = lax.rsqrt((ones + 4 * twos) / rows_all - mean * mean + EPSILON) * variant_ref[...]
     step = 64
 
     def chunk(at, carry):
@@ -149,27 +194,48 @@
         for place in range(PLACES):
             across = slice(place * width, (place + 1) * width)
             dosage = jnp.bitwise_and(jnp.right_shift(words, 2 * place), 3).astype(jnp.float32)
-            value = (dosage - mean_ref[:, across]) * scale_ref[:, across] * weight
+            value = (dosage - mean[place : place + 1]) * scale[place : place + 1] * weight
             matrix_ref[span, across] = value.astype(jnp.bfloat16)
         return carry
 
     lax.fori_loop(0, rows // step, chunk, 0)
 
 
-def standardize(words, sample_weight, column_mean, column_scale):
-    rows, width = words.shape
-    vmem = pl.BlockSpec(memory_space=pltpu.VMEM)
-    return pl.pallas_call(
-        standardize_kernel,
-        out_shape=jax.ShapeDtypeStruct((rows, PLACES * width), jnp.bfloat16),
-        in_specs=[vmem] * 4,
-        out_specs=vmem,
-        compiler_params=pltpu.CompilerParams(vmem_limit_bytes=VMEM_LIMIT),
-        cost_estimate=pl.CostEstimate(
-            flops=10**7, bytes_accessed=4 * 10**6, transcendentals=0
-        ),
-        name="standardize",
-    )(words, sample_weight[:, None], column_mean[None, :], column_scale[None, :])
+def sum_spread_kernel(*refs):
+    blocks_ref, spread_ref = refs[0], refs[-1]
+    total = blocks_ref[0].astype(jnp.float32)
+    for index in range(1, blocks_ref.shape[0]):
+        total = total + blocks_ref[index].astype(jnp.float32)
+    total = total.astype(spread_ref.dtype)
+    for index in range(spread_ref.shape[0]):
+        spread_ref[index, : total.shape[0]] = total
+    if len(refs) == 3:
+        tail = refs[1][...]
+        for index in range(spread_ref.shape[0]):
+            spread_ref[index, total.shape[0] :] = tail
+
+
+def sum_spread(blocks, *tail):
+    count, rows, width = blocks.shape
+    rows += sum(part.shape[0] for part in tail)
+    shape = jax.ShapeDtypeStruct((count, rows, width), blocks.dtype)
+    return call(sum_spread_kernel, "sum_spread", shape, (blocks, *tail))
+
+
+def product_kernel(core_ref, gathered_ref, product_ref, spread_ref, packed):
+    count = gathered_ref.shape[0]
+    own = product_ref.shape[0] // count
+    for index in range(count):
+        product_ref[index * own : (index + 1) * own] = gathered_ref[index, :own]
+    product = product_ref[...]
+    gram = lax.dot_general(
+        product, product, CONTRACT_ROWS, precision=HIGHEST, preferred_element_type=jnp.float32
+    )
+    packed[...] = pack(gram)
+    half = packed.shape[0] // 2
+    share = packed[pl.ds(pl.multiple_of(core_ref[0] * half, 8), half), :]
+    for index in range(spread_ref.shape[0]):
+        spread_ref[index] = share
 
 
 def apply_factor(panel, inverse):
@@ -188,53 +254,48 @@
     rows_local, width = dosage_words.shape
     rows_all = rows_local * lax.axis_size("row")
     cols_all = PLACES * width * lax.axis_size("col")
-    dosage = [
-        jnp.bitwise_and(jnp.right_shift(dosage_words, 2 * place), 3).astype(jnp.float32)
-        for place in range(PLACES)
-    ]
-    sums = jnp.concatenate(
-        [jnp.sum(part, axis=0) for part in dosage]
-        + [jnp.sum(part * part, axis=0) for part in dosage]
-    )
-    sums = jnp.sum(exchanged_gather(sums.reshape(-1, 128), "row"), axis=0)
-    totals, squares = sums.reshape(2, PLACES * width)
-    column_mean = totals / rows_all
-    column_scale = lax.rsqrt(squares / rows_all - column_mean * column_mean + EPSILON)
-    matrix = standardize(
-        dosage_words, sample_weight, column_mean, column_scale * variant_weight
-    )
     n_row, n_col = lax.axis_size("row"), lax.axis_size("col")
+    counts = call(
+        count_kernel,
+        "count",
+        jax.ShapeDtypeStruct((n_row, COUNT_ROWS, width), jnp.bfloat16),
+        (dosage_words,),
+    )
+    matrix = call(
+        standardize_kernel,
+        "standardize",
+        jax.ShapeDtypeStruct((rows_local, PLACES * width), jnp.bfloat16),
+        (
+            exchange(counts, "row"),
+            dosage_words,
+            sample_weight[:, None],
+            variant_weight.reshape(PLACES, width),
+        ),
+    )
     col = lax.axis_index("col")
     own, part = rows_local // n_col, RANK // n_col
     chunk = PLACES * width // n_row
 
     sketch_part = jnp.dot(matrix, omega, preferred_element_type=jnp.float32)
-    sketch_own = jnp.sum(exchange(sketch_part.reshape(n_col, own, RANK), "col"), axis=0)
-    sketch = exchanged_gather(sketch_own, "col").reshape(rows_local, RANK)
-
-    gram_share = lax.dynamic_slice_in_dim(local_gram(sketch), col * part, part, 0)
+    arrived = exchange(sketch_part.reshape(n_col, own, RANK), "col")
+    sketch = exchange(sum_spread(arrived), "col").reshape(rows_local, RANK)
+
     sketch_terms = jnp.concatenate(halves(sketch, 2), axis=1)
     back_terms = lax.dot_general(
         matrix, sketch_terms, CONTRACT_ROWS, preferred_element_type=jnp.float32
     )
     back_part = (back_terms[:, :RANK] + back_terms[:, RANK:]).astype(jnp.bfloat16)
+    arrived = exchange(back_part.reshape(n_row, chunk, RANK), "row")
+    gram_share = lax.dynamic_slice_in_dim(local_gram(sketch), col * part, part, 0)
     share_terms = jnp.concatenate(
         halves(gram_share, 3) + [jnp.zeros((part, RANK), jnp.bfloat16)], axis=0
     )
-    arrived = exchange(
-        jnp.concatenate(
-            [
-                back_part.reshape(n_row, chunk, RANK),
-                jnp.broadcast_to(share_terms[None], (n_row,) + share_terms.shape),
-            ],
-            axis=1,
-        ),
-        "row",
-    )
-    arrived = jnp.sum(arrived.astype(jnp.float32), axis=0)
-    back_own = arrived[:chunk].astype(jnp.bfloat16)
-    gram_share = jnp.sum(arrived[chunk:].reshape(4, part, RANK), axis=0)
-    back = exchanged_gather(back_own, "row").reshape(n_row * chunk, RANK)
+    arrived, share_terms = lax.optimization_barrier((arrived, share_terms))
+    gathered = exchange(sum_spread(arrived, share_terms), "row")
+    back = gathered[:, :chunk].reshape(n_row * chunk, RANK)
+    gram_share = jnp.sum(
+        gathered[:, chunk:].astype(jnp.float32).reshape(4 * n_row, part, RANK), axis=0
+    )
 
     product_part = jnp.dot(matrix, back, preferred_element_type=jnp.float32)
     back_gram = lax.dot_general(back, back, CONTRACT_ROWS, preferred_element_type=jnp.float32)
@@ -250,21 +311,23 @@
         ),
         "col",
     )
-    summed = jnp.sum(arrived[:, : own + part], axis=0)
     sketch_factor = inverse_factor(arrived[:, own + part :].reshape(RANK, RANK))
-    gathered = exchanged_gather(
-        jnp.concatenate([summed, jnp.zeros((part, RANK), jnp.float32)], axis=0), "col"
-    )
+    gathered = exchange(sum_spread(arrived), "col")
     gathered, sketch_factor = lax.optimization_barrier((gathered, sketch_factor))
-    product = gathered[:, :own].reshape(rows_local, RANK)
     back_gram = gathered[:, own : own + part].reshape(RANK, RANK)
 
-    packed = pack(local_gram(product))
-    half = packed.shape[0] // 2
     core = lax.rem(col, 2)
-    gathered = exchanged_gather(
-        lax.dynamic_slice_in_dim(packed, core * half, half, 0), "row"
-    )
+    product, spread = call(
+        product_kernel,
+        "product",
+        (
+            jax.ShapeDtypeStruct((rows_local, RANK), jnp.float32),
+            jax.ShapeDtypeStruct((n_row, PACKED_ROWS // 2, RANK), jnp.float32),
+        ),
+        (core.reshape(1), gathered),
+        scratch=[pltpu.VMEM((PACKED_ROWS, RANK), jnp.float32)],
+    )
+    gathered = exchange(spread, "row")
     back_factor = inverse_factor(congruent(back_gram, sketch_factor))
     factor = jnp.dot(back_factor, sketch_factor, precision=HIGHEST)
     right_full = apply_factor(back.astype(jnp.float32), factor)

time: 234 us -> 230 us (0.983)
  blocking collectives: 60.8 us -> 73 us
  waiting for transfers between devices: 84.3 us -> 73.8 us
  starting transfers between devices: 44.6 us -> 37.9 us
  Pallas kernels: 25.2 us -> 28.8 us
    all_to_all x3 -> x4, blocking collectives: 60.8 us -> 73 us  [exchange(): return lax.all_to_all(blocks, axis, split_axis=0, concat_axis=0, tiled=True)]
    all_to_all x6 -> x5, waiting for transfers between devices: 83.1 us -> 72.6 us  [exchange(): return lax.all_to_all(blocks, axis, split_axis=0, concat_axis=0, tiled=True)]
    all_to_all x6 -> x5, starting transfers between devices: 42.7 us -> 36 us  [exchange(): return lax.all_to_all(blocks, axis, split_axis=0, concat_axis=0, tiled=True)]
    broadcast_in_dim x8 -> x1, local copies, waits for them, and re-layouts: 4.57 us -> 0.82 us  [per_device(): sample_weight[:, None]]
    pallas_call x4 -> x9, Pallas kernels: 25.2 us -> 28.8 us  [call(): pl.pallas_call(kernel, out_shape=shapes, in_specs=[smem if operand.ndim =...]
  transfers between devices with their start and end apart: 7 -> 6, of which waited for: 7 -> 6; matrix products, arithmetic and copies ran while one was open for 2% -> 3% of each run, Pallas kernels for 7% -> 7%
where the time goes in v4:
time: 230 us; the launch traced here: 229 us
  waiting for transfers between devices  73.8 us (32%)
  blocking collectives  73 us (32%)
  starting transfers between devices  37.9 us (16%)
  Pallas kernels  28.8 us (13%)
  matrix products  7.79 us (3%)
  local copies, waits for them, and re-layouts  4.36 us (2%)
  other arithmetic  2.39 us (1%)
    all_to_all x4, blocking collectives, exchange(): return lax.all_to_all(blocks, axis, split_axis=0, concat_axis=0, tiled=True)  73 us
    all_to_all x5, waiting for transfers between devices, exchange(): return lax.all_to_all(blocks, axis, split_axis=0, concat_axis=0, tiled=True)  72.6 us
    all_to_all x5, starting transfers between devices, exchange(): return lax.all_to_all(blocks, axis, split_axis=0, concat_axis=0, tiled=True)  36 us
    pallas_call x9, Pallas kernels, call(): pl.pallas_call(kernel, out_shape=shapes, in_specs=[smem if operand.ndim =...  28.8 us
  transfers between devices with their start and end apart: 6, of which 6 were waited for; matrix products, arithmetic and copies ran while one was open for 3% of the time, Pallas kernels for 7%

profile of v4, /device:TPU:2, one launch (start us, length us, event | category | flops | bytes accessed | tf_op | source)
XLA Modules:
  0.0 228.8 jit_solution(5332214844217947217)
XLA Ops:
  0.6 0.0 copy-start
  0.6 0.0 copy-start.1
  0.7 1.1 copy-done.1
  1.7 1.4 count.1
  3.1 15.2 %all-to-all-start = ((bf16[16,16,256]{2,1,0:T(8,128)(2,1)}), bf16[16,16,256]{2,1,0:T(8,128)(2,1)S(1)}, u32[]{:S(2)}, u32[]{:S(2)}) async-start(bf16[16,16,256]{2,1,0:T(8,128)(2,1)} %count.1), calls=%async_computation | async-start | bytes 262144 | tf_op jit(solution)/shard_map/all_to_all | solution.py:22
  18.3 0.8 copy.14.weight_ref
  19.2 0.7 reshape.46.variant_ref
  19.9 13.2 %all-to-all-done.counts_ref = bf16[16,16,256]{2,1,0:T(8,128)(2,1)S(1)} async-done(((bf16[16,16,256]{2,1,0:T(8,128)(2,1)}), bf16[16,16,256]{2,1,0:T(8,128)(2,1)S(1)}, u32[]{:S(2)}, u32[]{:S(2)}) %all-to-all-start) | async-done | bytes 131104 | tf_op jit(solution)/shard_map/all_to_all | solution.py:22
  33.0 0.0 copy-start.2
  33.0 1.0 copy-done.2
  34.1 0.8 standardize.1
  34.9 0.0 copy-done
  34.9 0.6 fusion.15
  35.4 15.1 %all_to_all.45.refs_0_ = f32[32,16,128]{2,1,0:T(8,128)S(1)} all-to-all(f32[32,16,128]{2,1,0:T(8,128)S(1)} %bitcast.53), channel_id=1, replica_groups=mesh['row'=16,'col'=32] {'col'}, dimensions={0} | all-to-all | bytes 524288 | tf_op jit(solution)/shard_map/all_to_all | solution.py:22
  50.5 0.1 sum_spread.3
  50.6 12.5 %all_to_all.46 = f32[32,16,128]{2,1,0:T(8,128)S(1)} all-to-all(f32[32,16,128]{2,1,0:T(8,128)S(1)} %sum_spread.3), channel_id=1, replica_groups=mesh['row'=16,'col'=32] {'col'}, dimensions={0} | all-to-all | bytes 524288 | tf_op jit(solution)/shard_map/all_to_all | solution.py:22
  63.1 0.6 fusion.4
  63.7 0.8 fusion.1
  64.6 3.8 %all-to-all-start.3 = ((bf16[16,96,128]{2,1,0:T(8,128)(2,1)}), bf16[16,96,128]{2,1,0:T(8,128)(2,1)S(1)}, u32[]{:S(2)}, u32[]{:S(2)}) async-start(bf16[16,96,128]{2,1,0:T(8,128)(2,1)} %bitcast.5), calls=%async_computation.3 | async-start | bytes 786432 | tf_op jit(solution)/shard_map/all_to_all | solution.py:22
  68.4 0.1 pad.14.clone
  68.5 0.6 convolution_bitcast_fusion.1
  69.1 0.1 maximum_maximum_fusion.refs_1_
  69.2 24.5 %all-to-all-done.3.refs_0_ = bf16[16,96,128]{2,1,0:T(8,128)(2,1)S(1)} async-done(((bf16[16,96,128]{2,1,0:T(8,128)(2,1)}), bf16[16,96,128]{2,1,0:T(8,128)(2,1)S(1)}, u32[]{:S(2)}, u32[]{:S(2)}) %all-to-all-start.3) | async-done | bytes 393248 | tf_op jit(solution)/shard_map/all_to_all | solution.py:22
  93.7 0.1 sum_spread.4
  93.7 31.8 %all_to_all.47 = bf16[16,112,128]{2,1,0:T(8,128)(2,1)S(1)} all-to-all(bf16[16,112,128]{2,1,0:T(8,128)(2,1)S(1)} %sum_spread.4), channel_id=1, replica_groups=mesh['row'=16,'col'=32] {'row'}, dimensions={0} | all-to-all | bytes 917504 | tf_op jit(solution)/shard_map/all_to_all | solution.py:22
  125.5 0.1 convert_reduce_fusion.1
  125.6 0.3 convolution_bitcast_fusion
  125.9 0.6 fusion.16
  126.6 13.6 %all_to_all.48.refs_0_ = f32[32,24,128]{2,1,0:T(8,128)S(1)} all-to-all(f32[32,24,128]{2,1,0:T(8,128)S(1)} %pad_maximum_fusion), channel_id=1, replica_groups=mesh['row'=16,'col'=32] {'col'}, dimensions={0} | all-to-all | bytes 786432 | tf_op jit(solution)/shard_map/all_to_all | solution.py:22
  140.2 0.8 sum_spread.5
  141.0 5.0 %all-to-all-start.6 = ((f32[32,24,128]{2,1,0:T(8,128)}), f32[32,24,128]{2,1,0:T(8,128)S(1)}, u32[]{:S(2)}, u32[]{:S(2)}) async-start(f32[32,24,128]{2,1,0:T(8,128)} %sum_spread.5), calls=%async_computation.6 | async-start | bytes 786432 | tf_op jit(solution)/shard_map/all_to_all | solution.py:22
  146.0 8.2 %inverse_factor.3 = f32[128,128]{1,0:T(8,128)S(1)} custom-call(f32[128,128]{1,0:T(8,128)S(1)} %bitcast.50), custom_call_target="tpu_custom_call" | custom-call | flops 4000000000 | bytes 30000000 | tf_op jit(solution)/shard_map/inverse_factor/pallas_call | solution.py:137
  154.2 1.0 all-to-all-done.6.gathered_ref
  155.2 1.2 product.1
  156.5 5.9 %all-to-all-start.7 = ((f32[16,40,128]{2,1,0:T(8,128)}), f32[16,40,128]{2,1,0:T(8,128)S(1)}, u32[]{:S(2)}, u32[]{:S(2)}) async-start(f32[16,40,128]{2,1,0:T(8,128)} %get-tuple-element.14), calls=%async_computation.7 | async-start | bytes 655360 | tf_op jit(solution)/shard_map/all_to_all | solution.py:22
  162.4 0.2 fusion.17
  162.6 0.3 fusion.18.gram_ref
  162.9 8.2 %inverse_factor.4 = f32[128,128]{1,0:T(8,128)S(1)} custom-call(f32[128,128]{1,0:T(8,128)S(1)} %fusion.18.gram_ref), custom_call_target="tpu_custom_call" | custom-call | flops 4000000000 | bytes 30000000 | tf_op jit(solution)/shard_map/inverse_factor/pallas_call | solution.py:137
  171.0 0.2 fusion.19
  171.3 1.1 fusion.20
  172.3 11.6 %all-to-all-done.7 = f32[16,40,128]{2,1,0:T(8,128)S(1)} async-done(((f32[16,40,128]{2,1,0:T(8,128)}), f32[16,40,128]{2,1,0:T(8,128)S(1)}, u32[]{:S(2)}, u32[]{:S(2)}) %all-to-all-start.7) | async-done | bytes 327712 | tf_op jit(solution)/shard_map/all_to_all | solution.py:22
  184.0 1.9 collective-permute-start
  185.9 1.1 collective-permute-done
  187.1 0.1 slice.52
  187.1 0.1 fusion.14
  187.2 0.1 pad_dynamic-update-slice_fusion.1
  187.3 0.1 constant_dynamic-update-slice_fusion.1
  187.4 0.1 constant_dynamic-update-slice_fusion
  187.4 0.1 pad_dynamic-update-slice_fusion
  187.5 0.1 copy.15
  187.6 0.2 fusion.9
  187.8 0.3 fusion.21.gram_ref
  188.1 0.0 copy-start.3
  188.1 8.2 %inverse_factor.5 = f32[128,128]{1,0:T(8,128)S(1)} custom-call(f32[128,128]{1,0:T(8,128)S(1)} %fusion.21.gram_ref), custom_call_target="tpu_custom_call" | custom-call | flops 4000000000 | bytes 30000000 | tf_op jit(solution)/shard_map/inverse_factor/pallas_call | solution.py:137
  196.3 0.0 copy-done.3
  196.3 0.4 fusion.22
  196.7 1.2 fusion
  197.8 6.0 %all-to-all-start.8 = ((bf16[16,8,1536]{2,1,0:T(8,128)(2,1)}), bf16[16,8,1536]{2,1,0:T(8,128)(2,1)S(1)}, u32[]{:S(2)}, u32[]{:S(2)}) async-start(bf16[16,8,1536]{2,1,0:T(8,128)(2,1)} %fusion), calls=%async_computation.8 | async-start | bytes 786432 | tf_op jit(solution)/shard_map/all_to_all | solution.py:22
  203.8 1.4 convolution_multiply_fusion
  205.2 0.6 dynamic-slice_multiply_fusion
  205.8 22.3 %all-to-all-done.8 = bf16[16,8,1536]{2,1,0:T(8,128)(2,1)S(1)} async-done(((bf16[16,8,1536]{2,1,0:T(8,128)(2,1)}), bf16[16,8,1536]{2,1,0:T(8,128)(2,1)S(1)}, u32[]{:S(2)}, u32[]{:S(2)}) %all-to-all-start.8) | async-done | bytes 393248 | tf_op jit(solution)/shard_map/all_to_all | solution.py:22
  228.2 0.7 convert_reduce_fusion
  (13 shorter events, 0.2 us)
Async XLA Ops:
  0.6 34.2 %copy-start = (bf16[1536,128]{1,0:T(8,128)(2,1)S(1)}, bf16[1536,128]{1,0:T(8,128)(2,1)}, u32[]{:S(2)}) copy-start(bf16[1536,128]{1,0:T(8,128)(2,1)} %param.7) | copy-start | bytes 1179652
  0.6 1.1 copy-start.1
  3.1 29.9 %all-to-all-start = ((bf16[16,16,256]{2,1,0:T(8,128)(2,1)}), bf16[16,16,256]{2,1,0:T(8,128)(2,1)S(1)}, u32[]{:S(2)}, u32[]{:S(2)}) async-start(bf16[16,16,256]{2,1,0:T(8,128)(2,1)} %count.1), calls=%async_computation | async-start | bytes 262144 | tf_op jit(solution)/shard_map/all_to_all | solution.py:22
  33.0 1.0 copy-start.2
  64.6 29.1 %all-to-all-start.3 = ((bf16[16,96,128]{2,1,0:T(8,128)(2,1)}), bf16[16,96,128]{2,1,0:T(8,128)(2,1)S(1)}, u32[]{:S(2)}, u32[]{:S(2)}) async-start(bf16[16,96,128]{2,1,0:T(8,128)(2,1)} %bitcast.5), calls=%async_computation.3 | async-start | bytes 786432 | tf_op jit(solution)/shard_map/all_to_all | solution.py:22
  141.0 14.2 %all-to-all-start.6 = ((f32[32,24,128]{2,1,0:T(8,128)}), f32[32,24,128]{2,1,0:T(8,128)S(1)}, u32[]{:S(2)}, u32[]{:S(2)}) async-start(f32[32,24,128]{2,1,0:T(8,128)} %sum_spread.5), calls=%async_computation.6 | async-start | bytes 786432 | tf_op jit(solution)/shard_map/all_to_all | solution.py:22
  156.5 27.5 %all-to-all-start.7 = ((f32[16,40,128]{2,1,0:T(8,128)}), f32[16,40,128]{2,1,0:T(8,128)S(1)}, u32[]{:S(2)}, u32[]{:S(2)}) async-start(f32[16,40,128]{2,1,0:T(8,128)} %get-tuple-element.14), calls=%async_computation.7 | async-start | bytes 655360 | tf_op jit(solution)/shard_map/all_to_all | solution.py:22
  184.0 3.1 %collective-permute-start = (f32[40,128]{1,0:T(8,128)S(1)}, f32[40,128]{1,0:T(8,128)S(1)}, u32[]{:S(2)}, u32[]{:S(2)}) collective-permute-start(f32[40,128]{1,0:T(8,128)S(1)} %reduce_sum.28), channel_id=1, source_target_pairs={{0,1},{1,0},{2,3},{3,2},{4,5},{5,4},{6,7},{7,6},{8,9},{9,8},{10,11... | collective-permute-start | bytes 61448 | tf_op jit(solution)/shard_map/ppermute | solution.py:337
  188.1 8.2 %copy-start.3 = (f32[512,128]{1,0:T(8,128)S(1)}, f32[512,128]{1,0:T(8,128)}, u32[]{:S(2)}) copy-start(f32[512,128]{1,0:T(8,128)} %fusion.20) | copy-start | bytes 786436
  197.8 30.3 %all-to-all-start.8 = ((bf16[16,8,1536]{2,1,0:T(8,128)(2,1)}), bf16[16,8,1536]{2,1,0:T(8,128)(2,1)S(1)}, u32[]{:S(2)}, u32[]{:S(2)}) async-start(bf16[16,8,1536]{2,1,0:T(8,128)(2,1)} %fusion), calls=%async_computation.8 | async-start | bytes 786432 | tf_op jit(solution)/shard_map/all_to_all | solution.py:22

commit v5 on v4

--- a/solution.py
+++ b/solution.py
@@ -15,7 +15,8 @@
 CONTRACT_ROWS = (((0,), (0,)), ((), ()))
 HIGHEST = lax.Precision.HIGHEST
 VMEM_LIMIT = 32 * 1024 * 1024
-BLOCK = 8
+BLOCK = 16
+SUBLANES = 8
 
 
 def exchange(blocks, axis):
@@ -64,32 +65,40 @@
 
 def inverse_factor_kernel(gram_ref, inverse_ref, work):
     size = gram_ref.shape[0]
-    shape = (BLOCK, size)
+    whole, tile = (BLOCK, size), (SUBLANES, size)
     work[...] = gram_ref[...]
-    lane = lax.broadcasted_iota(jnp.int32, shape, 1)
-    sublane = lax.broadcasted_iota(jnp.int32, shape, 0)
+    lane = lax.broadcasted_iota(jnp.int32, whole, 1)
+    row_at = lax.broadcasted_iota(jnp.int32, whole, 0)
+    sublane = lax.broadcasted_iota(jnp.int32, tile, 0)
     all_lanes = lax.broadcasted_iota(jnp.int32, (size, size), 1)
 
     def spread(rows):
-        out = rows[0]
-        for index in range(1, BLOCK):
-            out = jnp.where(sublane == index, rows[index], out)
-        return out
+        tiles = []
+        for first in range(0, BLOCK, SUBLANES):
+            out = rows[first]
+            for index in range(1, SUBLANES):
+                out = jnp.where(sublane == index, rows[first + index], out)
+            tiles.append(out)
+        return jnp.concatenate(tiles, axis=0)
 
     def step(at, carry):
         base = pl.multiple_of(at * BLOCK, BLOCK)
         rows = work[pl.ds(base, BLOCK), :]
         turned = pltpu.roll(rows, lax.rem(size - base, size), 1)
-        columns = [jnp.broadcast_to(turned[:, j : j + 1], shape) for j in range(BLOCK)]
+        columns = [jnp.broadcast_to(turned[:, j : j + 1], whole) for j in range(BLOCK)]
         entry = {
-            (i, j): jnp.broadcast_to(columns[i][j : j + 1, :], shape)
+            (i, j): jnp.broadcast_to(columns[i][j : j + 1, :], tile)
             for j in range(BLOCK)
             for i in range(j, BLOCK)
         }
         within = jnp.logical_and(lane >= base, lane < base + BLOCK)
-        start = jnp.where(within, (lane - base == sublane).astype(jnp.float32), rows)
+        start = jnp.where(within, (lane - base == row_at).astype(jnp.float32), rows)
         done, pivots, reciprocals = [], [], []
         for j in range(BLOCK):
+            row = jnp.broadcast_to(start[j : j + 1, :], tile)
+            for k in range(j):
+                row = row - entry[j, k] * done[k]
+            done.append(row)
             pivots.append(entry[j, j])
             reciprocal = 1.0 / entry[j, j]
             reciprocals.append(reciprocal)
@@ -99,11 +108,6 @@
                     entry[i, k] = entry[i, k] - factors[i] * entry[k, j]
             for i in range(j + 1, BLOCK):
                 entry[i, j] = factors[i]
-        for i in range(BLOCK):
-            row = jnp.broadcast_to(start[i : i + 1, :], shape)
-            for j in range(i):
-                row = row - entry[i, j] * done[j]
-            done.append(row)
         block = spread(done)
         inverse_ref[pl.ds(base, BLOCK), :] = jnp.where(
             lane < base + BLOCK, block, 0.0
@@ -146,12 +150,14 @@
     )(*operands)
 
 
-def count_kernel(words_ref, spread_ref):
+def count_kernel(words_ref, spread_ref, kept_ref):
     rows, width = words_ref.shape
     step = 64
 
     def chunk(at, totals):
-        words = words_ref[pl.ds(pl.multiple_of(at * step, step), step), :]
+        span = pl.ds(pl.multiple_of(at * step, step), step)
+        words = words_ref[span, :]
+        kept_ref[span, :] = words
         bits = [
             jnp.bitwise_and(jnp.right_shift(words, 2 * place + bit), 1)
             for bit in range(2)
@@ -255,10 +261,13 @@
     rows_all = rows_local * lax.axis_size("row")
     cols_all = PLACES * width * lax.axis_size("col")
     n_row, n_col = lax.axis_size("row"), lax.axis_size("col")
-    counts = call(
+    counts, words = call(
         count_kernel,
         "count",
-        jax.ShapeDtypeStruct((n_row, COUNT_ROWS, width), jnp.bfloat16),
+        (
+            jax.ShapeDtypeStruct((n_row, COUNT_ROWS, width), jnp.bfloat16),
+            jax.ShapeDtypeStruct((rows_local, width), jnp.int32),
+        ),
         (dosage_words,),
     )
     matrix = call(
@@ -267,7 +276,7 @@
         jax.ShapeDtypeStruct((rows_local, PLACES * width), jnp.bfloat16),
         (
             exchange(counts, "row"),
-            dosage_words,
+            words,
             sample_weight[:, None],
             variant_weight.reshape(PLACES, width),
         ),
@@ -281,20 +290,29 @@
     sketch = exchange(sum_spread(arrived), "col").reshape(rows_local, RANK)
 
     sketch_terms = jnp.concatenate(halves(sketch, 2), axis=1)
-    back_terms = lax.dot_general(
-        matrix, sketch_terms, CONTRACT_ROWS, preferred_element_type=jnp.float32
-    )
-    back_part = (back_terms[:, :RANK] + back_terms[:, RANK:]).astype(jnp.bfloat16)
-    arrived = exchange(back_part.reshape(n_row, chunk, RANK), "row")
+    spans = [slice(0, n_row * chunk // 2), slice(n_row * chunk // 2, n_row * chunk)]
+    arrived = []
+    for span in spans:
+        terms = lax.dot_general(
+            matrix[:, span], sketch_terms, CONTRACT_ROWS, preferred_element_type=jnp.float32
+        )
+        back_part = (terms[:, :RANK] + terms[:, RANK:]).astype(jnp.bfloat16)
+        arrived.append(exchange(back_part.reshape(n_row, chunk // 2, RANK), "row"))
     gram_share = lax.dynamic_slice_in_dim(local_gram(sketch), col * part, part, 0)
     share_terms = jnp.concatenate(
         halves(gram_share, 3) + [jnp.zeros((part, RANK), jnp.bfloat16)], axis=0
     )
-    arrived, share_terms = lax.optimization_barrier((arrived, share_terms))
-    gathered = exchange(sum_spread(arrived, share_terms), "row")
-    back = gathered[:, :chunk].reshape(n_row * chunk, RANK)
+    first_half = exchange(sum_spread(arrived[0]), "row")
+    last_half = exchange(sum_spread(arrived[1], share_terms), "row")
     gram_share = jnp.sum(
-        gathered[:, chunk:].astype(jnp.float32).reshape(4 * n_row, part, RANK), axis=0
+        last_half[:, chunk // 2 :].astype(jnp.float32).reshape(4 * n_row, part, RANK), axis=0
+    )
+    back = jnp.concatenate(
+        [
+            first_half.reshape(n_row * chunk // 2, RANK),
+            last_half[:, : chunk // 2].reshape(n_row * chunk // 2, RANK),
+        ],
+        axis=0,
     )
 
     product_part = jnp.dot(matrix, back, preferred_element_type=jnp.float32)

time: 230 us -> 252 us (1.096)
  waiting for transfers between devices: 73.8 us -> 118 us
  blocking collectives: 73 us -> 41.3 us
  starting transfers between devices: 37.9 us -> 53.8 us
  Pallas kernels: 28.8 us -> 23.8 us
    all_to_all x5 -> x8, waiting for transfers between devices: 72.6 us -> 117 us  [exchange(): return lax.all_to_all(blocks, axis, split_axis=0, concat_axis=0, tiled=True)]
    all_to_all x4 -> x3, blocking collectives: 73 us -> 41.3 us  [exchange(): return lax.all_to_all(blocks, axis, split_axis=0, concat_axis=0, tiled=True)]
    all_to_all x5 -> x8, starting transfers between devices: 36 us -> 51.9 us  [exchange(): return lax.all_to_all(blocks, axis, split_axis=0, concat_axis=0, tiled=True)]
    pallas_call x9 -> x10, Pallas kernels: 28.8 us -> 23.8 us  [call(): pl.pallas_call(kernel, out_shape=shapes, in_specs=[smem if operand.ndim =...]
  transfers between devices with their start and end apart: 6 -> 9, of which waited for: 6 -> 9; matrix products, arithmetic and copies ran while one was open for 3% -> 3% of each run, Pallas kernels for 7% -> 5%
where the time goes in v5:
time: 252 us; the launch traced here: 251 us
  waiting for transfers between devices  118 us (47%)
  starting transfers between devices  53.8 us (21%)
  blocking collectives  41.3 us (16%)
  Pallas kernels  23.8 us (9%)
  matrix products  7.28 us (3%)
  local copies, waits for them, and re-layouts  3.32 us (1%)
  other arithmetic  3 us (1%)
    all_to_all x8, waiting for transfers between devices, exchange(): return lax.all_to_all(blocks, axis, split_axis=0, concat_axis=0, tiled=True)  117 us
    all_to_all x8, starting transfers between devices, exchange(): return lax.all_to_all(blocks, axis, split_axis=0, concat_axis=0, tiled=True)  51.9 us
    all_to_all x3, blocking collectives, exchange(): return lax.all_to_all(blocks, axis, split_axis=0, concat_axis=0, tiled=True)  41.3 us
    pallas_call x10, Pallas kernels, call(): pl.pallas_call(kernel, out_shape=shapes, in_specs=[smem if operand.ndim =...  23.8 us
  transfers between devices with their start and end apart: 9, of which 9 were waited for; matrix products, arithmetic and copies ran while one was open for 3% of the time, Pallas kernels for 5%

profile of v5, /device:TPU:2, one launch (start us, length us, event | category | flops | bytes accessed | tf_op | source)
XLA Modules:
  0.0 251.2 jit_solution(10818213551776861203)
XLA Ops:
  0.6 0.0 copy-start
  0.7 1.1 copy-done.1
  1.7 1.4 count.1
  3.1 15.2 %all-to-all-start = ((bf16[16,16,256]{2,1,0:T(8,128)(2,1)}), bf16[16,16,256]{2,1,0:T(8,128)(2,1)S(1)}, u32[]{:S(2)}, u32[]{:S(2)}) async-start(bf16[16,16,256]{2,1,0:T(8,128)(2,1)} %get-tuple-element.11), calls=%async_computation | async-start | bytes 262144 | tf_op jit(solution)/shard_map/all_to_all | solution.py:23
  18.3 0.7 reshape.53.variant_ref
  19.0 0.8 copy.14.weight_ref
  19.8 13.2 %all-to-all-done.counts_ref = bf16[16,16,256]{2,1,0:T(8,128)(2,1)S(1)} async-done(((bf16[16,16,256]{2,1,0:T(8,128)(2,1)}), bf16[16,16,256]{2,1,0:T(8,128)(2,1)S(1)}, u32[]{:S(2)}, u32[]{:S(2)}) %all-to-all-start) | async-done | bytes 131104 | tf_op jit(solution)/shard_map/all_to_all | solution.py:23
  33.0 0.8 standardize.1
  33.8 0.6 fusion.21
  34.4 15.1 %all_to_all.55.refs_0_ = f32[32,16,128]{2,1,0:T(8,128)S(1)} all-to-all(f32[32,16,128]{2,1,0:T(8,128)S(1)} %bitcast.45), channel_id=1, replica_groups=mesh['row'=16,'col'=32] {'col'}, dimensions={0} | all-to-all | bytes 524288 | tf_op jit(solution)/shard_map/all_to_all | solution.py:23
  49.5 0.1 sum_spread.4
  49.5 12.5 %all_to_all.56 = f32[32,16,128]{2,1,0:T(8,128)S(1)} all-to-all(f32[32,16,128]{2,1,0:T(8,128)S(1)} %sum_spread.4), channel_id=1, replica_groups=mesh['row'=16,'col'=32] {'col'}, dimensions={0} | all-to-all | bytes 524288 | tf_op jit(solution)/shard_map/all_to_all | solution.py:23
  62.0 0.4 fusion.1
  62.4 0.7 fusion.5
  63.2 3.8 %all-to-all-start.5 = ((bf16[16,48,128]{2,1,0:T(8,128)(2,1)}), bf16[16,48,128]{2,1,0:T(8,128)(2,1)S(1)}, u32[]{:S(2)}, u32[]{:S(2)}) async-start(bf16[16,48,128]{2,1,0:T(8,128)(2,1)} %bitcast.6), calls=%async_computation.5 | async-start | bytes 393216 | tf_op jit(solution)/shard_map/all_to_all | solution.py:23
  67.0 0.4 fusion.3
  67.4 0.7 fusion.6
  68.1 14.7 %all-to-all-done.5.refs_0_ = bf16[16,48,128]{2,1,0:T(8,128)(2,1)S(1)} async-done(((bf16[16,48,128]{2,1,0:T(8,128)(2,1)}), bf16[16,48,128]{2,1,0:T(8,128)(2,1)S(1)}, u32[]{:S(2)}, u32[]{:S(2)}) %all-to-all-start.5) | async-done | bytes 196640 | tf_op jit(solution)/shard_map/all_to_all | solution.py:23
  82.9 6.1 %all-to-all-start.3 = ((bf16[16,48,128]{2,1,0:T(8,128)(2,1)}), bf16[16,48,128]{2,1,0:T(8,128)(2,1)S(1)}, u32[]{:S(2)}, u32[]{:S(2)}) async-start(bf16[16,48,128]{2,1,0:T(8,128)(2,1)} %bitcast.4), calls=%async_computation.3 | async-start | bytes 393216 | tf_op jit(solution)/shard_map/all_to_all | solution.py:23
  89.0 0.1 pad.16.clone
  89.1 0.6 convolution_bitcast_fusion
  89.7 0.1 maximum_maximum_fusion.refs_1_
  89.8 0.8 sum_spread.6
  90.5 14.9 %all-to-all-done.3.refs_0_ = bf16[16,48,128]{2,1,0:T(8,128)(2,1)S(1)} async-done(((bf16[16,48,128]{2,1,0:T(8,128)(2,1)}), bf16[16,48,128]{2,1,0:T(8,128)(2,1)S(1)}, u32[]{:S(2)}, u32[]{:S(2)}) %all-to-all-start.3) | async-done | bytes 196640 | tf_op jit(solution)/shard_map/all_to_all | solution.py:23
  105.4 4.9 %all-to-all-start.6 = ((bf16[16,64,128]{2,1,0:T(8,128)(2,1)}), bf16[16,64,128]{2,1,0:T(8,128)(2,1)S(1)}, u32[]{:S(2)}, u32[]{:S(2)}) async-start(bf16[16,64,128]{2,1,0:T(8,128)(2,1)} %sum_spread.6), calls=%async_computation.6 | async-start | bytes 524288 | tf_op jit(solution)/shard_map/all_to_all | solution.py:23
  110.4 0.7 sum_spread.5
  111.1 17.6 %all-to-all-done.6 = bf16[16,64,128]{2,1,0:T(8,128)(2,1)S(1)} async-done(((bf16[16,64,128]{2,1,0:T(8,128)(2,1)}), bf16[16,64,128]{2,1,0:T(8,128)(2,1)S(1)}, u32[]{:S(2)}, u32[]{:S(2)}) %all-to-all-start.6) | async-done | bytes 262176 | tf_op jit(solution)/shard_map/all_to_all | solution.py:23
  128.6 5.9 %all-to-all-start.4 = ((bf16[16,48,128]{2,1,0:T(8,128)(2,1)}), bf16[16,48,128]{2,1,0:T(8,128)(2,1)S(1)}, u32[]{:S(2)}, u32[]{:S(2)}) async-start(bf16[16,48,128]{2,1,0:T(8,128)(2,1)} %sum_spread.5), calls=%async_computation.4 | async-start | bytes 393216 | tf_op jit(solution)/shard_map/all_to_all | solution.py:23
  134.6 16.3 %all-to-all-done.4 = bf16[16,48,128]{2,1,0:T(8,128)(2,1)S(1)} async-done(((bf16[16,48,128]{2,1,0:T(8,128)(2,1)}), bf16[16,48,128]{2,1,0:T(8,128)(2,1)S(1)}, u32[]{:S(2)}, u32[]{:S(2)}) %all-to-all-start.4) | async-done | bytes 196640 | tf_op jit(solution)/shard_map/all_to_all | solution.py:23
  150.9 0.3 fusion.10
  151.2 0.6 fusion.11
  151.8 0.1 convert_reduce_fusion.1
  152.0 13.7 %all_to_all.57.refs_0_ = f32[32,24,128]{2,1,0:T(8,128)S(1)} all-to-all(f32[32,24,128]{2,1,0:T(8,128)S(1)} %pad_maximum_fusion.1), channel_id=1, replica_groups=mesh['row'=16,'col'=32] {'col'}, dimensions={0} | all-to-all | bytes 786432 | tf_op jit(solution)/shard_map/all_to_all | solution.py:23
  165.7 0.8 sum_spread.7
  166.5 5.0 %all-to-all-start.8 = ((f32[32,24,128]{2,1,0:T(8,128)}), f32[32,24,128]{2,1,0:T(8,128)S(1)}, u32[]{:S(2)}, u32[]{:S(2)}) async-start(f32[32,24,128]{2,1,0:T(8,128)} %sum_spread.7), calls=%async_computation.8 | async-start | bytes 786432 | tf_op jit(solution)/shard_map/all_to_all | solution.py:23
  171.5 6.0 %inverse_factor.3 = f32[128,128]{1,0:T(8,128)S(1)} custom-call(f32[128,128]{1,0:T(8,128)S(1)} %bitcast.44), custom_call_target="tpu_custom_call" | custom-call | flops 4000000000 | bytes 30000000 | tf_op jit(solution)/shard_map/inverse_factor/pallas_call | solution.py:141
  177.6 3.1 %all-to-all-done.8.gathered_ref = f32[32,24,128]{2,1,0:T(8,128)S(1)} async-done(((f32[32,24,128]{2,1,0:T(8,128)}), f32[32,24,128]{2,1,0:T(8,128)S(1)}, u32[]{:S(2)}, u32[]{:S(2)}) %all-to-all-start.8) | async-done | bytes 393248 | tf_op jit(solution)/shard_map/all_to_all | solution.py:23
  180.7 1.2 product.1
  182.0 4.9 %all-to-all-start.9 = ((f32[16,40,128]{2,1,0:T(8,128)}), f32[16,40,128]{2,1,0:T(8,128)S(1)}, u32[]{:S(2)}, u32[]{:S(2)}) async-start(f32[16,40,128]{2,1,0:T(8,128)} %get-tuple-element.14), calls=%async_computation.9 | async-start | bytes 655360 | tf_op jit(solution)/shard_map/all_to_all | solution.py:23
  186.9 0.2 fusion.22
  187.1 0.3 fusion.23.gram_ref
  187.4 6.0 %inverse_factor.4 = f32[128,128]{1,0:T(8,128)S(1)} custom-call(f32[128,128]{1,0:T(8,128)S(1)} %fusion.23.gram_ref), custom_call_target="tpu_custom_call" | custom-call | flops 4000000000 | bytes 30000000 | tf_op jit(solution)/shard_map/inverse_factor/pallas_call | solution.py:141
  193.4 0.2 fusion.24
  193.6 0.4 fusion.25
  194.0 14.4 %all-to-all-done.9 = f32[16,40,128]{2,1,0:T(8,128)S(1)} async-done(((f32[16,40,128]{2,1,0:T(8,128)}), f32[16,40,128]{2,1,0:T(8,128)S(1)}, u32[]{:S(2)}, u32[]{:S(2)}) %all-to-all-start.9) | async-done | bytes 327712 | tf_op jit(solution)/shard_map/all_to_all | solution.py:23
  208.5 1.9 collective-permute-start
  210.4 1.1 collective-permute-done
  211.6 0.1 slice.72
  211.6 0.1 fusion.20
  211.7 0.1 pad_dynamic-update-slice_fusion.1
  211.8 0.1 constant_dynamic-update-slice_fusion.1
  211.9 0.1 constant_dynamic-update-slice_fusion
  211.9 0.1 pad_dynamic-update-slice_fusion
  212.0 0.1 copy.15
  212.1 0.2 fusion.12
  212.3 0.3 fusion.26.gram_ref
  212.6 6.0 %inverse_factor.5 = f32[128,128]{1,0:T(8,128)S(1)} custom-call(f32[128,128]{1,0:T(8,128)S(1)} %fusion.26.gram_ref), custom_call_target="tpu_custom_call" | custom-call | flops 4000000000 | bytes 30000000 | tf_op jit(solution)/shard_map/inverse_factor/pallas_call | solution.py:141
  218.7 0.4 fusion.27
  219.1 1.2 fusion
  220.2 6.0 %all-to-all-start.10 = ((bf16[16,8,1536]{2,1,0:T(8,128)(2,1)}), bf16[16,8,1536]{2,1,0:T(8,128)(2,1)S(1)}, u32[]{:S(2)}, u32[]{:S(2)}) async-start(bf16[16,8,1536]{2,1,0:T(8,128)(2,1)} %fusion), calls=%async_computation.10 | async-start | bytes 786432 | tf_op jit(solution)/shard_map/all_to_all | solution.py:23
  226.2 1.4 convolution_multiply_fusion
  227.6 0.6 dynamic-slice_multiply_fusion
  228.2 22.3 %all-to-all-done.10 = bf16[16,8,1536]{2,1,0:T(8,128)(2,1)S(1)} async-done(((bf16[16,8,1536]{2,1,0:T(8,128)(2,1)}), bf16[16,8,1536]{2,1,0:T(8,128)(2,1)S(1)}, u32[]{:S(2)}, u32[]{:S(2)}) %all-to-all-start.10) | async-done | bytes 393248 | tf_op jit(solution)/shard_map/all_to_all | solution.py:23
  250.5 0.7 convert_reduce_fusion
  (19 shorter events, 0.2 us)
Async XLA Ops:
  0.6 33.1 %copy-start = (bf16[1536,128]{1,0:T(8,128)(2,1)S(1)}, bf16[1536,128]{1,0:T(8,128)(2,1)}, u32[]{:S(2)}) copy-start(bf16[1536,128]{1,0:T(8,128)(2,1)} %param.7) | copy-start | bytes 1179652
  0.6 1.1 copy-start.1
  3.1 29.9 %all-to-all-start = ((bf16[16,16,256]{2,1,0:T(8,128)(2,1)}), bf16[16,16,256]{2,1,0:T(8,128)(2,1)S(1)}, u32[]{:S(2)}, u32[]{:S(2)}) async-start(bf16[16,16,256]{2,1,0:T(8,128)(2,1)} %get-tuple-element.11), calls=%async_computation | async-start | bytes 262144 | tf_op jit(solution)/shard_map/all_to_all | solution.py:23
  63.2 19.7 %all-to-all-start.5 = ((bf16[16,48,128]{2,1,0:T(8,128)(2,1)}), bf16[16,48,128]{2,1,0:T(8,128)(2,1)S(1)}, u32[]{:S(2)}, u32[]{:S(2)}) async-start(bf16[16,48,128]{2,1,0:T(8,128)(2,1)} %bitcast.6), calls=%async_computation.5 | async-start | bytes 393216 | tf_op jit(solution)/shard_map/all_to_all | solution.py:23
  82.9 22.6 %all-to-all-start.3 = ((bf16[16,48,128]{2,1,0:T(8,128)(2,1)}), bf16[16,48,128]{2,1,0:T(8,128)(2,1)S(1)}, u32[]{:S(2)}, u32[]{:S(2)}) async-start(bf16[16,48,128]{2,1,0:T(8,128)(2,1)} %bitcast.4), calls=%async_computation.3 | async-start | bytes 393216 | tf_op jit(solution)/shard_map/all_to_all | solution.py:23
  105.4 23.2 %all-to-all-start.6 = ((bf16[16,64,128]{2,1,0:T(8,128)(2,1)}), bf16[16,64,128]{2,1,0:T(8,128)(2,1)S(1)}, u32[]{:S(2)}, u32[]{:S(2)}) async-start(bf16[16,64,128]{2,1,0:T(8,128)(2,1)} %sum_spread.6), calls=%async_computation.6 | async-start | bytes 524288 | tf_op jit(solution)/shard_map/all_to_all | solution.py:23
  128.6 22.3 %all-to-all-start.4 = ((bf16[16,48,128]{2,1,0:T(8,128)(2,1)}), bf16[16,48,128]{2,1,0:T(8,128)(2,1)S(1)}, u32[]{:S(2)}, u32[]{:S(2)}) async-start(bf16[16,48,128]{2,1,0:T(8,128)(2,1)} %sum_spread.5), calls=%async_computation.4 | async-start | bytes 393216 | tf_op jit(solution)/shard_map/all_to_all | solution.py:23
  134.6 17.2 %copy-start.2 = (bf16[16,48,128]{2,1,0:T(8,128)(2,1)}, bf16[16,48,128]{2,1,0:T(8,128)(2,1)S(1)}, u32[]{:S(2)}) copy-start(bf16[16,48,128]{2,1,0:T(8,128)(2,1)S(1)} %slice.68) | copy-start | bytes 589828
  166.5 14.2 %all-to-all-start.8 = ((f32[32,24,128]{2,1,0:T(8,128)}), f32[32,24,128]{2,1,0:T(8,128)S(1)}, u32[]{:S(2)}, u32[]{:S(2)}) async-start(f32[32,24,128]{2,1,0:T(8,128)} %sum_spread.7), calls=%async_computation.8 | async-start | bytes 786432 | tf_op jit(solution)/shard_map/all_to_all | solution.py:23
  182.0 26.5 %all-to-all-start.9 = ((f32[16,40,128]{2,1,0:T(8,128)}), f32[16,40,128]{2,1,0:T(8,128)S(1)}, u32[]{:S(2)}, u32[]{:S(2)}) async-start(f32[16,40,128]{2,1,0:T(8,128)} %get-tuple-element.14), calls=%async_computation.9 | async-start | bytes 655360 | tf_op jit(solution)/shard_map/all_to_all | solution.py:23
  208.5 3.1 %collective-permute-start = (f32[40,128]{1,0:T(8,128)S(1)}, f32[40,128]{1,0:T(8,128)S(1)}, u32[]{:S(2)}, u32[]{:S(2)}) collective-permute-start(f32[40,128]{1,0:T(8,128)S(1)} %reduce_sum.28), channel_id=1, source_target_pairs={{0,1},{1,0},{2,3},{3,2},{4,5},{5,4},{6,7},{7,6},{8,9},{9,8},{10,11... | collective-permute-start | bytes 61448 | tf_op jit(solution)/shard_map/ppermute | solution.py:355
  219.0 7.2 %copy-start.3 = (bf16[16,48,128]{2,1,0:T(8,128)(2,1)S(1)}, bf16[16,48,128]{2,1,0:T(8,128)(2,1)}, u32[]{:S(2)}) copy-start(bf16[16,48,128]{2,1,0:T(8,128)(2,1)} %copy-done.2) | copy-start | bytes 589828
  220.2 30.3 %all-to-all-start.10 = ((bf16[16,8,1536]{2,1,0:T(8,128)(2,1)}), bf16[16,8,1536]{2,1,0:T(8,128)(2,1)S(1)}, u32[]{:S(2)}, u32[]{:S(2)}) async-start(bf16[16,8,1536]{2,1,0:T(8,128)(2,1)} %fusion), calls=%async_computation.10 | async-start | bytes 786432 | tf_op jit(solution)/shard_map/all_to_all | solution.py:23

commit v6 on v5

--- a/solution.py
+++ b/solution.py
@@ -11,7 +11,7 @@
 PLACES = 6
 RANK = 128
 COUNT_ROWS = 16
-PACKED_ROWS = 80
+NEAR = 8
 CONTRACT_ROWS = (((0,), (0,)), ((), ()))
 HIGHEST = lax.Precision.HIGHEST
 VMEM_LIMIT = 32 * 1024 * 1024
@@ -19,8 +19,10 @@
 SUBLANES = 8
 
 
-def exchange(blocks, axis):
-    return lax.all_to_all(blocks, axis, split_axis=0, concat_axis=0, tiled=True)
+def exchange(blocks, axis, groups=None):
+    return lax.all_to_all(
+        blocks, axis, split_axis=0, concat_axis=0, axis_index_groups=groups, tiled=True
+    )
 
 
 def halves(values, count):
@@ -30,37 +32,6 @@
         values = values - term
         terms.append(term.astype(jnp.bfloat16))
     return terms
-
-
-def pack(gram):
-    return jnp.concatenate(
-        [
-            gram[0:32],
-            jnp.concatenate([gram[96:128, 96:128], gram[32:64, 32:128]], axis=1),
-            jnp.concatenate([gram[80:96, 64:128], gram[64:80, 64:128]], axis=1),
-        ],
-        axis=0,
-    )
-
-
-def unpack_upper(packed):
-    zeros = jnp.zeros((32, 128), jnp.float32)
-    return jnp.concatenate(
-        [
-            packed[0:32],
-            jnp.concatenate([zeros[:, :32], packed[32:64, 32:128]], axis=1),
-            jnp.concatenate([zeros[:16, :64], packed[64:80, 64:128]], axis=1),
-            jnp.concatenate([zeros[:16, :64], packed[64:80, 0:64]], axis=1),
-            jnp.concatenate([zeros[:, :96], packed[32:64, 0:32]], axis=1),
-        ],
-        axis=0,
-    )
-
-
-def symmetric(upper):
-    rows = lax.broadcasted_iota(jnp.int32, upper.shape, 0)
-    columns = lax.broadcasted_iota(jnp.int32, upper.shape, 1)
-    return jnp.where(rows <= columns, upper, upper.T)
 
 
 def inverse_factor_kernel(gram_ref, inverse_ref, work):
@@ -221,27 +192,27 @@
             spread_ref[index, total.shape[0] :] = tail
 
 
-def sum_spread(blocks, *tail):
-    count, rows, width = blocks.shape
+def sum_spread(blocks, *tail, count=None):
+    rows, width = blocks.shape[1:]
+    count = count or blocks.shape[0]
     rows += sum(part.shape[0] for part in tail)
     shape = jax.ShapeDtypeStruct((count, rows, width), blocks.dtype)
     return call(sum_spread_kernel, "sum_spread", shape, (blocks, *tail))
 
 
-def product_kernel(core_ref, gathered_ref, product_ref, spread_ref, packed):
+def product_kernel(place_ref, gathered_ref, product_ref, spread_ref, gram):
     count = gathered_ref.shape[0]
     own = product_ref.shape[0] // count
     for index in range(count):
         product_ref[index * own : (index + 1) * own] = gathered_ref[index, :own]
     product = product_ref[...]
-    gram = lax.dot_general(
+    gram[...] = lax.dot_general(
         product, product, CONTRACT_ROWS, precision=HIGHEST, preferred_element_type=jnp.float32
     )
-    packed[...] = pack(gram)
-    half = packed.shape[0] // 2
-    share = packed[pl.ds(pl.multiple_of(core_ref[0] * half, 8), half), :]
+    share = gram.shape[0] // NEAR
+    rows = gram[pl.ds(pl.multiple_of(place_ref[0] * share, share), share), :]
     for index in range(spread_ref.shape[0]):
-        spread_ref[index] = share
+        spread_ref[index] = rows
 
 
 def apply_factor(panel, inverse):
@@ -290,29 +261,20 @@
     sketch = exchange(sum_spread(arrived), "col").reshape(rows_local, RANK)
 
     sketch_terms = jnp.concatenate(halves(sketch, 2), axis=1)
-    spans = [slice(0, n_row * chunk // 2), slice(n_row * chunk // 2, n_row * chunk)]
-    arrived = []
-    for span in spans:
-        terms = lax.dot_general(
-            matrix[:, span], sketch_terms, CONTRACT_ROWS, preferred_element_type=jnp.float32
-        )
-        back_part = (terms[:, :RANK] + terms[:, RANK:]).astype(jnp.bfloat16)
-        arrived.append(exchange(back_part.reshape(n_row, chunk // 2, RANK), "row"))
+    back_terms = lax.dot_general(
+        matrix, sketch_terms, CONTRACT_ROWS, preferred_element_type=jnp.float32
+    )
+    back_part = (back_terms[:, :RANK] + back_terms[:, RANK:]).astype(jnp.bfloat16)
+    arrived = exchange(back_part.reshape(n_row, chunk, RANK), "row")
     gram_share = lax.dynamic_slice_in_dim(local_gram(sketch), col * part, part, 0)
     share_terms = jnp.concatenate(
         halves(gram_share, 3) + [jnp.zeros((part, RANK), jnp.bfloat16)], axis=0
     )
-    first_half = exchange(sum_spread(arrived[0]), "row")
-    last_half = exchange(sum_spread(arrived[1], share_terms), "row")
+    arrived, share_terms = lax.optimization_barrier((arrived, share_terms))
+    gathered = exchange(sum_spread(arrived, share_terms), "row")
+    back = gathered[:, :chunk].reshape(n_row * chunk, RANK)
     gram_share = jnp.sum(
-        last_half[:, chunk // 2 :].astype(jnp.float32).reshape(4 * n_row, part, RANK), axis=0
-    )
-    back = jnp.concatenate(
-        [
-            first_half.reshape(n_row * chunk // 2, RANK),
-            last_half[:, : chunk // 2].reshape(n_row * chunk // 2, RANK),
-        ],
-        axis=0,
+        gathered[:, chunk:].astype(jnp.float32).reshape(4 * n_row, part, RANK), axis=0
     )
 
     product_part = jnp.dot(matrix, back, preferred_element_type=jnp.float32)
@@ -334,16 +296,16 @@
     gathered, sketch_factor = lax.optimization_barrier((gathered, sketch_factor))
     back_gram = gathered[:, own : own + part].reshape(RANK, RANK)
 
-    core = lax.rem(col, 2)
+    place = lax.rem(col, NEAR)
     product, spread = call(
         product_kernel,
         "product",
         (
             jax.ShapeDtypeStruct((rows_local, RANK), jnp.float32),
-            jax.ShapeDtypeStruct((n_row, PACKED_ROWS // 2, RANK), jnp.float32),
+            jax.ShapeDtypeStruct((n_row, RANK // NEAR, RANK), jnp.float32),
         ),
-        (core.reshape(1), gathered),
-        scratch=[pltpu.VMEM((PACKED_ROWS, RANK), jnp.float32)],
+        (place.reshape(1), gathered),
+        scratch=[pltpu.VMEM((RANK, RANK), jnp.float32)],
     )
     gathered = exchange(spread, "row")
     back_factor = inverse_factor(congruent(back_gram, sketch_factor))
@@ -351,14 +313,9 @@
     right_full = apply_factor(back.astype(jnp.float32), factor)
     product = apply_factor(product, factor)
     gathered, product = lax.optimization_barrier((gathered, product))
-    packed = jnp.sum(gathered, axis=0)
-    other = lax.ppermute(packed, "col", [(index, index ^ 1) for index in range(n_col)])
-    packed = jnp.where(
-        core == 0,
-        jnp.concatenate([packed, other], axis=0),
-        jnp.concatenate([other, packed], axis=0),
-    )
-    gram = congruent(symmetric(unpack_upper(packed)), factor)
+    near = [list(range(first, first + NEAR)) for first in range(0, n_col, NEAR)]
+    gram = exchange(sum_spread(gathered, count=NEAR), "col", near).reshape(RANK, RANK)
+    gram = congruent(gram, factor)
     second = apply_factor(product, inverse_factor(gram))
     second_own = lax.dynamic_slice_in_dim(second, col * own, own, 0)
 

time: 252 us -> 222 us (0.88)
  waiting for transfers between devices: 118 us -> 69.6 us
  blocking collectives: 41.3 us -> 81.6 us
  starting transfers between devices: 53.8 us -> 34.3 us
    all_to_all x8 -> x5, waiting for transfers between devices: 117 us -> 69.6 us  [exchange(): lax.all_to_all(blocks, axis, split_axis=0, concat_axis=0, axis_index_grou...]
    all_to_all x3 -> x5, blocking collectives: 41.3 us -> 81.6 us  [exchange(): lax.all_to_all(blocks, axis, split_axis=0, concat_axis=0, axis_index_grou...]
    all_to_all x8 -> x5, starting transfers between devices: 51.9 us -> 34.3 us  [exchange(): lax.all_to_all(blocks, axis, split_axis=0, concat_axis=0, axis_index_grou...]
  transfers between devices with their start and end apart: 9 -> 5, of which waited for: 9 -> 5; matrix products, arithmetic and copies ran while one was open for 3% -> 2% of each run, Pallas kernels for 5% -> 5%
where the time goes in v6:
time: 222 us; the launch traced here: 221 us
  blocking collectives  81.6 us (37%)
  waiting for transfers between devices  69.6 us (31%)
  starting transfers between devices  34.3 us (15%)
  Pallas kernels  22.3 us (10%)
  matrix products  7.06 us (3%)
  local copies, waits for them, and re-layouts  2.77 us (1%)
  other arithmetic  2.36 us (1%)
    all_to_all x5, blocking collectives, exchange(): lax.all_to_all(blocks, axis, split_axis=0, concat_axis=0, axis_index_grou...  81.6 us
    all_to_all x5, waiting for transfers between devices, exchange(): lax.all_to_all(blocks, axis, split_axis=0, concat_axis=0, axis_index_grou...  69.6 us
    all_to_all x5, starting transfers between devices, exchange(): lax.all_to_all(blocks, axis, split_axis=0, concat_axis=0, axis_index_grou...  34.3 us
    pallas_call x10, Pallas kernels, call(): pl.pallas_call(kernel, out_shape=shapes, in_specs=[smem if operand.ndim =...  22.3 us
  transfers between devices with their start and end apart: 5, of which 5 were waited for; matrix products, arithmetic and copies ran while one was open for 2% of the time, Pallas kernels for 5%

profile of v6, /device:TPU:2, one launch (start us, length us, event | category | flops | bytes accessed | tf_op | source)
XLA Modules:
  0.0 220.9 jit_solution(6832685714786264500)
XLA Ops:
  0.6 0.0 copy-start
  0.6 0.0 copy-start.1
  0.7 1.1 copy-done.1
  1.7 1.4 count.1
  3.1 15.2 %all-to-all-start = ((bf16[16,16,256]{2,1,0:T(8,128)(2,1)}), bf16[16,16,256]{2,1,0:T(8,128)(2,1)S(1)}, u32[]{:S(2)}, u32[]{:S(2)}) async-start(bf16[16,16,256]{2,1,0:T(8,128)(2,1)} %get-tuple-element.13), calls=%async_computation | async-start | bytes 262144 | tf_op jit(solution)/shard_map/all_to_all | solution.py:23
  18.3 0.8 copy.9.weight_ref
  19.1 0.7 reshape.49.variant_ref
  19.8 13.2 %all-to-all-done.counts_ref = bf16[16,16,256]{2,1,0:T(8,128)(2,1)S(1)} async-done(((bf16[16,16,256]{2,1,0:T(8,128)(2,1)}), bf16[16,16,256]{2,1,0:T(8,128)(2,1)S(1)}, u32[]{:S(2)}, u32[]{:S(2)}) %all-to-all-start) | async-done | bytes 131104 | tf_op jit(solution)/shard_map/all_to_all | solution.py:23
  33.0 0.8 standardize.1
  33.8 0.0 copy-done
  33.8 0.6 fusion.13
  34.4 15.1 %all_to_all.50.refs_0_ = f32[32,16,128]{2,1,0:T(8,128)S(1)} all-to-all(f32[32,16,128]{2,1,0:T(8,128)S(1)} %bitcast.52), channel_id=1, replica_groups=mesh['row'=16,'col'=32] {'col'}, dimensions={0} | all-to-all | bytes 524288 | tf_op jit(solution)/shard_map/all_to_all | solution.py:23
  49.5 0.1 sum_spread.4
  49.5 12.5 %all_to_all.51 = f32[32,16,128]{2,1,0:T(8,128)S(1)} all-to-all(f32[32,16,128]{2,1,0:T(8,128)S(1)} %sum_spread.4), channel_id=1, replica_groups=mesh['row'=16,'col'=32] {'col'}, dimensions={0} | all-to-all | bytes 524288 | tf_op jit(solution)/shard_map/all_to_all | solution.py:23
  62.0 0.6 fusion.4
  62.6 0.8 fusion.1
  63.5 3.8 %all-to-all-start.3 = ((bf16[16,96,128]{2,1,0:T(8,128)(2,1)}), bf16[16,96,128]{2,1,0:T(8,128)(2,1)S(1)}, u32[]{:S(2)}, u32[]{:S(2)}) async-start(bf16[16,96,128]{2,1,0:T(8,128)(2,1)} %bitcast.5), calls=%async_computation.3 | async-start | bytes 786432 | tf_op jit(solution)/shard_map/all_to_all | solution.py:23
  67.3 0.1 pad.6.clone
  67.4 0.6 convolution_bitcast_fusion.1
  68.0 0.1 maximum_maximum_fusion.refs_1_
  68.1 24.5 %all-to-all-done.3.refs_0_ = bf16[16,96,128]{2,1,0:T(8,128)(2,1)S(1)} async-done(((bf16[16,96,128]{2,1,0:T(8,128)(2,1)}), bf16[16,96,128]{2,1,0:T(8,128)(2,1)S(1)}, u32[]{:S(2)}, u32[]{:S(2)}) %all-to-all-start.3) | async-done | bytes 393248 | tf_op jit(solution)/shard_map/all_to_all | solution.py:23
  92.6 0.1 sum_spread.5
  92.7 31.7 %all_to_all.52 = bf16[16,112,128]{2,1,0:T(8,128)(2,1)S(1)} all-to-all(bf16[16,112,128]{2,1,0:T(8,128)(2,1)S(1)} %sum_spread.5), channel_id=1, replica_groups=mesh['row'=16,'col'=32] {'row'}, dimensions={0} | all-to-all | bytes 917504 | tf_op jit(solution)/shard_map/all_to_all | solution.py:23
  124.4 0.1 convert_reduce_fusion.1
  124.5 0.3 convolution_bitcast_fusion
  124.8 0.6 fusion.14
  125.5 13.6 %all_to_all.53.refs_0_ = f32[32,24,128]{2,1,0:T(8,128)S(1)} all-to-all(f32[32,24,128]{2,1,0:T(8,128)S(1)} %pad_maximum_fusion), channel_id=1, replica_groups=mesh['row'=16,'col'=32] {'col'}, dimensions={0} | all-to-all | bytes 786432 | tf_op jit(solution)/shard_map/all_to_all | solution.py:23
  139.1 0.8 sum_spread.6
  139.9 5.0 %all-to-all-start.6 = ((f32[32,24,128]{2,1,0:T(8,128)}), f32[32,24,128]{2,1,0:T(8,128)S(1)}, u32[]{:S(2)}, u32[]{:S(2)}) async-start(f32[32,24,128]{2,1,0:T(8,128)} %sum_spread.6), calls=%async_computation.6 | async-start | bytes 786432 | tf_op jit(solution)/shard_map/all_to_all | solution.py:23
  144.9 6.0 %inverse_factor.3 = f32[128,128]{1,0:T(8,128)S(1)} custom-call(f32[128,128]{1,0:T(8,128)S(1)} %bitcast.49), custom_call_target="tpu_custom_call" | custom-call | flops 4000000000 | bytes 30000000 | tf_op jit(solution)/shard_map/inverse_factor/pallas_call | solution.py:112
  151.0 3.1 %all-to-all-done.6.gathered_ref = f32[32,24,128]{2,1,0:T(8,128)S(1)} async-done(((f32[32,24,128]{2,1,0:T(8,128)}), f32[32,24,128]{2,1,0:T(8,128)S(1)}, u32[]{:S(2)}, u32[]{:S(2)}) %all-to-all-start.6) | async-done | bytes 393248 | tf_op jit(solution)/shard_map/all_to_all | solution.py:23
  154.1 0.2 fusion.15
  154.3 0.3 fusion.16.gram_ref
  154.6 1.1 product.1
  155.7 5.9 %all-to-all-start.7 = ((f32[16,16,128]{2,1,0:T(8,128)}), f32[16,16,128]{2,1,0:T(8,128)S(1)}, u32[]{:S(2)}, u32[]{:S(2)}) async-start(f32[16,16,128]{2,1,0:T(8,128)} %get-tuple-element.18), calls=%async_computation.7 | async-start | bytes 262144 | tf_op jit(solution)/shard_map/all_to_all | solution.py:23
  161.6 6.0 %inverse_factor.4 = f32[128,128]{1,0:T(8,128)S(1)} custom-call(f32[128,128]{1,0:T(8,128)S(1)} %fusion.16.gram_ref), custom_call_target="tpu_custom_call" | custom-call | flops 4000000000 | bytes 30000000 | tf_op jit(solution)/shard_map/inverse_factor/pallas_call | solution.py:112
  167.7 0.2 fusion.17
  167.9 0.4 fusion.18
  168.3 7.4 %all-to-all-done.7.refs_0_ = f32[16,16,128]{2,1,0:T(8,128)S(1)} async-done(((f32[16,16,128]{2,1,0:T(8,128)}), f32[16,16,128]{2,1,0:T(8,128)S(1)}, u32[]{:S(2)}, u32[]{:S(2)}) %all-to-all-start.7) | async-done | bytes 131104 | tf_op jit(solution)/shard_map/all_to_all | solution.py:23
  175.7 8.7 %all_to_all.54 = f32[8,16,128]{2,1,0:T(8,128)S(1)} all-to-all(f32[8,16,128]{2,1,0:T(8,128)S(1)} %sum_spread.7), channel_id=1, replica_groups={{0,1,2,3,4,5,6,7},{8,9,10,11,12,13,14,15},{16,17,18,19,20,21,22,23},{24..., dimensions={0} | all-to-all | bytes 131072 | tf_op jit(solution)/shard_map/all_to_all | solution.py:23
  184.4 0.2 fusion.19
  184.6 0.3 fusion.20.gram_ref
  184.9 6.0 %inverse_factor.5 = f32[128,128]{1,0:T(8,128)S(1)} custom-call(f32[128,128]{1,0:T(8,128)S(1)} %fusion.20.gram_ref), custom_call_target="tpu_custom_call" | custom-call | flops 4000000000 | bytes 30000000 | tf_op jit(solution)/shard_map/inverse_factor/pallas_call | solution.py:112
  190.9 0.4 fusion.21
  191.3 1.2 fusion
  192.4 4.4 %all-to-all-start.9 = ((bf16[16,8,1536]{2,1,0:T(8,128)(2,1)}), bf16[16,8,1536]{2,1,0:T(8,128)(2,1)S(1)}, u32[]{:S(2)}, u32[]{:S(2)}) async-start(bf16[16,8,1536]{2,1,0:T(8,128)(2,1)} %fusion), calls=%async_computation.9 | async-start | bytes 786432 | tf_op jit(solution)/shard_map/all_to_all | solution.py:23
  196.8 1.4 convolution_multiply_fusion
  198.2 0.6 dynamic-slice_multiply_fusion
  198.8 21.4 %all-to-all-done.9 = bf16[16,8,1536]{2,1,0:T(8,128)(2,1)S(1)} async-done(((bf16[16,8,1536]{2,1,0:T(8,128)(2,1)}), bf16[16,8,1536]{2,1,0:T(8,128)(2,1)S(1)}, u32[]{:S(2)}, u32[]{:S(2)}) %all-to-all-start.9) | async-done | bytes 393248 | tf_op jit(solution)/shard_map/all_to_all | solution.py:23
  220.2 0.7 convert_reduce_fusion
  (10 shorter events, 0.2 us)
Async XLA Ops:
  0.6 33.1 %copy-start = (bf16[1536,128]{1,0:T(8,128)(2,1)S(1)}, bf16[1536,128]{1,0:T(8,128)(2,1)}, u32[]{:S(2)}) copy-start(bf16[1536,128]{1,0:T(8,128)(2,1)} %param.7) | copy-start | bytes 1179652
  0.6 1.1 copy-start.1
  3.1 29.9 %all-to-all-start = ((bf16[16,16,256]{2,1,0:T(8,128)(2,1)}), bf16[16,16,256]{2,1,0:T(8,128)(2,1)S(1)}, u32[]{:S(2)}, u32[]{:S(2)}) async-start(bf16[16,16,256]{2,1,0:T(8,128)(2,1)} %get-tuple-element.13), calls=%async_computation | async-start | bytes 262144 | tf_op jit(solution)/shard_map/all_to_all | solution.py:23
  63.5 29.1 %all-to-all-start.3 = ((bf16[16,96,128]{2,1,0:T(8,128)(2,1)}), bf16[16,96,128]{2,1,0:T(8,128)(2,1)S(1)}, u32[]{:S(2)}, u32[]{:S(2)}) async-start(bf16[16,96,128]{2,1,0:T(8,128)(2,1)} %bitcast.5), calls=%async_computation.3 | async-start | bytes 786432 | tf_op jit(solution)/shard_map/all_to_all | solution.py:23
  139.9 14.2 %all-to-all-start.6 = ((f32[32,24,128]{2,1,0:T(8,128)}), f32[32,24,128]{2,1,0:T(8,128)S(1)}, u32[]{:S(2)}, u32[]{:S(2)}) async-start(f32[32,24,128]{2,1,0:T(8,128)} %sum_spread.6), calls=%async_computation.6 | async-start | bytes 786432 | tf_op jit(solution)/shard_map/all_to_all | solution.py:23
  155.7 20.0 %all-to-all-start.7 = ((f32[16,16,128]{2,1,0:T(8,128)}), f32[16,16,128]{2,1,0:T(8,128)S(1)}, u32[]{:S(2)}, u32[]{:S(2)}) async-start(f32[16,16,128]{2,1,0:T(8,128)} %get-tuple-element.18), calls=%async_computation.7 | async-start | bytes 262144 | tf_op jit(solution)/shard_map/all_to_all | solution.py:23
  192.4 27.8 %all-to-all-start.9 = ((bf16[16,8,1536]{2,1,0:T(8,128)(2,1)}), bf16[16,8,1536]{2,1,0:T(8,128)(2,1)S(1)}, u32[]{:S(2)}, u32[]{:S(2)}) async-start(bf16[16,8,1536]{2,1,0:T(8,128)(2,1)} %fusion), calls=%async_computation.9 | async-start | bytes 786432 | tf_op jit(solution)/shard_map/all_to_all | solution.py:23

commit v7 on v6

--- a/solution.py
+++ b/solution.py
@@ -17,6 +17,7 @@
 VMEM_LIMIT = 32 * 1024 * 1024
 BLOCK = 16
 SUBLANES = 8
+WORD_PIECES = 4
 
 
 def exchange(blocks, axis, groups=None):
@@ -34,10 +35,18 @@
     return terms
 
 
-def inverse_factor_kernel(gram_ref, inverse_ref, work):
+def inverted(values):
+    guess = pl.reciprocal(values, approx=True)
+    for _ in range(2):
+        guess = guess * (2.0 - values * guess)
+    return guess
+
+
+def inverse_factor_kernel(*refs):
+    gram_ref, inverse_ref, work = refs[0], refs[-2], refs[-1]
     size = gram_ref.shape[0]
     whole, tile = (BLOCK, size), (SUBLANES, size)
-    work[...] = gram_ref[...]
+    work[...] = congruent(gram_ref[...], refs[1][...]) if len(refs) == 4 else gram_ref[...]
     lane = lax.broadcasted_iota(jnp.int32, whole, 1)
     row_at = lax.broadcasted_iota(jnp.int32, whole, 0)
     sublane = lax.broadcasted_iota(jnp.int32, tile, 0)
@@ -71,12 +80,16 @@
                 row = row - entry[j, k] * done[k]
             done.append(row)
             pivots.append(entry[j, j])
-            reciprocal = 1.0 / entry[j, j]
+            reciprocal = inverted(entry[j, j])
             reciprocals.append(reciprocal)
             factors = {i: entry[i, j] * reciprocal for i in range(j + 1, BLOCK)}
             for i in range(j + 1, BLOCK):
                 for k in range(j + 1, i + 1):
-                    entry[i, k] = entry[i, k] - factors[i] * entry[k, j]
+                    if k == j + 1:
+                        change = (entry[i, j] * entry[k, j]) * reciprocal
+                    else:
+                        change = factors[i] * entry[k, j]
+                    entry[i, k] = entry[i, k] - change
             for i in range(j + 1, BLOCK):
                 entry[i, j] = factors[i]
         block = spread(done)
@@ -94,25 +107,27 @@
     lax.fori_loop(0, size // BLOCK, step, 0)
 
 
-def inverse_factor(gram_sum):
+def inverse_factor(gram_sum, *factor):
     return call(
         inverse_factor_kernel,
         "inverse_factor",
         jax.ShapeDtypeStruct(gram_sum.shape, jnp.float32),
-        (gram_sum,),
+        (gram_sum, *factor),
         scratch=[pltpu.VMEM(gram_sum.shape, jnp.float32)],
         flops=4 * 10**9,
         moved=3 * 10**7,
     )
 
 
-def call(kernel, name, shapes, operands, scratch=(), flops=10**7, moved=4 * 10**6):
+def call(
+    kernel, name, shapes, operands, scratch=(), specs=None, flops=10**7, moved=4 * 10**6
+):
     vmem = pl.BlockSpec(memory_space=pltpu.VMEM)
     smem = pl.BlockSpec(memory_space=pltpu.SMEM)
     return pl.pallas_call(
         kernel,
         out_shape=shapes,
-        in_specs=[smem if operand.ndim == 1 else vmem for operand in operands],
+        in_specs=specs or [smem if operand.ndim == 1 else vmem for operand in operands],
         out_specs=jax.tree.map(lambda _: vmem, shapes),
         scratch_shapes=scratch,
         compiler_params=pltpu.CompilerParams(vmem_limit_bytes=VMEM_LIMIT),
@@ -121,14 +136,20 @@
     )(*operands)
 
 
-def count_kernel(words_ref, spread_ref, kept_ref):
+def count_kernel(words_ref, spread_ref, kept_ref, arrived):
     rows, width = words_ref.shape
     step = 64
+    pieces = arrived.shape[0]
+    copies = []
+    for index in range(pieces):
+        span = pl.ds(index * (rows // pieces), rows // pieces)
+        copies.append(
+            pltpu.make_async_copy(words_ref.at[span, :], kept_ref.at[span, :], arrived.at[index])
+        )
+        copies[-1].start()
 
     def chunk(at, totals):
-        span = pl.ds(pl.multiple_of(at * step, step), step)
-        words = words_ref[span, :]
-        kept_ref[span, :] = words
+        words = kept_ref[pl.ds(pl.multiple_of(at * step, step), step), :]
         bits = [
             jnp.bitwise_and(jnp.right_shift(words, 2 * place + bit), 1)
             for bit in range(2)
@@ -140,7 +161,11 @@
         )
 
     zeros = jnp.zeros((8, width), jnp.int32)
-    totals = lax.fori_loop(0, rows // step, chunk, (zeros,) * (2 * PLACES))
+    totals = (zeros,) * (2 * PLACES)
+    steps = rows // step // pieces
+    for index, copy in enumerate(copies):
+        copy.wait()
+        totals = lax.fori_loop(index * steps, (index + 1) * steps, chunk, totals)
     shape = (COUNT_ROWS, width)
     sublane = lax.broadcasted_iota(jnp.int32, shape, 0)
     out = jnp.zeros(shape, jnp.float32)
@@ -178,26 +203,18 @@
     lax.fori_loop(0, rows // step, chunk, 0)
 
 
-def sum_spread_kernel(*refs):
-    blocks_ref, spread_ref = refs[0], refs[-1]
-    total = blocks_ref[0].astype(jnp.float32)
+def sum_spread_kernel(blocks_ref, spread_ref):
+    total = blocks_ref[0]
     for index in range(1, blocks_ref.shape[0]):
-        total = total + blocks_ref[index].astype(jnp.float32)
-    total = total.astype(spread_ref.dtype)
+        total = total + blocks_ref[index]
     for index in range(spread_ref.shape[0]):
-        spread_ref[index, : total.shape[0]] = total
-    if len(refs) == 3:
-        tail = refs[1][...]
-        for index in range(spread_ref.shape[0]):
-            spread_ref[index, total.shape[0] :] = tail
-
-
-def sum_spread(blocks, *tail, count=None):
+        spread_ref[index] = total
+
+
+def sum_spread(blocks, count=None):
     rows, width = blocks.shape[1:]
-    count = count or blocks.shape[0]
-    rows += sum(part.shape[0] for part in tail)
-    shape = jax.ShapeDtypeStruct((count, rows, width), blocks.dtype)
-    return call(sum_spread_kernel, "sum_spread", shape, (blocks, *tail))
+    shape = jax.ShapeDtypeStruct((count or blocks.shape[0], rows, width), jnp.float32)
+    return call(sum_spread_kernel, "sum_spread", shape, (blocks,))
 
 
 def product_kernel(place_ref, gathered_ref, product_ref, spread_ref, gram):
@@ -216,11 +233,16 @@
 
 
 def apply_factor(panel, inverse):
-    return lax.dot_general(panel, inverse, (((1,), (1,)), ((), ())), precision=HIGHEST)
+    return lax.dot_general(
+        panel, inverse, (((1,), (1,)), ((), ())), precision=HIGHEST, preferred_element_type=jnp.float32
+    )
 
 
 def congruent(gram, factor):
-    return apply_factor(jnp.dot(factor, gram, precision=HIGHEST), factor)
+    half = lax.dot_general(
+        factor, gram, (((1,), (0,)), ((), ())), precision=HIGHEST, preferred_element_type=jnp.float32
+    )
+    return apply_factor(half, factor)
 
 
 def local_gram(panel):
@@ -240,6 +262,8 @@
             jax.ShapeDtypeStruct((rows_local, width), jnp.int32),
         ),
         (dosage_words,),
+        scratch=[pltpu.SemaphoreType.DMA((WORD_PIECES,))],
+        specs=[pl.BlockSpec(memory_space=pltpu.HBM)],
     )
     matrix = call(
         standardize_kernel,
@@ -260,18 +284,19 @@
     arrived = exchange(sketch_part.reshape(n_col, own, RANK), "col")
     sketch = exchange(sum_spread(arrived), "col").reshape(rows_local, RANK)
 
-    sketch_terms = jnp.concatenate(halves(sketch, 2), axis=1)
-    back_terms = lax.dot_general(
-        matrix, sketch_terms, CONTRACT_ROWS, preferred_element_type=jnp.float32
-    )
-    back_part = (back_terms[:, :RANK] + back_terms[:, RANK:]).astype(jnp.bfloat16)
+    back_part = lax.dot_general(
+        matrix, sketch.astype(jnp.bfloat16), CONTRACT_ROWS, preferred_element_type=jnp.float32
+    ).astype(jnp.bfloat16)
     arrived = exchange(back_part.reshape(n_row, chunk, RANK), "row")
     gram_share = lax.dynamic_slice_in_dim(local_gram(sketch), col * part, part, 0)
     share_terms = jnp.concatenate(
         halves(gram_share, 3) + [jnp.zeros((part, RANK), jnp.bfloat16)], axis=0
     )
     arrived, share_terms = lax.optimization_barrier((arrived, share_terms))
-    gathered = exchange(sum_spread(arrived, share_terms), "row")
+    back_own = jnp.sum(arrived.astype(jnp.float32), axis=0).astype(jnp.bfloat16)
+    back_own = jnp.concatenate([back_own, share_terms], axis=0)
+    gathered = lax.all_gather(back_own, "row", axis=0, tiled=True)
+    gathered = gathered.reshape(n_row, chunk + 4 * part, RANK)
     back = gathered[:, :chunk].reshape(n_row * chunk, RANK)
     gram_share = jnp.sum(
         gathered[:, chunk:].astype(jnp.float32).reshape(4 * n_row, part, RANK), axis=0
@@ -308,15 +333,14 @@
         scratch=[pltpu.VMEM((RANK, RANK), jnp.float32)],
     )
     gathered = exchange(spread, "row")
-    back_factor = inverse_factor(congruent(back_gram, sketch_factor))
+    back_factor = inverse_factor(back_gram, sketch_factor)
     factor = jnp.dot(back_factor, sketch_factor, precision=HIGHEST)
     right_full = apply_factor(back.astype(jnp.float32), factor)
     product = apply_factor(product, factor)
     gathered, product = lax.optimization_barrier((gathered, product))
     near = [list(range(first, first + NEAR)) for first in range(0, n_col, NEAR)]
     gram = exchange(sum_spread(gathered, count=NEAR), "col", near).reshape(RANK, RANK)
-    gram = congruent(gram, factor)
-    second = apply_factor(product, inverse_factor(gram))
+    second = apply_factor(product, inverse_factor(gram, factor))
     second_own = lax.dynamic_slice_in_dim(second, col * own, own, 0)
 
     projection_part = lax.dot_general(

time: 222 us -> 221 us (level)
  the two profiles are of different devices: /device:TPU:2 before, /device:TPU:64 now
where the time goes in v7:
time: 221 us; the launch traced here: 220 us
  blocking collectives  83.1 us (38%)
  waiting for transfers between devices  64.4 us (29%)
  starting transfers between devices  36 us (16%)
  Pallas kernels  24.9 us (11%)
  matrix products  6.89 us (3%)
  local copies, waits for them, and re-layouts  2.76 us (1%)
    all_to_all x5, waiting for transfers between devices, exchange(): lax.all_to_all(blocks, axis, split_axis=0, concat_axis=0, axis_index_grou...  64.4 us
    all_to_all x4, blocking collectives, exchange(): lax.all_to_all(blocks, axis, split_axis=0, concat_axis=0, axis_index_grou...  50.4 us
    all_to_all x5, starting transfers between devices, exchange(): lax.all_to_all(blocks, axis, split_axis=0, concat_axis=0, axis_index_grou...  36 us
    all_gather x1, blocking collectives, per_device(): gathered = lax.all_gather(back_own, 'row', axis=0, tiled=True)  32.7 us
    pallas_call x9, Pallas kernels, call(): pl.pallas_call(kernel, out_shape=shapes, in_specs=specs or [smem if opera...  24.9 us
  transfers between devices with their start and end apart: 5, of which 5 were waited for; matrix products, arithmetic and copies ran while one was open for 2% of the time, Pallas kernels for 6%

profile of v7, /device:TPU:64, one launch (start us, length us, event | category | flops | bytes accessed | tf_op | source)
XLA Modules:
  0.0 220.4 jit_solution(1819811445830240247)
XLA Ops:
  0.6 0.0 copy-start
  0.6 0.0 copy-start.1
  0.7 1.1 copy-done.1
  1.7 2.1 count.1
  3.8 14.8 %all-to-all-start = ((bf16[16,16,256]{2,1,0:T(8,128)(2,1)}), bf16[16,16,256]{2,1,0:T(8,128)(2,1)S(1)}, u32[]{:S(2)}, u32[]{:S(2)}) async-start(bf16[16,16,256]{2,1,0:T(8,128)(2,1)} %get-tuple-element.13), calls=%async_computation | async-start | bytes 262144 | tf_op jit(solution)/shard_map/all_to_all | solution.py:24
  18.6 0.7 reshape.51.variant_ref
  19.3 0.8 copy.9.weight_ref
  20.1 11.9 %all-to-all-done.counts_ref = bf16[16,16,256]{2,1,0:T(8,128)(2,1)S(1)} async-done(((bf16[16,16,256]{2,1,0:T(8,128)(2,1)}), bf16[16,16,256]{2,1,0:T(8,128)(2,1)S(1)}, u32[]{:S(2)}, u32[]{:S(2)}) %all-to-all-start) | async-done | bytes 131104 | tf_op jit(solution)/shard_map/all_to_all | solution.py:24
  32.1 0.8 standardize.1
  32.8 0.0 copy-done
  32.9 0.6 fusion.5
  33.4 16.0 %all_to_all.45.blocks_ref = f32[32,16,128]{2,1,0:T(8,128)S(1)} all-to-all(f32[32,16,128]{2,1,0:T(8,128)S(1)} %bitcast.49), channel_id=1, replica_groups=mesh['row'=16,'col'=32] {'col'}, dimensions={0} | all-to-all | bytes 524288 | tf_op jit(solution)/shard_map/all_to_all | solution.py:24
  49.4 0.1 sum_spread.3
  49.5 12.5 %all_to_all.46 = f32[32,16,128]{2,1,0:T(8,128)S(1)} all-to-all(f32[32,16,128]{2,1,0:T(8,128)S(1)} %sum_spread.3), channel_id=1, replica_groups=mesh['row'=16,'col'=32] {'col'}, dimensions={0} | all-to-all | bytes 524288 | tf_op jit(solution)/shard_map/all_to_all | solution.py:24
  62.0 1.4 convolution_convert_fusion.1
  63.4 5.1 %all-to-all-start.3 = ((bf16[16,96,128]{2,1,0:T(8,128)(2,1)}), bf16[16,96,128]{2,1,0:T(8,128)(2,1)S(1)}, u32[]{:S(2)}, u32[]{:S(2)}) async-start(bf16[16,96,128]{2,1,0:T(8,128)(2,1)} %bitcast.5), calls=%async_computation.3 | async-start | bytes 786432 | tf_op jit(solution)/shard_map/all_to_all | solution.py:24
  68.4 0.1 pad.8.clone
  68.5 0.6 convolution_bitcast_fusion.1
  69.1 0.1 maximum_maximum_fusion
  69.2 20.8 %all-to-all-done.3 = bf16[16,96,128]{2,1,0:T(8,128)(2,1)S(1)} async-done(((bf16[16,96,128]{2,1,0:T(8,128)(2,1)}), bf16[16,96,128]{2,1,0:T(8,128)(2,1)S(1)}, u32[]{:S(2)}, u32[]{:S(2)}) %all-to-all-start.3) | async-done | bytes 393248 | tf_op jit(solution)/shard_map/all_to_all | solution.py:24
  90.0 0.1 reduce_sum.30
  90.0 32.7 %all_gather.3 = bf16[1792,128]{1,0:T(8,128)(2,1)S(1)} all-gather(bf16[112,128]{1,0:T(8,128)(2,1)S(1)} %pad_maximum_fusion.1), channel_id=1, replica_groups=mesh['row'=16,'col'=32] {'row'}, dimensions={0}, use_global_device_ids=true | all-gather | bytes 487424 | tf_op jit(solution)/shard_map/all_gather | solution.py:298
  122.8 0.3 convolution_bitcast_fusion
  123.1 0.1 convert_reduce_fusion.1
  123.2 0.6 fusion.6
  123.8 13.9 %all_to_all.47.blocks_ref = f32[32,24,128]{2,1,0:T(8,128)S(1)} all-to-all(f32[32,24,128]{2,1,0:T(8,128)S(1)} %pad_maximum_fusion), channel_id=1, replica_groups=mesh['row'=16,'col'=32] {'col'}, dimensions={0} | all-to-all | bytes 786432 | tf_op jit(solution)/shard_map/all_to_all | solution.py:24
  137.8 0.8 sum_spread.4
  138.6 3.9 %all-to-all-start.5 = ((f32[32,24,128]{2,1,0:T(8,128)}), f32[32,24,128]{2,1,0:T(8,128)S(1)}, u32[]{:S(2)}, u32[]{:S(2)}) async-start(f32[32,24,128]{2,1,0:T(8,128)} %sum_spread.4), calls=%async_computation.5 | async-start | bytes 786432 | tf_op jit(solution)/shard_map/all_to_all | solution.py:24
  142.5 6.4 %inverse_factor.3.refs_1_ = f32[128,128]{1,0:T(8,128)S(1)} custom-call(f32[128,128]{1,0:T(8,128)S(1)} %bitcast.42), custom_call_target="tpu_custom_call" | custom-call | flops 4000000000 | bytes 30000000 | tf_op jit(solution)/shard_map/inverse_factor/pallas_call | solution.py:127
  148.9 3.9 %all-to-all-done.5.gathered_ref = f32[32,24,128]{2,1,0:T(8,128)S(1)} async-done(((f32[32,24,128]{2,1,0:T(8,128)}), f32[32,24,128]{2,1,0:T(8,128)S(1)}, u32[]{:S(2)}, u32[]{:S(2)}) %all-to-all-start.5) | async-done | bytes 393248 | tf_op jit(solution)/shard_map/all_to_all | solution.py:24
  152.8 1.1 product.1
  153.9 6.9 %all-to-all-start.6 = ((f32[16,16,128]{2,1,0:T(8,128)}), f32[16,16,128]{2,1,0:T(8,128)S(1)}, u32[]{:S(2)}, u32[]{:S(2)}) async-start(f32[16,16,128]{2,1,0:T(8,128)} %get-tuple-element.18), calls=%async_computation.6 | async-start | bytes 262144 | tf_op jit(solution)/shard_map/all_to_all | solution.py:24
  160.8 6.9 %inverse_factor.4 = f32[128,128]{1,0:T(8,128)S(1)} custom-call(f32[128,128]{1,0:T(8,128)S(1)} %bitcast.41, f32[128,128]{1,0:T(8,128)S(1)} %inverse_factor.3.refs_1_), custom_call_target="tpu_custom_call" | custom-call | flops 4000000000 | bytes 30000000 | tf_op jit(solution)/shard_map/inverse_factor/pallas_call | solution.py:127
  167.6 0.2 fusion.7.refs_1_
  167.8 0.4 fusion.8
  168.2 6.7 %all-to-all-done.6.blocks_ref = f32[16,16,128]{2,1,0:T(8,128)S(1)} async-done(((f32[16,16,128]{2,1,0:T(8,128)}), f32[16,16,128]{2,1,0:T(8,128)S(1)}, u32[]{:S(2)}, u32[]{:S(2)}) %all-to-all-start.6) | async-done | bytes 131104 | tf_op jit(solution)/shard_map/all_to_all | solution.py:24
  175.0 8.0 %all_to_all.48 = f32[8,16,128]{2,1,0:T(8,128)S(1)} all-to-all(f32[8,16,128]{2,1,0:T(8,128)S(1)} %sum_spread.5), channel_id=1, replica_groups={{0,1,2,3,4,5,6,7},{8,9,10,11,12,13,14,15},{16,17,18,19,20,21,22,23},{24..., dimensions={0} | all-to-all | bytes 131072 | tf_op jit(solution)/shard_map/all_to_all | solution.py:24
  183.0 6.9 %inverse_factor.5 = f32[128,128]{1,0:T(8,128)S(1)} custom-call(f32[128,128]{1,0:T(8,128)S(1)} %bitcast.43, f32[128,128]{1,0:T(8,128)S(1)} %fusion.7.refs_1_), custom_call_target="tpu_custom_call" | custom-call | flops 4000000000 | bytes 30000000 | tf_op jit(solution)/shard_map/inverse_factor/pallas_call | solution.py:127
  189.8 0.4 fusion.9
  190.2 1.2 fusion
  191.4 5.3 %all-to-all-start.8 = ((bf16[16,8,1536]{2,1,0:T(8,128)(2,1)}), bf16[16,8,1536]{2,1,0:T(8,128)(2,1)S(1)}, u32[]{:S(2)}, u32[]{:S(2)}) async-start(bf16[16,8,1536]{2,1,0:T(8,128)(2,1)} %fusion), calls=%async_computation.8 | async-start | bytes 786432 | tf_op jit(solution)/shard_map/all_to_all | solution.py:24
  196.7 1.4 convolution_multiply_fusion
  198.1 0.6 dynamic-slice_multiply_fusion
  198.7 21.0 %all-to-all-done.8 = bf16[16,8,1536]{2,1,0:T(8,128)(2,1)S(1)} async-done(((bf16[16,8,1536]{2,1,0:T(8,128)(2,1)}), bf16[16,8,1536]{2,1,0:T(8,128)(2,1)S(1)}, u32[]{:S(2)}, u32[]{:S(2)}) %all-to-all-start.8) | async-done | bytes 393248 | tf_op jit(solution)/shard_map/all_to_all | solution.py:24
  219.7 0.7 convert_reduce_fusion
  (11 shorter events, 0.2 us)
Async XLA Ops:
  0.6 32.2 %copy-start = (bf16[1536,128]{1,0:T(8,128)(2,1)S(1)}, bf16[1536,128]{1,0:T(8,128)(2,1)}, u32[]{:S(2)}) copy-start(bf16[1536,128]{1,0:T(8,128)(2,1)} %param.7) | copy-start | bytes 1179652
  0.6 1.1 copy-start.1
  3.8 28.2 %all-to-all-start = ((bf16[16,16,256]{2,1,0:T(8,128)(2,1)}), bf16[16,16,256]{2,1,0:T(8,128)(2,1)S(1)}, u32[]{:S(2)}, u32[]{:S(2)}) async-start(bf16[16,16,256]{2,1,0:T(8,128)(2,1)} %get-tuple-element.13), calls=%async_computation | async-start | bytes 262144 | tf_op jit(solution)/shard_map/all_to_all | solution.py:24
  63.4 26.6 %all-to-all-start.3 = ((bf16[16,96,128]{2,1,0:T(8,128)(2,1)}), bf16[16,96,128]{2,1,0:T(8,128)(2,1)S(1)}, u32[]{:S(2)}, u32[]{:S(2)}) async-start(bf16[16,96,128]{2,1,0:T(8,128)(2,1)} %bitcast.5), calls=%async_computation.3 | async-start | bytes 786432 | tf_op jit(solution)/shard_map/all_to_all | solution.py:24
  138.6 14.2 %all-to-all-start.5 = ((f32[32,24,128]{2,1,0:T(8,128)}), f32[32,24,128]{2,1,0:T(8,128)S(1)}, u32[]{:S(2)}, u32[]{:S(2)}) async-start(f32[32,24,128]{2,1,0:T(8,128)} %sum_spread.4), calls=%async_computation.5 | async-start | bytes 786432 | tf_op jit(solution)/shard_map/all_to_all | solution.py:24
  153.9 21.1 %all-to-all-start.6 = ((f32[16,16,128]{2,1,0:T(8,128)}), f32[16,16,128]{2,1,0:T(8,128)S(1)}, u32[]{:S(2)}, u32[]{:S(2)}) async-start(f32[16,16,128]{2,1,0:T(8,128)} %get-tuple-element.18), calls=%async_computation.6 | async-start | bytes 262144 | tf_op jit(solution)/shard_map/all_to_all | solution.py:24
  191.4 28.4 %all-to-all-start.8 = ((bf16[16,8,1536]{2,1,0:T(8,128)(2,1)}), bf16[16,8,1536]{2,1,0:T(8,128)(2,1)S(1)}, u32[]{:S(2)}, u32[]{:S(2)}) async-start(bf16[16,8,1536]{2,1,0:T(8,128)(2,1)} %fusion), calls=%async_computation.8 | async-start | bytes 786432 | tf_op jit(solution)/shard_map/all_to_all | solution.py:24

commit v8 on v7

--- a/solution.py
+++ b/solution.py
@@ -1,3 +1,4 @@
+import functools
 import math
 
 import jax
@@ -16,8 +17,7 @@
 HIGHEST = lax.Precision.HIGHEST
 VMEM_LIMIT = 32 * 1024 * 1024
 BLOCK = 16
-SUBLANES = 8
-WORD_PIECES = 4
+SUBLANES, LANES = 8, 128
 
 
 def exchange(blocks, axis, groups=None):
@@ -35,18 +35,9 @@
     return terms
 
 
-def inverted(values):
-    guess = pl.reciprocal(values, approx=True)
-    for _ in range(2):
-        guess = guess * (2.0 - values * guess)
-    return guess
-
-
-def inverse_factor_kernel(*refs):
-    gram_ref, inverse_ref, work = refs[0], refs[-2], refs[-1]
-    size = gram_ref.shape[0]
+def eliminate(inverse_ref, work):
+    size = work.shape[0]
     whole, tile = (BLOCK, size), (SUBLANES, size)
-    work[...] = congruent(gram_ref[...], refs[1][...]) if len(refs) == 4 else gram_ref[...]
     lane = lax.broadcasted_iota(jnp.int32, whole, 1)
     row_at = lax.broadcasted_iota(jnp.int32, whole, 0)
     sublane = lax.broadcasted_iota(jnp.int32, tile, 0)
@@ -80,16 +71,12 @@
                 row = row - entry[j, k] * done[k]
             done.append(row)
             pivots.append(entry[j, j])
-            reciprocal = inverted(entry[j, j])
+            reciprocal = 1.0 / entry[j, j]
             reciprocals.append(reciprocal)
             factors = {i: entry[i, j] * reciprocal for i in range(j + 1, BLOCK)}
             for i in range(j + 1, BLOCK):
                 for k in range(j + 1, i + 1):
-                    if k == j + 1:
-                        change = (entry[i, j] * entry[k, j]) * reciprocal
-                    else:
-                        change = factors[i] * entry[k, j]
-                    entry[i, k] = entry[i, k] - change
+                    entry[i, k] = entry[i, k] - factors[i] * entry[k, j]
             for i in range(j + 1, BLOCK):
                 entry[i, j] = factors[i]
         block = spread(done)
@@ -107,6 +94,12 @@
     lax.fori_loop(0, size // BLOCK, step, 0)
 
 
+def inverse_factor_kernel(*refs):
+    work = refs[-1]
+    work[...] = refs[0][...] if len(refs) == 3 else congruent(refs[0][...], refs[1][...])
+    eliminate(refs[-2], work)
+
+
 def inverse_factor(gram_sum, *factor):
     return call(
         inverse_factor_kernel,
@@ -119,15 +112,24 @@
     )
 
 
-def call(
-    kernel, name, shapes, operands, scratch=(), specs=None, flops=10**7, moved=4 * 10**6
+def second_kernel(
+    root, col_ref, gram_ref, factor_ref, product_ref, own_ref, half_ref, inverse, work
 ):
+    work[...] = congruent(gram_ref[...], factor_ref[...])
+    eliminate(inverse, work)
+    half_ref[...] = apply_factor(product_ref[...], inverse[...]).astype(jnp.bfloat16)
+    own = own_ref.shape[0]
+    rows = product_ref[pl.ds(pl.multiple_of(col_ref[0] * own, own), own), :]
+    own_ref[...] = apply_factor(rows, inverse[...]) * root
+
+
+def call(kernel, name, shapes, operands, scratch=(), flops=10**7, moved=4 * 10**6):
     vmem = pl.BlockSpec(memory_space=pltpu.VMEM)
     smem = pl.BlockSpec(memory_space=pltpu.SMEM)
     return pl.pallas_call(
         kernel,
         out_shape=shapes,
-        in_specs=specs or [smem if operand.ndim == 1 else vmem for operand in operands],
+        in_specs=[smem if operand.ndim == 1 else vmem for operand in operands],
         out_specs=jax.tree.map(lambda _: vmem, shapes),
         scratch_shapes=scratch,
         compiler_params=pltpu.CompilerParams(vmem_limit_bytes=VMEM_LIMIT),
@@ -136,20 +138,14 @@
     )(*operands)
 
 
-def count_kernel(words_ref, spread_ref, kept_ref, arrived):
+def count_kernel(words_ref, spread_ref, kept_ref):
     rows, width = words_ref.shape
     step = 64
-    pieces = arrived.shape[0]
-    copies = []
-    for index in range(pieces):
-        span = pl.ds(index * (rows // pieces), rows // pieces)
-        copies.append(
-            pltpu.make_async_copy(words_ref.at[span, :], kept_ref.at[span, :], arrived.at[index])
-        )
-        copies[-1].start()
 
     def chunk(at, totals):
-        words = kept_ref[pl.ds(pl.multiple_of(at * step, step), step), :]
+        span = pl.ds(pl.multiple_of(at * step, step), step)
+        words = words_ref[span, :]
+        kept_ref[span, :] = words
         bits = [
             jnp.bitwise_and(jnp.right_shift(words, 2 * place + bit), 1)
             for bit in range(2)
@@ -161,11 +157,7 @@
         )
 
     zeros = jnp.zeros((8, width), jnp.int32)
-    totals = (zeros,) * (2 * PLACES)
-    steps = rows // step // pieces
-    for index, copy in enumerate(copies):
-        copy.wait()
-        totals = lax.fori_loop(index * steps, (index + 1) * steps, chunk, totals)
+    totals = lax.fori_loop(0, rows // step, chunk, (zeros,) * (2 * PLACES))
     shape = (COUNT_ROWS, width)
     sublane = lax.broadcasted_iota(jnp.int32, shape, 0)
     out = jnp.zeros(shape, jnp.float32)
@@ -186,18 +178,22 @@
     counts = counts + rows_all / 2
     ones, twos = counts[:PLACES], counts[PLACES : 2 * PLACES]
     mean = (ones + 2 * twos) / rows_all
-    scale = lax.rsqrt((ones + 4 * twos) / rows_all - mean * mean + EPSILON) * variant_ref[...]
-    step = 64
+    scale = lax.rsqrt((ones + 4 * twos) / rows_all - mean * mean + EPSILON)
+    lanes = variant_ref.shape[1]
+    step = weight_ref.shape[1]
 
     def chunk(at, carry):
         span = pl.ds(pl.multiple_of(at * step, step), step)
-        words = words_ref[span, :]
-        weight = jnp.broadcast_to(weight_ref[span, :], (step, width))
+        weight = jnp.broadcast_to(weight_ref[pl.ds(at, 1), :], (step, step)).T[:, :lanes]
         for place in range(PLACES):
-            across = slice(place * width, (place + 1) * width)
-            dosage = jnp.bitwise_and(jnp.right_shift(words, 2 * place), 3).astype(jnp.float32)
-            value = (dosage - mean[place : place + 1]) * scale[place : place + 1] * weight
-            matrix_ref[span, across] = value.astype(jnp.bfloat16)
+            for first in range(0, width, lanes):
+                column = place * width + first
+                words = words_ref[span, first : first + lanes]
+                dosage = jnp.bitwise_and(jnp.right_shift(words, 2 * place), 3).astype(jnp.float32)
+                at_place = (slice(place, place + 1), slice(first, first + lanes))
+                variant = variant_ref[column // lanes : column // lanes + 1, :]
+                value = (dosage - mean[at_place]) * (scale[at_place] * variant) * weight
+                matrix_ref[span, column : column + lanes] = value.astype(jnp.bfloat16)
         return carry
 
     lax.fori_loop(0, rows // step, chunk, 0)
@@ -207,13 +203,14 @@
     total = blocks_ref[0]
     for index in range(1, blocks_ref.shape[0]):
         total = total + blocks_ref[index]
+    total = total.astype(spread_ref.dtype)
     for index in range(spread_ref.shape[0]):
         spread_ref[index] = total
 
 
-def sum_spread(blocks, count=None):
+def sum_spread(blocks, count=None, kind=jnp.float32):
     rows, width = blocks.shape[1:]
-    shape = jax.ShapeDtypeStruct((count or blocks.shape[0], rows, width), jnp.float32)
+    shape = jax.ShapeDtypeStruct((count or blocks.shape[0], rows, width), kind)
     return call(sum_spread_kernel, "sum_spread", shape, (blocks,))
 
 
@@ -246,7 +243,7 @@
 
 
 def local_gram(panel):
-    return lax.dot_general(panel, panel, CONTRACT_ROWS, precision=HIGHEST)
+    return lax.dot_general(panel, panel, CONTRACT_ROWS, preferred_element_type=jnp.float32)
 
 
 def per_device(dosage_words, sample_weight, variant_weight, omega):
@@ -262,8 +259,6 @@
             jax.ShapeDtypeStruct((rows_local, width), jnp.int32),
         ),
         (dosage_words,),
-        scratch=[pltpu.SemaphoreType.DMA((WORD_PIECES,))],
-        specs=[pl.BlockSpec(memory_space=pltpu.HBM)],
     )
     matrix = call(
         standardize_kernel,
@@ -272,8 +267,8 @@
         (
             exchange(counts, "row"),
             words,
-            sample_weight[:, None],
-            variant_weight.reshape(PLACES, width),
+            sample_weight.reshape(-1, LANES),
+            variant_weight.reshape(-1, LANES),
         ),
     )
     col = lax.axis_index("col")
@@ -282,10 +277,10 @@
 
     sketch_part = jnp.dot(matrix, omega, preferred_element_type=jnp.float32)
     arrived = exchange(sketch_part.reshape(n_col, own, RANK), "col")
-    sketch = exchange(sum_spread(arrived), "col").reshape(rows_local, RANK)
+    sketch = exchange(sum_spread(arrived, kind=jnp.bfloat16), "col").reshape(rows_local, RANK)
 
     back_part = lax.dot_general(
-        matrix, sketch.astype(jnp.bfloat16), CONTRACT_ROWS, preferred_element_type=jnp.float32
+        matrix, sketch, CONTRACT_ROWS, preferred_element_type=jnp.float32
     ).astype(jnp.bfloat16)
     arrived = exchange(back_part.reshape(n_row, chunk, RANK), "row")
     gram_share = lax.dynamic_slice_in_dim(local_gram(sketch), col * part, part, 0)
@@ -303,8 +298,7 @@
     )
 
     product_part = jnp.dot(matrix, back, preferred_element_type=jnp.float32)
-    back_gram = lax.dot_general(back, back, CONTRACT_ROWS, preferred_element_type=jnp.float32)
-    back_gram = lax.optimization_barrier(back_gram)
+    back_gram = lax.optimization_barrier(local_gram(back))
     arrived = exchange(
         jnp.concatenate(
             [
@@ -335,20 +329,27 @@
     gathered = exchange(spread, "row")
     back_factor = inverse_factor(back_gram, sketch_factor)
     factor = jnp.dot(back_factor, sketch_factor, precision=HIGHEST)
-    right_full = apply_factor(back.astype(jnp.float32), factor)
+    right_basis = apply_factor(back.astype(jnp.float32), factor) * math.sqrt(cols_all)
     product = apply_factor(product, factor)
-    gathered, product = lax.optimization_barrier((gathered, product))
+    gathered, product, right_basis = lax.optimization_barrier((gathered, product, right_basis))
     near = [list(range(first, first + NEAR)) for first in range(0, n_col, NEAR)]
     gram = exchange(sum_spread(gathered, count=NEAR), "col", near).reshape(RANK, RANK)
-    second = apply_factor(product, inverse_factor(gram, factor))
-    second_own = lax.dynamic_slice_in_dim(second, col * own, own, 0)
-
+    basis, second = call(
+        functools.partial(second_kernel, math.sqrt(rows_all)),
+        "second",
+        (
+            jax.ShapeDtypeStruct((own, RANK), jnp.float32),
+            jax.ShapeDtypeStruct((rows_local, RANK), jnp.bfloat16),
+        ),
+        (col.reshape(1), gram, factor, product),
+        scratch=[pltpu.VMEM((RANK, RANK), jnp.float32)] * 2,
+    )
     projection_part = lax.dot_general(
-        second.astype(jnp.bfloat16), matrix, CONTRACT_ROWS, preferred_element_type=jnp.float32
+        second, matrix, CONTRACT_ROWS, preferred_element_type=jnp.float32
     ).astype(jnp.bfloat16)
     arrived = exchange(projection_part.reshape(n_row, RANK // n_row, -1), "row")
     projection = jnp.sum(arrived.astype(jnp.float32), axis=0).T
-    return (second_own * math.sqrt(rows_all), right_full * math.sqrt(cols_all), projection)
+    return (basis, right_basis, projection)
 
 
 def solution(mesh):

time: 221 us -> 225 us (1.018)
  the two profiles are of different devices: /device:TPU:64 before, /device:TPU:2 now
where the time goes in v8:
time: 225 us
  blocking collectives  138 us (61%)
  waiting for transfers between devices  39.3 us (17%)
  Pallas kernels  23.6 us (10%)
  starting transfers between devices  13.5 us (6%)
  matrix products  5.38 us (2%)
  local copies, waits for them, and re-layouts  2.62 us (1%)
    all_to_all x6, blocking collectives, exchange(): lax.all_to_all(blocks, axis, split_axis=0, concat_axis=0, axis_index_grou...  106 us
    all_to_all x3, waiting for transfers between devices, exchange(): lax.all_to_all(blocks, axis, split_axis=0, concat_axis=0, axis_index_grou...  39.3 us
    all_gather x1, blocking collectives, per_device(): gathered = lax.all_gather(back_own, 'row', axis=0, tiled=True)  32.4 us
    pallas_call x9, Pallas kernels, call(): pl.pallas_call(kernel, out_shape=shapes, in_specs=[smem if operand.ndim =...  23.6 us
    all_to_all x3, starting transfers between devices, exchange(): lax.all_to_all(blocks, axis, split_axis=0, concat_axis=0, axis_index_grou...  13.5 us
  transfers between devices with their start and end apart: 3, of which 3 were waited for; matrix products, arithmetic and copies ran while one was open for 1% of the time, Pallas kernels for 3%

profile of v8, /device:TPU:2, one launch (start us, length us, event | category | flops | bytes accessed | tf_op | source)
XLA Modules:
  0.0 224.6 jit_solution(16383884525982854916)
XLA Ops:
  0.6 0.0 copy-start
  0.6 0.0 copy-start.1
  0.7 1.1 copy-done.1
  1.7 0.7 count.1
  2.5 29.7 %all_to_all.45.counts_ref = bf16[16,16,256]{2,1,0:T(8,128)(2,1)S(1)} all-to-all(bf16[16,16,256]{2,1,0:T(8,128)(2,1)S(1)} %get-tuple-element.16), channel_id=1, replica_groups=mesh['row'=16,'col'=32] {'row'}, dimensions={0} | all-to-all | bytes 262144 | tf_op jit(solution)/shard_map/all_to_all | solution.py:24
  32.1 0.0 copy-start.2
  32.1 0.7 copy-done.2
  32.8 0.0 copy-start.3
  32.8 0.7 copy-done.3
  33.5 0.8 standardize.1
  34.3 0.0 copy-done
  34.3 0.6 fusion.4
  34.9 15.1 %all_to_all.46.blocks_ref = f32[32,16,128]{2,1,0:T(8,128)S(1)} all-to-all(f32[32,16,128]{2,1,0:T(8,128)S(1)} %bitcast.52), channel_id=1, replica_groups=mesh['row'=16,'col'=32] {'col'}, dimensions={0} | all-to-all | bytes 524288 | tf_op jit(solution)/shard_map/all_to_all | solution.py:24
  50.1 11.4 %all_to_all.47 = bf16[32,16,128]{2,1,0:T(8,128)(2,1)S(1)} all-to-all(bf16[32,16,128]{2,1,0:T(8,128)(2,1)S(1)} %sum_spread.3), channel_id=1, replica_groups=mesh['row'=16,'col'=32] {'col'}, dimensions={0} | all-to-all | bytes 262144 | tf_op jit(solution)/shard_map/all_to_all | solution.py:24
  61.5 1.4 convolution_convert_fusion.1
  62.8 3.8 %all-to-all-start.3 = ((bf16[16,96,128]{2,1,0:T(8,128)(2,1)}), bf16[16,96,128]{2,1,0:T(8,128)(2,1)S(1)}, u32[]{:S(2)}, u32[]{:S(2)}) async-start(bf16[16,96,128]{2,1,0:T(8,128)(2,1)} %bitcast.7), calls=%async_computation.3 | async-start | bytes 786432 | tf_op jit(solution)/shard_map/all_to_all | solution.py:24
  66.7 0.1 pad.8.clone
  66.8 0.2 convolution_bitcast_fusion.1
  67.0 0.1 maximum_maximum_fusion
  67.1 23.9 %all-to-all-done.3 = bf16[16,96,128]{2,1,0:T(8,128)(2,1)S(1)} async-done(((bf16[16,96,128]{2,1,0:T(8,128)(2,1)}), bf16[16,96,128]{2,1,0:T(8,128)(2,1)S(1)}, u32[]{:S(2)}, u32[]{:S(2)}) %all-to-all-start.3) | async-done | bytes 393248 | tf_op jit(solution)/shard_map/all_to_all | solution.py:24
  91.0 0.1 reduce_sum.30
  91.1 32.4 %all_gather.3 = bf16[1792,128]{1,0:T(8,128)(2,1)S(1)} all-gather(bf16[112,128]{1,0:T(8,128)(2,1)S(1)} %pad_maximum_fusion.1), channel_id=1, replica_groups=mesh['row'=16,'col'=32] {'row'}, dimensions={0}, use_global_device_ids=true | all-gather | bytes 487424 | tf_op jit(solution)/shard_map/all_gather | solution.py:293
  123.5 0.3 convolution_bitcast_fusion
  123.8 0.1 convert_reduce_fusion.1
  123.9 0.6 fusion.5
  124.6 13.5 %all_to_all.48.blocks_ref = f32[32,24,128]{2,1,0:T(8,128)S(1)} all-to-all(f32[32,24,128]{2,1,0:T(8,128)S(1)} %pad_maximum_fusion), channel_id=1, replica_groups=mesh['row'=16,'col'=32] {'col'}, dimensions={0} | all-to-all | bytes 786432 | tf_op jit(solution)/shard_map/all_to_all | solution.py:24
  138.0 0.8 sum_spread.4
  138.8 5.0 %all-to-all-start.5 = ((f32[32,24,128]{2,1,0:T(8,128)}), f32[32,24,128]{2,1,0:T(8,128)S(1)}, u32[]{:S(2)}, u32[]{:S(2)}) async-start(f32[32,24,128]{2,1,0:T(8,128)} %sum_spread.4), calls=%async_computation.5 | async-start | bytes 786432 | tf_op jit(solution)/shard_map/all_to_all | solution.py:24
  143.9 6.0 %inverse_factor.2.refs_1_ = f32[128,128]{1,0:T(8,128)S(1)} custom-call(f32[128,128]{1,0:T(8,128)S(1)} %bitcast.44), custom_call_target="tpu_custom_call" | custom-call | flops 4000000000 | bytes 30000000 | tf_op jit(solution)/shard_map/inverse_factor/pallas_call | solution.py:129
  149.9 3.1 %all-to-all-done.5.gathered_ref = f32[32,24,128]{2,1,0:T(8,128)S(1)} async-done(((f32[32,24,128]{2,1,0:T(8,128)}), f32[32,24,128]{2,1,0:T(8,128)S(1)}, u32[]{:S(2)}, u32[]{:S(2)}) %all-to-all-start.5) | async-done | bytes 393248 | tf_op jit(solution)/shard_map/all_to_all | solution.py:24
  153.0 1.1 product.1
  154.1 6.5 %inverse_factor.3 = f32[128,128]{1,0:T(8,128)S(1)} custom-call(f32[128,128]{1,0:T(8,128)S(1)} %bitcast.43, f32[128,128]{1,0:T(8,128)S(1)} %inverse_factor.2.refs_1_), custom_call_target="tpu_custom_call" | custom-call | flops 4000000000 | bytes 30000000 | tf_op jit(solution)/shard_map/inverse_factor/pallas_call | solution.py:129
  160.7 0.2 fusion.6.factor_ref
  160.9 4.7 %all-to-all-start.6 = ((f32[16,16,128]{2,1,0:T(8,128)}), f32[16,16,128]{2,1,0:T(8,128)S(1)}, u32[]{:S(2)}, u32[]{:S(2)}) async-start(f32[16,16,128]{2,1,0:T(8,128)} %get-tuple-element.21), calls=%async_computation.6 | async-start | bytes 262144 | tf_op jit(solution)/shard_map/all_to_all | solution.py:24
  165.6 0.4 fusion.7.product_ref
  166.0 1.4 convolution_multiply_fusion
  167.4 12.3 %all-to-all-done.6.blocks_ref = f32[16,16,128]{2,1,0:T(8,128)S(1)} async-done(((f32[16,16,128]{2,1,0:T(8,128)}), f32[16,16,128]{2,1,0:T(8,128)S(1)}, u32[]{:S(2)}, u32[]{:S(2)}) %all-to-all-start.6) | async-done | bytes 131104 | tf_op jit(solution)/shard_map/all_to_all | solution.py:24
  179.6 8.7 %all_to_all.49 = f32[8,16,128]{2,1,0:T(8,128)S(1)} all-to-all(f32[8,16,128]{2,1,0:T(8,128)S(1)} %sum_spread.5), channel_id=1, replica_groups={{0,1,2,3,4,5,6,7},{8,9,10,11,12,13,14,15},{16,17,18,19,20,21,22,23},{24..., dimensions={0} | all-to-all | bytes 131072 | tf_op jit(solution)/shard_map/all_to_all | solution.py:24
  188.3 7.6 %second.1 = (f32[16,128]{1,0:T(8,128)}, bf16[512,128]{1,0:T(8,128)(2,1)S(1)}) custom-call(s32[1]{0:T(128)} %bitcast.col_ref, f32[128,128]{1,0:T(8,128)S(1)} %bitcast.42, f32[128,128]{1,0:T(8,128)S(1)} %fusion.6.factor_ref, f32[512,128]{1,0:T(8,128)S(1)} %fusion.7.product_ref), custom_call_target="tpu_custom_call" | custom-call | flops 10000000 | bytes 4000000 | tf_op jit(solution)/shard_map/second/pallas_call | solution.py:129
  195.9 0.4 fusion
  196.3 27.6 %all_to_all.50 = bf16[16,8,1536]{2,1,0:T(8,128)(2,1)S(1)} all-to-all(bf16[16,8,1536]{2,1,0:T(8,128)(2,1)S(1)} %fusion), channel_id=1, replica_groups=mesh['row'=16,'col'=32] {'row'}, dimensions={0} | all-to-all | bytes 786432 | tf_op jit(solution)/shard_map/all_to_all | solution.py:24
  223.9 0.7 convert_reduce_fusion
  (11 shorter events, 0.2 us)
Async XLA Ops:
  0.6 33.7 %copy-start = (bf16[1536,128]{1,0:T(8,128)(2,1)S(1)}, bf16[1536,128]{1,0:T(8,128)(2,1)}, u32[]{:S(2)}) copy-start(bf16[1536,128]{1,0:T(8,128)(2,1)} %param.7) | copy-start | bytes 1179652
  0.6 1.1 copy-start.1
  32.1 0.7 copy-start.2
  32.8 0.7 copy-start.3
  62.8 28.2 %all-to-all-start.3 = ((bf16[16,96,128]{2,1,0:T(8,128)(2,1)}), bf16[16,96,128]{2,1,0:T(8,128)(2,1)S(1)}, u32[]{:S(2)}, u32[]{:S(2)}) async-start(bf16[16,96,128]{2,1,0:T(8,128)(2,1)} %bitcast.7), calls=%async_computation.3 | async-start | bytes 786432 | tf_op jit(solution)/shard_map/all_to_all | solution.py:24
  138.8 14.2 %all-to-all-start.5 = ((f32[32,24,128]{2,1,0:T(8,128)}), f32[32,24,128]{2,1,0:T(8,128)S(1)}, u32[]{:S(2)}, u32[]{:S(2)}) async-start(f32[32,24,128]{2,1,0:T(8,128)} %sum_spread.4), calls=%async_computation.5 | async-start | bytes 786432 | tf_op jit(solution)/shard_map/all_to_all | solution.py:24
  160.9 18.7 %all-to-all-start.6 = ((f32[16,16,128]{2,1,0:T(8,128)}), f32[16,16,128]{2,1,0:T(8,128)S(1)}, u32[]{:S(2)}, u32[]{:S(2)}) async-start(f32[16,16,128]{2,1,0:T(8,128)} %get-tuple-element.21), calls=%async_computation.6 | async-start | bytes 262144 | tf_op jit(solution)/shard_map/all_to_all | solution.py:24

commit v9 on v8

--- a/solution.py
+++ b/solution.py
@@ -94,22 +94,54 @@
     lax.fori_loop(0, size // BLOCK, step, 0)
 
 
-def inverse_factor_kernel(*refs):
-    work = refs[-1]
-    work[...] = refs[0][...] if len(refs) == 3 else congruent(refs[0][...], refs[1][...])
-    eliminate(refs[-2], work)
-
-
-def inverse_factor(gram_sum, *factor):
+def inverse_factor_kernel(gram_ref, inverse_ref, work):
+    work[...] = gram_ref[...]
+    eliminate(inverse_ref, work)
+
+
+def inverse_factor(gram_sum):
     return call(
         inverse_factor_kernel,
         "inverse_factor",
         jax.ShapeDtypeStruct(gram_sum.shape, jnp.float32),
-        (gram_sum, *factor),
+        (gram_sum,),
         scratch=[pltpu.VMEM(gram_sum.shape, jnp.float32)],
         flops=4 * 10**9,
         moved=3 * 10**7,
     )
+
+
+def back_factor_kernel(
+    root,
+    gram_ref,
+    sketch_factor_ref,
+    back_ref,
+    product_ref,
+    factor_ref,
+    right_ref,
+    scaled_ref,
+    inverse,
+    work,
+):
+    work[...] = congruent(gram_ref[...], sketch_factor_ref[...])
+    eliminate(inverse, work)
+    factor = lax.dot_general(
+        inverse[...],
+        sketch_factor_ref[...],
+        (((1,), (0,)), ((), ())),
+        precision=HIGHEST,
+        preferred_element_type=jnp.float32,
+    )
+    factor_ref[...] = factor
+    step = 256
+
+    def right_rows(at, carry):
+        span = pl.ds(pl.multiple_of(at * step, step), step)
+        right_ref[span, :] = apply_factor(back_ref[span, :].astype(jnp.float32), factor) * root
+        return carry
+
+    lax.fori_loop(0, back_ref.shape[0] // step, right_rows, 0)
+    scaled_ref[...] = apply_factor(product_ref[...], factor)
 
 
 def second_kernel(
@@ -138,7 +170,9 @@
     )(*operands)
 
 
-def count_kernel(words_ref, spread_ref, kept_ref):
+def count_kernel(words_ref, weight_ref, variant_ref, spread_ref, kept_ref, *kept):
+    kept[0][...] = weight_ref[...]
+    kept[1][...] = variant_ref[...]
     rows, width = words_ref.shape
     step = 64
 
@@ -251,25 +285,22 @@
     rows_all = rows_local * lax.axis_size("row")
     cols_all = PLACES * width * lax.axis_size("col")
     n_row, n_col = lax.axis_size("row"), lax.axis_size("col")
-    counts, words = call(
+    weights = (sample_weight.reshape(-1, LANES), variant_weight.reshape(-1, LANES))
+    counts, *kept = call(
         count_kernel,
         "count",
         (
             jax.ShapeDtypeStruct((n_row, COUNT_ROWS, width), jnp.bfloat16),
-            jax.ShapeDtypeStruct((rows_local, width), jnp.int32),
+            jax.ShapeDtypeStruct(dosage_words.shape, jnp.int32),
+            *(jax.ShapeDtypeStruct(weight.shape, jnp.float32) for weight in weights),
         ),
-        (dosage_words,),
+        (dosage_words, *weights),
     )
     matrix = call(
         standardize_kernel,
         "standardize",
         jax.ShapeDtypeStruct((rows_local, PLACES * width), jnp.bfloat16),
-        (
-            exchange(counts, "row"),
-            words,
-            sample_weight.reshape(-1, LANES),
-            variant_weight.reshape(-1, LANES),
-        ),
+        (exchange(counts, "row"), *kept),
     )
     col = lax.axis_index("col")
     own, part = rows_local // n_col, RANK // n_col
@@ -279,15 +310,15 @@
     arrived = exchange(sketch_part.reshape(n_col, own, RANK), "col")
     sketch = exchange(sum_spread(arrived, kind=jnp.bfloat16), "col").reshape(rows_local, RANK)
 
+    gram_share = lax.dynamic_slice_in_dim(local_gram(sketch), col * part, part, 0)
+    share_terms = jnp.concatenate(
+        halves(gram_share, 3) + [jnp.zeros((part, RANK), jnp.bfloat16)], axis=0
+    )
     back_part = lax.dot_general(
         matrix, sketch, CONTRACT_ROWS, preferred_element_type=jnp.float32
     ).astype(jnp.bfloat16)
+    back_part, share_terms = lax.optimization_barrier((back_part, share_terms))
     arrived = exchange(back_part.reshape(n_row, chunk, RANK), "row")
-    gram_share = lax.dynamic_slice_in_dim(local_gram(sketch), col * part, part, 0)
-    share_terms = jnp.concatenate(
-        halves(gram_share, 3) + [jnp.zeros((part, RANK), jnp.bfloat16)], axis=0
-    )
-    arrived, share_terms = lax.optimization_barrier((arrived, share_terms))
     back_own = jnp.sum(arrived.astype(jnp.float32), axis=0).astype(jnp.bfloat16)
     back_own = jnp.concatenate([back_own, share_terms], axis=0)
     gathered = lax.all_gather(back_own, "row", axis=0, tiled=True)
@@ -327,11 +358,20 @@
         scratch=[pltpu.VMEM((RANK, RANK), jnp.float32)],
     )
     gathered = exchange(spread, "row")
-    back_factor = inverse_factor(back_gram, sketch_factor)
-    factor = jnp.dot(back_factor, sketch_factor, precision=HIGHEST)
-    right_basis = apply_factor(back.astype(jnp.float32), factor) * math.sqrt(cols_all)
-    product = apply_factor(product, factor)
-    gathered, product, right_basis = lax.optimization_barrier((gathered, product, right_basis))
+    factor, right_basis, product = call(
+        functools.partial(back_factor_kernel, math.sqrt(cols_all)),
+        "back_factor",
+        (
+            jax.ShapeDtypeStruct((RANK, RANK), jnp.float32),
+            jax.ShapeDtypeStruct(back.shape, jnp.float32),
+            jax.ShapeDtypeStruct((rows_local, RANK), jnp.float32),
+        ),
+        (back_gram, sketch_factor, back, product),
+        scratch=[pltpu.VMEM((RANK, RANK), jnp.float32)] * 2,
+        flops=4 * 10**9,
+        moved=3 * 10**7,
+    )
+    gathered, product = lax.optimization_barrier((gathered, product))
     near = [list(range(first, first + NEAR)) for first in range(0, n_col, NEAR)]
     gram = exchange(sum_spread(gathered, count=NEAR), "col", near).reshape(RANK, RANK)
     basis, second = call(

time: 225 us -> 221 us (0.982)
  the two profiles are of different devices: /device:TPU:2 before, /device:TPU:64 now
where the time goes in v9:
time: 221 us; the launch traced here: 220 us
  blocking collectives  155 us (70%)
  Pallas kernels  27.1 us (12%)
  waiting for transfers between devices  16.7 us (8%)
  starting transfers between devices  15 us (7%)
  matrix products  2.67 us (1%)
  local copies, waits for them, and re-layouts  2.62 us (1%)
    all_to_all x6, blocking collectives, exchange(): lax.all_to_all(blocks, axis, split_axis=0, concat_axis=0, axis_index_grou...  122 us
    all_gather x1, blocking collectives, per_device(): gathered = lax.all_gather(back_own, 'row', axis=0, tiled=True)  32.5 us
    pallas_call x9, Pallas kernels, call(): pl.pallas_call(kernel, out_shape=shapes, in_specs=[smem if operand.ndim =...  27.1 us
    all_to_all x3, waiting for transfers between devices, exchange(): lax.all_to_all(blocks, axis, split_axis=0, concat_axis=0, axis_index_grou...  16.7 us
    all_to_all x3, starting transfers between devices, exchange(): lax.all_to_all(blocks, axis, split_axis=0, concat_axis=0, axis_index_grou...  15 us
  transfers between devices with their start and end apart: 3, of which 3 were waited for; matrix products, arithmetic and copies ran while one was open for 0% of the time, Pallas kernels for 7%

profile of v9, /device:TPU:64, one launch (start us, length us, event | category | flops | bytes accessed | tf_op | source)
XLA Modules:
  0.0 220.5 jit_solution(10284787243634885510)
XLA Ops:
  0.6 0.0 copy-start
  0.6 0.0 copy-start.1
  0.7 1.1 copy-done.1
  1.7 0.0 copy-start.2
  1.7 0.7 copy-done.2
  2.4 0.0 copy-start.3
  2.4 0.7 copy-done.3
  3.1 0.7 count.1
  3.8 28.0 %all_to_all.45.counts_ref = bf16[16,16,256]{2,1,0:T(8,128)(2,1)S(1)} all-to-all(bf16[16,16,256]{2,1,0:T(8,128)(2,1)S(1)} %get-tuple-element.20), channel_id=1, replica_groups=mesh['row'=16,'col'=32] {'row'}, dimensions={0} | all-to-all | bytes 262144 | tf_op jit(solution)/shard_map/all_to_all | solution.py:24
  31.9 0.8 standardize.1
  32.7 0.0 copy-done
  32.7 0.6 fusion.4
  33.2 16.0 %all_to_all.46.blocks_ref = f32[32,16,128]{2,1,0:T(8,128)S(1)} all-to-all(f32[32,16,128]{2,1,0:T(8,128)S(1)} %bitcast.47), channel_id=1, replica_groups=mesh['row'=16,'col'=32] {'col'}, dimensions={0} | all-to-all | bytes 524288 | tf_op jit(solution)/shard_map/all_to_all | solution.py:24
  49.3 0.7 sum_spread.3
  50.0 3.9 %all-to-all-start.2 = ((bf16[32,16,128]{2,1,0:T(8,128)(2,1)}), bf16[32,16,128]{2,1,0:T(8,128)(2,1)S(1)}, u32[]{:S(2)}, u32[]{:S(2)}) async-start(bf16[32,16,128]{2,1,0:T(8,128)(2,1)} %sum_spread.3), calls=%async_computation.2 | async-start | bytes 262144 | tf_op jit(solution)/shard_map/all_to_all | solution.py:24
  53.8 0.1 pad.8.clone
  53.9 7.7 %all-to-all-done.2 = bf16[32,16,128]{2,1,0:T(8,128)(2,1)S(1)} async-done(((bf16[32,16,128]{2,1,0:T(8,128)(2,1)}), bf16[32,16,128]{2,1,0:T(8,128)(2,1)S(1)}, u32[]{:S(2)}, u32[]{:S(2)}) %all-to-all-start.2) | async-done | bytes 131104 | tf_op jit(solution)/shard_map/all_to_all | solution.py:24
  61.6 0.6 convolution_convert_fusion.1
  62.3 0.2 convolution_bitcast_fusion.1
  62.5 0.1 maximum_maximum_fusion
  62.6 26.3 %all_to_all.47 = bf16[16,96,128]{2,1,0:T(8,128)(2,1)S(1)} all-to-all(bf16[16,96,128]{2,1,0:T(8,128)(2,1)S(1)} %bitcast.46), channel_id=1, replica_groups=mesh['row'=16,'col'=32] {'row'}, dimensions={0} | all-to-all | bytes 786432 | tf_op jit(solution)/shard_map/all_to_all | solution.py:24
  88.9 0.1 reduce_sum.30
  88.9 32.5 %all_gather.3 = bf16[1792,128]{1,0:T(8,128)(2,1)S(1)} all-gather(bf16[112,128]{1,0:T(8,128)(2,1)S(1)} %pad_maximum_fusion.1), channel_id=1, replica_groups=mesh['row'=16,'col'=32] {'row'}, dimensions={0}, use_global_device_ids=true | all-gather | bytes 487424 | tf_op jit(solution)/shard_map/all_gather | solution.py:324
  121.4 0.3 convolution_bitcast_fusion
  121.8 0.1 convert_reduce_fusion.1
  121.8 0.6 fusion.5
  122.5 13.8 %all_to_all.48.blocks_ref = f32[32,24,128]{2,1,0:T(8,128)S(1)} all-to-all(f32[32,24,128]{2,1,0:T(8,128)S(1)} %pad_maximum_fusion), channel_id=1, replica_groups=mesh['row'=16,'col'=32] {'col'}, dimensions={0} | all-to-all | bytes 786432 | tf_op jit(solution)/shard_map/all_to_all | solution.py:24
  136.3 0.8 sum_spread.4
  137.1 3.9 %all-to-all-start.5 = ((f32[32,24,128]{2,1,0:T(8,128)}), f32[32,24,128]{2,1,0:T(8,128)S(1)}, u32[]{:S(2)}, u32[]{:S(2)}) async-start(f32[32,24,128]{2,1,0:T(8,128)} %sum_spread.4), calls=%async_computation.5 | async-start | bytes 786432 | tf_op jit(solution)/shard_map/all_to_all | solution.py:24
  141.0 6.0 %inverse_factor.1.sketch_factor_ref = f32[128,128]{1,0:T(8,128)S(1)} custom-call(f32[128,128]{1,0:T(8,128)S(1)} %bitcast.40), custom_call_target="tpu_custom_call" | custom-call | flops 4000000000 | bytes 30000000 | tf_op jit(solution)/shard_map/inverse_factor/pallas_call | solution.py:161
  147.0 4.2 %all-to-all-done.5.gathered_ref = f32[32,24,128]{2,1,0:T(8,128)S(1)} async-done(((f32[32,24,128]{2,1,0:T(8,128)}), f32[32,24,128]{2,1,0:T(8,128)S(1)}, u32[]{:S(2)}, u32[]{:S(2)}) %all-to-all-start.5) | async-done | bytes 393248 | tf_op jit(solution)/shard_map/all_to_all | solution.py:24
  151.3 1.1 product.1
  152.4 7.2 %all-to-all-start.6 = ((f32[16,16,128]{2,1,0:T(8,128)}), f32[16,16,128]{2,1,0:T(8,128)S(1)}, u32[]{:S(2)}, u32[]{:S(2)}) async-start(f32[16,16,128]{2,1,0:T(8,128)} %get-tuple-element.27), calls=%async_computation.6 | async-start | bytes 262144 | tf_op jit(solution)/shard_map/all_to_all | solution.py:24
  159.6 9.4 %back_factor.1 = (f32[128,128]{1,0:T(8,128)S(1)}, f32[1536,128]{1,0:T(8,128)}, f32[512,128]{1,0:T(8,128)S(1)}) custom-call(f32[128,128]{1,0:T(8,128)S(1)} %bitcast.39, f32[128,128]{1,0:T(8,128)S(1)} %inverse_factor.1.sketch_factor_ref, bf16[1536,128]{1,0:T(8,128)(2,1)S(1)} %bitcast.37, f32[512,128]{1,0:T(8,128)S(1)} %get-tuple-element.29.product_ref), custom_call_target="tpu_custom_call" | custom-call | flops 4000000000 | bytes 30000000 | tf_op jit(solution)/shard_map/back_factor/pallas_call | solution.py:161
  169.0 4.8 %all-to-all-done.6.blocks_ref = f32[16,16,128]{2,1,0:T(8,128)S(1)} async-done(((f32[16,16,128]{2,1,0:T(8,128)}), f32[16,16,128]{2,1,0:T(8,128)S(1)}, u32[]{:S(2)}, u32[]{:S(2)}) %all-to-all-start.6) | async-done | bytes 131104 | tf_op jit(solution)/shard_map/all_to_all | solution.py:24
  173.8 8.0 %all_to_all.49 = f32[8,16,128]{2,1,0:T(8,128)S(1)} all-to-all(f32[8,16,128]{2,1,0:T(8,128)S(1)} %sum_spread.5), channel_id=1, replica_groups={{0,1,2,3,4,5,6,7},{8,9,10,11,12,13,14,15},{16,17,18,19,20,21,22,23},{24..., dimensions={0} | all-to-all | bytes 131072 | tf_op jit(solution)/shard_map/all_to_all | solution.py:24
  181.8 7.6 %second.1 = (f32[16,128]{1,0:T(8,128)}, bf16[512,128]{1,0:T(8,128)(2,1)S(1)}) custom-call(s32[1]{0:T(128)} %bitcast.col_ref, f32[128,128]{1,0:T(8,128)S(1)} %bitcast.38, f32[128,128]{1,0:T(8,128)S(1)} %get-tuple-element.32.factor_ref, f32[512,128]{1,0:T(8,128)S(1)} %get-tuple-element.33.product_ref), custom_call_target="tpu_custom_call" | custom-call | flops 10000000 | bytes 4000000 | tf_op jit(solution)/shard_map/second/pallas_call | solution.py:161
  189.4 0.4 fusion
  189.8 30.0 %all_to_all.50 = bf16[16,8,1536]{2,1,0:T(8,128)(2,1)S(1)} all-to-all(bf16[16,8,1536]{2,1,0:T(8,128)(2,1)S(1)} %fusion), channel_id=1, replica_groups=mesh['row'=16,'col'=32] {'row'}, dimensions={0} | all-to-all | bytes 786432 | tf_op jit(solution)/shard_map/all_to_all | solution.py:24
  219.8 0.7 convert_reduce_fusion
  (10 shorter events, 0.2 us)
Async XLA Ops:
  0.6 32.0 %copy-start = (bf16[1536,128]{1,0:T(8,128)(2,1)S(1)}, bf16[1536,128]{1,0:T(8,128)(2,1)}, u32[]{:S(2)}) copy-start(bf16[1536,128]{1,0:T(8,128)(2,1)} %param.7) | copy-start | bytes 1179652
  0.6 1.1 copy-start.1
  1.7 0.7 copy-start.2
  2.4 0.7 copy-start.3
  50.0 11.7 %all-to-all-start.2 = ((bf16[32,16,128]{2,1,0:T(8,128)(2,1)}), bf16[32,16,128]{2,1,0:T(8,128)(2,1)S(1)}, u32[]{:S(2)}, u32[]{:S(2)}) async-start(bf16[32,16,128]{2,1,0:T(8,128)(2,1)} %sum_spread.3), calls=%async_computation.2 | async-start | bytes 262144 | tf_op jit(solution)/shard_map/all_to_all | solution.py:24
  137.1 14.2 %all-to-all-start.5 = ((f32[32,24,128]{2,1,0:T(8,128)}), f32[32,24,128]{2,1,0:T(8,128)S(1)}, u32[]{:S(2)}, u32[]{:S(2)}) async-start(f32[32,24,128]{2,1,0:T(8,128)} %sum_spread.4), calls=%async_computation.5 | async-start | bytes 786432 | tf_op jit(solution)/shard_map/all_to_all | solution.py:24
  152.4 21.4 %all-to-all-start.6 = ((f32[16,16,128]{2,1,0:T(8,128)}), f32[16,16,128]{2,1,0:T(8,128)S(1)}, u32[]{:S(2)}, u32[]{:S(2)}) async-start(f32[16,16,128]{2,1,0:T(8,128)} %get-tuple-element.27), calls=%async_computation.6 | async-start | bytes 262144 | tf_op jit(solution)/shard_map/all_to_all | solution.py:24

commit v10 on v9

--- a/solution.py
+++ b/solution.py
@@ -26,13 +26,13 @@
     )
 
 
-def halves(values, count):
-    terms = []
+def terms(values, count):
+    parts = []
     for index in range(count):
         term = lax.reduce_precision(values, exponent_bits=8, mantissa_bits=7)
         values = values - term
-        terms.append(term.astype(jnp.bfloat16))
-    return terms
+        parts.append(term.astype(jnp.bfloat16))
+    return parts
 
 
 def eliminate(inverse_ref, work):
@@ -170,9 +170,7 @@
     )(*operands)
 
 
-def count_kernel(words_ref, weight_ref, variant_ref, spread_ref, kept_ref, *kept):
-    kept[0][...] = weight_ref[...]
-    kept[1][...] = variant_ref[...]
+def count_kernel(words_ref, spread_ref, kept_ref):
     rows, width = words_ref.shape
     step = 64
 
@@ -203,7 +201,7 @@
         spread_ref[index] = out
 
 
-def standardize_kernel(counts_ref, words_ref, weight_ref, variant_ref, matrix_ref):
+def standardize_kernel(counts_ref, words_ref, weights_ref, matrix_ref):
     rows, width = words_ref.shape
     rows_all = rows * counts_ref.shape[0]
     counts = counts_ref[0].astype(jnp.float32)
@@ -213,19 +211,19 @@
     ones, twos = counts[:PLACES], counts[PLACES : 2 * PLACES]
     mean = (ones + 2 * twos) / rows_all
     scale = lax.rsqrt((ones + 4 * twos) / rows_all - mean * mean + EPSILON)
-    lanes = variant_ref.shape[1]
-    step = weight_ref.shape[1]
+    step = lanes = weights_ref.shape[1]
 
     def chunk(at, carry):
         span = pl.ds(pl.multiple_of(at * step, step), step)
-        weight = jnp.broadcast_to(weight_ref[pl.ds(at, 1), :], (step, step)).T[:, :lanes]
+        weight = jnp.broadcast_to(weights_ref[pl.ds(at, 1), :], (step, lanes)).T
         for place in range(PLACES):
             for first in range(0, width, lanes):
                 column = place * width + first
                 words = words_ref[span, first : first + lanes]
                 dosage = jnp.bitwise_and(jnp.right_shift(words, 2 * place), 3).astype(jnp.float32)
                 at_place = (slice(place, place + 1), slice(first, first + lanes))
-                variant = variant_ref[column // lanes : column // lanes + 1, :]
+                variant_at = (rows + column) // lanes
+                variant = weights_ref[variant_at : variant_at + 1, :]
                 value = (dosage - mean[at_place]) * (scale[at_place] * variant) * weight
                 matrix_ref[span, column : column + lanes] = value.astype(jnp.bfloat16)
         return carry
@@ -285,22 +283,24 @@
     rows_all = rows_local * lax.axis_size("row")
     cols_all = PLACES * width * lax.axis_size("col")
     n_row, n_col = lax.axis_size("row"), lax.axis_size("col")
-    weights = (sample_weight.reshape(-1, LANES), variant_weight.reshape(-1, LANES))
-    counts, *kept = call(
+    weights = jnp.concatenate(
+        [sample_weight.reshape(-1, LANES), variant_weight.reshape(-1, LANES)], axis=0
+    )
+    dosage_words, weights = lax.optimization_barrier((dosage_words, weights))
+    counts, words = call(
         count_kernel,
         "count",
         (
             jax.ShapeDtypeStruct((n_row, COUNT_ROWS, width), jnp.bfloat16),
             jax.ShapeDtypeStruct(dosage_words.shape, jnp.int32),
-            *(jax.ShapeDtypeStruct(weight.shape, jnp.float32) for weight in weights),
-        ),
-        (dosage_words, *weights),
+        ),
+        (dosage_words,),
     )
     matrix = call(
         standardize_kernel,
         "standardize",
         jax.ShapeDtypeStruct((rows_local, PLACES * width), jnp.bfloat16),
-        (exchange(counts, "row"), *kept),
+        (exchange(counts, "row"), words, weights),
     )
     col = lax.axis_index("col")
     own, part = rows_local // n_col, RANK // n_col
@@ -311,9 +311,7 @@
     sketch = exchange(sum_spread(arrived, kind=jnp.bfloat16), "col").reshape(rows_local, RANK)
 
     gram_share = lax.dynamic_slice_in_dim(local_gram(sketch), col * part, part, 0)
-    share_terms = jnp.concatenate(
-        halves(gram_share, 3) + [jnp.zeros((part, RANK), jnp.bfloat16)], axis=0
-    )
+    share_terms = jnp.concatenate(terms(gram_share, 4), axis=0)
     back_part = lax.dot_general(
         matrix, sketch, CONTRACT_ROWS, preferred_element_type=jnp.float32
     ).astype(jnp.bfloat16)

time: 221 us -> 220 us (level)
  no operation moved by 1% of the time
where the time goes in v10:
time: 220 us
  blocking collectives  155 us (70%)
  Pallas kernels  27.1 us (12%)
  waiting for transfers between devices  16.8 us (8%)
  starting transfers between devices  15.1 us (7%)
  matrix products  2.68 us (1%)
    all_to_all x6, blocking collectives, exchange(): lax.all_to_all(blocks, axis, split_axis=0, concat_axis=0, axis_index_grou...  122 us
    all_gather x1, blocking collectives, per_device(): gathered = lax.all_gather(back_own, 'row', axis=0, tiled=True)  32.5 us
    pallas_call x9, Pallas kernels, call(): pl.pallas_call(kernel, out_shape=shapes, in_specs=[smem if operand.ndim =...  27.1 us
    all_to_all x3, waiting for transfers between devices, exchange(): lax.all_to_all(blocks, axis, split_axis=0, concat_axis=0, axis_index_grou...  16.8 us
    all_to_all x3, starting transfers between devices, exchange(): lax.all_to_all(blocks, axis, split_axis=0, concat_axis=0, axis_index_grou...  15.1 us
  transfers between devices with their start and end apart: 3, of which 3 were waited for; matrix products, arithmetic and copies ran while one was open for 0% of the time, Pallas kernels for 7%

profile of v10, /device:TPU:64, one launch (start us, length us, event | category | flops | bytes accessed | tf_op | source)
XLA Modules:
  0.0 219.8 jit_solution(8226249354198756320)
XLA Ops:
  0.6 0.0 copy-start
  0.6 0.8 pad_maximum_fusion.2.weights_ref
  1.4 0.0 copy-start.1
  1.4 1.0 copy-done.1
  2.4 0.7 count.1
  3.2 28.0 %all_to_all.45.counts_ref = bf16[16,16,256]{2,1,0:T(8,128)(2,1)S(1)} all-to-all(bf16[16,16,256]{2,1,0:T(8,128)(2,1)S(1)} %get-tuple-element.21), channel_id=1, replica_groups=mesh['row'=16,'col'=32] {'row'}, dimensions={0} | all-to-all | bytes 262144 | tf_op jit(solution)/shard_map/all_to_all | solution.py:24
  31.2 0.8 standardize.1
  32.0 0.0 copy-done
  32.0 0.6 fusion.4
  32.6 16.0 %all_to_all.46.blocks_ref = f32[32,16,128]{2,1,0:T(8,128)S(1)} all-to-all(f32[32,16,128]{2,1,0:T(8,128)S(1)} %bitcast.45), channel_id=1, replica_groups=mesh['row'=16,'col'=32] {'col'}, dimensions={0} | all-to-all | bytes 524288 | tf_op jit(solution)/shard_map/all_to_all | solution.py:24
  48.6 0.7 sum_spread.3
  49.3 3.9 %all-to-all-start.2 = ((bf16[32,16,128]{2,1,0:T(8,128)(2,1)}), bf16[32,16,128]{2,1,0:T(8,128)(2,1)S(1)}, u32[]{:S(2)}, u32[]{:S(2)}) async-start(bf16[32,16,128]{2,1,0:T(8,128)(2,1)} %sum_spread.3), calls=%async_computation.2 | async-start | bytes 262144 | tf_op jit(solution)/shard_map/all_to_all | solution.py:24
  53.2 7.8 %all-to-all-done.2 = bf16[32,16,128]{2,1,0:T(8,128)(2,1)S(1)} async-done(((bf16[32,16,128]{2,1,0:T(8,128)(2,1)}), bf16[32,16,128]{2,1,0:T(8,128)(2,1)S(1)}, u32[]{:S(2)}, u32[]{:S(2)}) %all-to-all-start.2) | async-done | bytes 131104 | tf_op jit(solution)/shard_map/all_to_all | solution.py:24
  61.0 0.6 convolution_convert_fusion.1
  61.6 0.2 convolution_bitcast_fusion.1
  61.8 26.3 %all_to_all.47 = bf16[16,96,128]{2,1,0:T(8,128)(2,1)S(1)} all-to-all(bf16[16,96,128]{2,1,0:T(8,128)(2,1)S(1)} %bitcast.44), channel_id=1, replica_groups=mesh['row'=16,'col'=32] {'row'}, dimensions={0} | all-to-all | bytes 786432 | tf_op jit(solution)/shard_map/all_to_all | solution.py:24
  88.1 0.1 reduce_sum.30
  88.2 32.5 %all_gather.3 = bf16[1792,128]{1,0:T(8,128)(2,1)S(1)} all-gather(bf16[112,128]{1,0:T(8,128)(2,1)S(1)} %pad_maximum_fusion.1), channel_id=1, replica_groups=mesh['row'=16,'col'=32] {'row'}, dimensions={0}, use_global_device_ids=true | all-gather | bytes 487424 | tf_op jit(solution)/shard_map/all_gather | solution.py:322
  120.7 0.3 convolution_bitcast_fusion
  121.0 0.1 convert_reduce_fusion.1
  121.1 0.6 fusion.5
  121.7 13.7 %all_to_all.48.blocks_ref = f32[32,24,128]{2,1,0:T(8,128)S(1)} all-to-all(f32[32,24,128]{2,1,0:T(8,128)S(1)} %pad_maximum_fusion), channel_id=1, replica_groups=mesh['row'=16,'col'=32] {'col'}, dimensions={0} | all-to-all | bytes 786432 | tf_op jit(solution)/shard_map/all_to_all | solution.py:24
  135.5 0.8 sum_spread.4
  136.3 3.9 %all-to-all-start.5 = ((f32[32,24,128]{2,1,0:T(8,128)}), f32[32,24,128]{2,1,0:T(8,128)S(1)}, u32[]{:S(2)}, u32[]{:S(2)}) async-start(f32[32,24,128]{2,1,0:T(8,128)} %sum_spread.4), calls=%async_computation.5 | async-start | bytes 786432 | tf_op jit(solution)/shard_map/all_to_all | solution.py:24
  140.2 6.0 %inverse_factor.1.sketch_factor_ref = f32[128,128]{1,0:T(8,128)S(1)} custom-call(f32[128,128]{1,0:T(8,128)S(1)} %bitcast.40), custom_call_target="tpu_custom_call" | custom-call | flops 4000000000 | bytes 30000000 | tf_op jit(solution)/shard_map/inverse_factor/pallas_call | solution.py:161
  146.2 4.2 %all-to-all-done.5.gathered_ref = f32[32,24,128]{2,1,0:T(8,128)S(1)} async-done(((f32[32,24,128]{2,1,0:T(8,128)}), f32[32,24,128]{2,1,0:T(8,128)S(1)}, u32[]{:S(2)}, u32[]{:S(2)}) %all-to-all-start.5) | async-done | bytes 393248 | tf_op jit(solution)/shard_map/all_to_all | solution.py:24
  150.5 1.1 product.1
  151.6 7.3 %all-to-all-start.6 = ((f32[16,16,128]{2,1,0:T(8,128)}), f32[16,16,128]{2,1,0:T(8,128)S(1)}, u32[]{:S(2)}, u32[]{:S(2)}) async-start(f32[16,16,128]{2,1,0:T(8,128)} %get-tuple-element.27), calls=%async_computation.6 | async-start | bytes 262144 | tf_op jit(solution)/shard_map/all_to_all | solution.py:24
  158.9 9.4 %back_factor.1 = (f32[128,128]{1,0:T(8,128)S(1)}, f32[1536,128]{1,0:T(8,128)}, f32[512,128]{1,0:T(8,128)S(1)}) custom-call(f32[128,128]{1,0:T(8,128)S(1)} %bitcast.39, f32[128,128]{1,0:T(8,128)S(1)} %inverse_factor.1.sketch_factor_ref, bf16[1536,128]{1,0:T(8,128)(2,1)S(1)} %bitcast.37, f32[512,128]{1,0:T(8,128)S(1)} %get-tuple-element.29.product_ref), custom_call_target="tpu_custom_call" | custom-call | flops 4000000000 | bytes 30000000 | tf_op jit(solution)/shard_map/back_factor/pallas_call | solution.py:161
  168.3 4.8 %all-to-all-done.6.blocks_ref = f32[16,16,128]{2,1,0:T(8,128)S(1)} async-done(((f32[16,16,128]{2,1,0:T(8,128)}), f32[16,16,128]{2,1,0:T(8,128)S(1)}, u32[]{:S(2)}, u32[]{:S(2)}) %all-to-all-start.6) | async-done | bytes 131104 | tf_op jit(solution)/shard_map/all_to_all | solution.py:24
  173.1 8.0 %all_to_all.49 = f32[8,16,128]{2,1,0:T(8,128)S(1)} all-to-all(f32[8,16,128]{2,1,0:T(8,128)S(1)} %sum_spread.5), channel_id=1, replica_groups={{0,1,2,3,4,5,6,7},{8,9,10,11,12,13,14,15},{16,17,18,19,20,21,22,23},{24..., dimensions={0} | all-to-all | bytes 131072 | tf_op jit(solution)/shard_map/all_to_all | solution.py:24
  181.1 7.6 %second.1 = (f32[16,128]{1,0:T(8,128)}, bf16[512,128]{1,0:T(8,128)(2,1)S(1)}) custom-call(s32[1]{0:T(128)} %bitcast.col_ref, f32[128,128]{1,0:T(8,128)S(1)} %bitcast.38, f32[128,128]{1,0:T(8,128)S(1)} %get-tuple-element.32.factor_ref, f32[512,128]{1,0:T(8,128)S(1)} %get-tuple-element.33.product_ref), custom_call_target="tpu_custom_call" | custom-call | flops 10000000 | bytes 4000000 | tf_op jit(solution)/shard_map/second/pallas_call | solution.py:161
  188.7 0.4 fusion
  189.1 30.0 %all_to_all.50 = bf16[16,8,1536]{2,1,0:T(8,128)(2,1)S(1)} all-to-all(bf16[16,8,1536]{2,1,0:T(8,128)(2,1)S(1)} %fusion), channel_id=1, replica_groups=mesh['row'=16,'col'=32] {'row'}, dimensions={0} | all-to-all | bytes 786432 | tf_op jit(solution)/shard_map/all_to_all | solution.py:24
  219.1 0.7 convert_reduce_fusion
  (10 shorter events, 0.2 us)
Async XLA Ops:
  0.6 31.4 %copy-start = (bf16[1536,128]{1,0:T(8,128)(2,1)S(1)}, bf16[1536,128]{1,0:T(8,128)(2,1)}, u32[]{:S(2)}) copy-start(bf16[1536,128]{1,0:T(8,128)(2,1)} %param.7) | copy-start | bytes 1179652
  1.4 1.0 copy-start.1
  49.3 11.7 %all-to-all-start.2 = ((bf16[32,16,128]{2,1,0:T(8,128)(2,1)}), bf16[32,16,128]{2,1,0:T(8,128)(2,1)S(1)}, u32[]{:S(2)}, u32[]{:S(2)}) async-start(bf16[32,16,128]{2,1,0:T(8,128)(2,1)} %sum_spread.3), calls=%async_computation.2 | async-start | bytes 262144 | tf_op jit(solution)/shard_map/all_to_all | solution.py:24
  136.3 14.2 %all-to-all-start.5 = ((f32[32,24,128]{2,1,0:T(8,128)}), f32[32,24,128]{2,1,0:T(8,128)S(1)}, u32[]{:S(2)}, u32[]{:S(2)}) async-start(f32[32,24,128]{2,1,0:T(8,128)} %sum_spread.4), calls=%async_computation.5 | async-start | bytes 786432 | tf_op jit(solution)/shard_map/all_to_all | solution.py:24
  151.6 21.5 %all-to-all-start.6 = ((f32[16,16,128]{2,1,0:T(8,128)}), f32[16,16,128]{2,1,0:T(8,128)S(1)}, u32[]{:S(2)}, u32[]{:S(2)}) async-start(f32[16,16,128]{2,1,0:T(8,128)} %get-tuple-element.27), calls=%async_computation.6 | async-start | bytes 262144 | tf_op jit(solution)/shard_map/all_to_all | solution.py:24

commit v11 on v10

--- a/solution.py
+++ b/solution.py
@@ -232,9 +232,9 @@
 
 
 def sum_spread_kernel(blocks_ref, spread_ref):
-    total = blocks_ref[0]
+    total = blocks_ref[0].astype(jnp.float32)
     for index in range(1, blocks_ref.shape[0]):
-        total = total + blocks_ref[index]
+        total = total + blocks_ref[index].astype(jnp.float32)
     total = total.astype(spread_ref.dtype)
     for index in range(spread_ref.shape[0]):
         spread_ref[index] = total
@@ -286,7 +286,8 @@
     weights = jnp.concatenate(
         [sample_weight.reshape(-1, LANES), variant_weight.reshape(-1, LANES)], axis=0
     )
-    dosage_words, weights = lax.optimization_barrier((dosage_words, weights))
+    share_at = (lax.axis_index("col") * (RANK // n_col)).astype(jnp.uint32)
+    dosage_words, weights, share_at = lax.optimization_barrier((dosage_words, weights, share_at))
     counts, words = call(
         count_kernel,
         "count",
@@ -306,11 +307,11 @@
     own, part = rows_local // n_col, RANK // n_col
     chunk = PLACES * width // n_row
 
-    sketch_part = jnp.dot(matrix, omega, preferred_element_type=jnp.float32)
+    sketch_part = jnp.dot(matrix, omega, preferred_element_type=jnp.float32).astype(jnp.bfloat16)
     arrived = exchange(sketch_part.reshape(n_col, own, RANK), "col")
     sketch = exchange(sum_spread(arrived, kind=jnp.bfloat16), "col").reshape(rows_local, RANK)
 
-    gram_share = lax.dynamic_slice_in_dim(local_gram(sketch), col * part, part, 0)
+    gram_share = lax.dynamic_slice_in_dim(local_gram(sketch), share_at, part, 0)
     share_terms = jnp.concatenate(terms(gram_share, 4), axis=0)
     back_part = lax.dot_general(
         matrix, sketch, CONTRACT_ROWS, preferred_element_type=jnp.float32

time: 220 us -> 218 us (level)
  blocking collectives: 155 us -> 165 us
  waiting for transfers between devices: 16.8 us -> 9.01 us
  starting transfers between devices: 15.1 us -> 11.2 us
    all_to_all x6 -> x7, blocking collectives: 122 us -> 132 us  [exchange(): lax.all_to_all(blocks, axis, split_axis=0, concat_axis=0, axis_index_grou...]
    all_to_all x3 -> x2, waiting for transfers between devices: 16.8 us -> 9.01 us  [exchange(): lax.all_to_all(blocks, axis, split_axis=0, concat_axis=0, axis_index_grou...]
    all_to_all x3 -> x2, starting transfers between devices: 15.1 us -> 11.2 us  [exchange(): lax.all_to_all(blocks, axis, split_axis=0, concat_axis=0, axis_index_grou...]
  transfers between devices with their start and end apart: 3 -> 2, of which waited for: 3 -> 2; matrix products, arithmetic and copies ran while one was open for 0% -> 0% of each run, Pallas kernels for 7% -> 7%
where the time goes in v11:
time: 218 us
  blocking collectives  165 us (76%)
  Pallas kernels  26.4 us (12%)
  starting transfers between devices  11.2 us (5%)
  waiting for transfers between devices  9.01 us (4%)
  matrix products  2.68 us (1%)
    all_to_all x7, blocking collectives, exchange(): lax.all_to_all(blocks, axis, split_axis=0, concat_axis=0, axis_index_grou...  132 us
    all_gather x1, blocking collectives, per_device(): gathered = lax.all_gather(back_own, 'row', axis=0, tiled=True)  32.5 us
    pallas_call x9, Pallas kernels, call(): pl.pallas_call(kernel, out_shape=shapes, in_specs=[smem if operand.ndim =...  26.4 us
    all_to_all x2, starting transfers between devices, exchange(): lax.all_to_all(blocks, axis, split_axis=0, concat_axis=0, axis_index_grou...  11.2 us
    all_to_all x2, waiting for transfers between devices, exchange(): lax.all_to_all(blocks, axis, split_axis=0, concat_axis=0, axis_index_grou...  9.01 us
  transfers between devices with their start and end apart: 2, of which 2 were waited for; matrix products, arithmetic and copies ran while one was open for 0% of the time, Pallas kernels for 7%

profile of v11, /device:TPU:64, one launch (start us, length us, event | category | flops | bytes accessed | tf_op | source)
XLA Modules:
  0.0 217.7 jit_solution(13891365757677812229)
XLA Ops:
  0.6 0.0 copy-start
  0.7 0.8 pad_maximum_fusion.2.weights_ref
  1.4 0.0 copy-start.1
  1.4 1.0 copy-done.1
  2.4 0.7 count.1
  3.2 28.0 %all_to_all.45.counts_ref = bf16[16,16,256]{2,1,0:T(8,128)(2,1)S(1)} all-to-all(bf16[16,16,256]{2,1,0:T(8,128)(2,1)S(1)} %get-tuple-element.22), channel_id=1, replica_groups=mesh['row'=16,'col'=32] {'row'}, dimensions={0} | all-to-all | bytes 262144 | tf_op jit(solution)/shard_map/all_to_all | solution.py:24
  31.2 0.8 standardize.1
  32.0 0.0 copy-done
  32.0 0.6 convolution_convert_fusion.2
  32.6 14.9 %all_to_all.46.blocks_ref = bf16[32,16,128]{2,1,0:T(8,128)(2,1)S(1)} all-to-all(bf16[32,16,128]{2,1,0:T(8,128)(2,1)S(1)} %bitcast.46), channel_id=1, replica_groups=mesh['row'=16,'col'=32] {'col'}, dimensions={0} | all-to-all | bytes 262144 | tf_op jit(solution)/shard_map/all_to_all | solution.py:24
  47.5 11.3 %all_to_all.47 = bf16[32,16,128]{2,1,0:T(8,128)(2,1)S(1)} all-to-all(bf16[32,16,128]{2,1,0:T(8,128)(2,1)S(1)} %sum_spread.3), channel_id=1, replica_groups=mesh['row'=16,'col'=32] {'col'}, dimensions={0} | all-to-all | bytes 262144 | tf_op jit(solution)/shard_map/all_to_all | solution.py:24
  58.8 0.6 convolution_convert_fusion.1
  59.4 0.2 convolution_bitcast_fusion.1
  59.7 26.3 %all_to_all.48 = bf16[16,96,128]{2,1,0:T(8,128)(2,1)S(1)} all-to-all(bf16[16,96,128]{2,1,0:T(8,128)(2,1)S(1)} %bitcast.44), channel_id=1, replica_groups=mesh['row'=16,'col'=32] {'row'}, dimensions={0} | all-to-all | bytes 786432 | tf_op jit(solution)/shard_map/all_to_all | solution.py:24
  86.0 0.1 reduce_sum.30
  86.1 32.5 %all_gather.3 = bf16[1792,128]{1,0:T(8,128)(2,1)S(1)} all-gather(bf16[112,128]{1,0:T(8,128)(2,1)S(1)} %pad_maximum_fusion.1), channel_id=1, replica_groups=mesh['row'=16,'col'=32] {'row'}, dimensions={0}, use_global_device_ids=true | all-gather | bytes 487424 | tf_op jit(solution)/shard_map/all_gather | solution.py:323
  118.5 0.3 convolution_bitcast_fusion
  118.9 0.1 convert_reduce_fusion.1
  119.0 0.6 fusion.4
  119.6 13.8 %all_to_all.49.blocks_ref = f32[32,24,128]{2,1,0:T(8,128)S(1)} all-to-all(f32[32,24,128]{2,1,0:T(8,128)S(1)} %pad_maximum_fusion), channel_id=1, replica_groups=mesh['row'=16,'col'=32] {'col'}, dimensions={0} | all-to-all | bytes 786432 | tf_op jit(solution)/shard_map/all_to_all | solution.py:24
  133.4 0.8 sum_spread.4
  134.2 3.9 %all-to-all-start.5 = ((f32[32,24,128]{2,1,0:T(8,128)}), f32[32,24,128]{2,1,0:T(8,128)S(1)}, u32[]{:S(2)}, u32[]{:S(2)}) async-start(f32[32,24,128]{2,1,0:T(8,128)} %sum_spread.4), calls=%async_computation.5 | async-start | bytes 786432 | tf_op jit(solution)/shard_map/all_to_all | solution.py:24
  138.1 6.0 %inverse_factor.1.sketch_factor_ref = f32[128,128]{1,0:T(8,128)S(1)} custom-call(f32[128,128]{1,0:T(8,128)S(1)} %bitcast.40), custom_call_target="tpu_custom_call" | custom-call | flops 4000000000 | bytes 30000000 | tf_op jit(solution)/shard_map/inverse_factor/pallas_call | solution.py:161
  144.1 4.2 %all-to-all-done.5.gathered_ref = f32[32,24,128]{2,1,0:T(8,128)S(1)} async-done(((f32[32,24,128]{2,1,0:T(8,128)}), f32[32,24,128]{2,1,0:T(8,128)S(1)}, u32[]{:S(2)}, u32[]{:S(2)}) %all-to-all-start.5) | async-done | bytes 393248 | tf_op jit(solution)/shard_map/all_to_all | solution.py:24
  148.4 1.1 product.1
  149.5 7.3 %all-to-all-start.6 = ((f32[16,16,128]{2,1,0:T(8,128)}), f32[16,16,128]{2,1,0:T(8,128)S(1)}, u32[]{:S(2)}, u32[]{:S(2)}) async-start(f32[16,16,128]{2,1,0:T(8,128)} %get-tuple-element.29), calls=%async_computation.6 | async-start | bytes 262144 | tf_op jit(solution)/shard_map/all_to_all | solution.py:24
  156.8 9.4 %back_factor.1 = (f32[128,128]{1,0:T(8,128)S(1)}, f32[1536,128]{1,0:T(8,128)}, f32[512,128]{1,0:T(8,128)S(1)}) custom-call(f32[128,128]{1,0:T(8,128)S(1)} %bitcast.39, f32[128,128]{1,0:T(8,128)S(1)} %inverse_factor.1.sketch_factor_ref, bf16[1536,128]{1,0:T(8,128)(2,1)S(1)} %bitcast.37, f32[512,128]{1,0:T(8,128)S(1)} %get-tuple-element.31.product_ref), custom_call_target="tpu_custom_call" | custom-call | flops 4000000000 | bytes 30000000 | tf_op jit(solution)/shard_map/back_factor/pallas_call | solution.py:161
  166.2 4.8 %all-to-all-done.6.blocks_ref = f32[16,16,128]{2,1,0:T(8,128)S(1)} async-done(((f32[16,16,128]{2,1,0:T(8,128)}), f32[16,16,128]{2,1,0:T(8,128)S(1)}, u32[]{:S(2)}, u32[]{:S(2)}) %all-to-all-start.6) | async-done | bytes 131104 | tf_op jit(solution)/shard_map/all_to_all | solution.py:24
  171.0 8.0 %all_to_all.50 = f32[8,16,128]{2,1,0:T(8,128)S(1)} all-to-all(f32[8,16,128]{2,1,0:T(8,128)S(1)} %sum_spread.5), channel_id=1, replica_groups={{0,1,2,3,4,5,6,7},{8,9,10,11,12,13,14,15},{16,17,18,19,20,21,22,23},{24..., dimensions={0} | all-to-all | bytes 131072 | tf_op jit(solution)/shard_map/all_to_all | solution.py:24
  179.0 7.6 %second.1 = (f32[16,128]{1,0:T(8,128)}, bf16[512,128]{1,0:T(8,128)(2,1)S(1)}) custom-call(s32[1]{0:T(128)} %bitcast.col_ref, f32[128,128]{1,0:T(8,128)S(1)} %bitcast.38, f32[128,128]{1,0:T(8,128)S(1)} %get-tuple-element.34.factor_ref, f32[512,128]{1,0:T(8,128)S(1)} %get-tuple-element.35.product_ref), custom_call_target="tpu_custom_call" | custom-call | flops 10000000 | bytes 4000000 | tf_op jit(solution)/shard_map/second/pallas_call | solution.py:161
  186.6 0.4 fusion
  187.0 30.0 %all_to_all.51 = bf16[16,8,1536]{2,1,0:T(8,128)(2,1)S(1)} all-to-all(bf16[16,8,1536]{2,1,0:T(8,128)(2,1)S(1)} %fusion), channel_id=1, replica_groups=mesh['row'=16,'col'=32] {'row'}, dimensions={0} | all-to-all | bytes 786432 | tf_op jit(solution)/shard_map/all_to_all | solution.py:24
  217.0 0.7 convert_reduce_fusion
  (11 shorter events, 0.2 us)
Async XLA Ops:
  0.6 31.4 %copy-start = (bf16[1536,128]{1,0:T(8,128)(2,1)S(1)}, bf16[1536,128]{1,0:T(8,128)(2,1)}, u32[]{:S(2)}) copy-start(bf16[1536,128]{1,0:T(8,128)(2,1)} %param.7) | copy-start | bytes 1179652
  1.4 1.0 copy-start.1
  134.2 14.2 %all-to-all-start.5 = ((f32[32,24,128]{2,1,0:T(8,128)}), f32[32,24,128]{2,1,0:T(8,128)S(1)}, u32[]{:S(2)}, u32[]{:S(2)}) async-start(f32[32,24,128]{2,1,0:T(8,128)} %sum_spread.4), calls=%async_computation.5 | async-start | bytes 786432 | tf_op jit(solution)/shard_map/all_to_all | solution.py:24
  149.5 21.5 %all-to-all-start.6 = ((f32[16,16,128]{2,1,0:T(8,128)}), f32[16,16,128]{2,1,0:T(8,128)S(1)}, u32[]{:S(2)}, u32[]{:S(2)}) async-start(f32[16,16,128]{2,1,0:T(8,128)} %get-tuple-element.29), calls=%async_computation.6 | async-start | bytes 262144 | tf_op jit(solution)/shard_map/all_to_all | solution.py:24

commit v12 on v11

--- a/solution.py
+++ b/solution.py
@@ -16,7 +16,7 @@
 CONTRACT_ROWS = (((0,), (0,)), ((), ()))
 HIGHEST = lax.Precision.HIGHEST
 VMEM_LIMIT = 32 * 1024 * 1024
-BLOCK = 16
+BLOCK = 32
 SUBLANES, LANES = 8, 128
 
 

time: 218 us -> 227 us (1.041)
  the two profiles are of different devices: /device:TPU:64 before, /device:TPU:8 now
where the time goes in v12:
time: 227 us; the launch traced here: 226 us
  blocking collectives  171 us (75%)
  Pallas kernels  36.7 us (16%)
  starting transfers between devices  10.4 us (5%)
  matrix products  2.68 us (1%)
    all_to_all x7, blocking collectives, exchange(): lax.all_to_all(blocks, axis, split_axis=0, concat_axis=0, axis_index_grou...  139 us
    pallas_call x9, Pallas kernels, call(): pl.pallas_call(kernel, out_shape=shapes, in_specs=[smem if operand.ndim =...  36.7 us
    all_gather x1, blocking collectives, per_device(): gathered = lax.all_gather(back_own, 'row', axis=0, tiled=True)  32.2 us
    all_to_all x2, starting transfers between devices, exchange(): lax.all_to_all(blocks, axis, split_axis=0, concat_axis=0, axis_index_grou...  10.4 us
  transfers between devices with their start and end apart: 2, of which 1 were waited for; matrix products, arithmetic and copies ran while one was open for 0% of the time, Pallas kernels for 10%

profile of v12, /device:TPU:8, one launch (start us, length us, event | category | flops | bytes accessed | tf_op | source)
XLA Modules:
  0.0 226.4 jit_solution(90850147086929602)
XLA Ops:
  0.6 0.0 copy-start
  0.7 0.8 pad_maximum_fusion.2.weights_ref
  1.4 0.0 copy-start.1
  1.4 1.0 copy-done.1
  2.4 0.7 count.1
  3.2 29.7 %all_to_all.45.counts_ref = bf16[16,16,256]{2,1,0:T(8,128)(2,1)S(1)} all-to-all(bf16[16,16,256]{2,1,0:T(8,128)(2,1)S(1)} %get-tuple-element.22), channel_id=1, replica_groups=mesh['row'=16,'col'=32] {'row'}, dimensions={0} | all-to-all | bytes 262144 | tf_op jit(solution)/shard_map/all_to_all | solution.py:24
  32.9 0.8 standardize.1
  33.7 0.0 copy-done
  33.7 0.6 convolution_convert_fusion.2
  34.2 13.9 %all_to_all.46.blocks_ref = bf16[32,16,128]{2,1,0:T(8,128)(2,1)S(1)} all-to-all(bf16[32,16,128]{2,1,0:T(8,128)(2,1)S(1)} %bitcast.46), channel_id=1, replica_groups=mesh['row'=16,'col'=32] {'col'}, dimensions={0} | all-to-all | bytes 262144 | tf_op jit(solution)/shard_map/all_to_all | solution.py:24
  48.2 11.3 %all_to_all.47 = bf16[32,16,128]{2,1,0:T(8,128)(2,1)S(1)} all-to-all(bf16[32,16,128]{2,1,0:T(8,128)(2,1)S(1)} %sum_spread.3), channel_id=1, replica_groups=mesh['row'=16,'col'=32] {'col'}, dimensions={0} | all-to-all | bytes 262144 | tf_op jit(solution)/shard_map/all_to_all | solution.py:24
  59.5 0.6 convolution_convert_fusion.1
  60.1 0.2 convolution_bitcast_fusion.1
  60.4 27.9 %all_to_all.48 = bf16[16,96,128]{2,1,0:T(8,128)(2,1)S(1)} all-to-all(bf16[16,96,128]{2,1,0:T(8,128)(2,1)S(1)} %bitcast.44), channel_id=1, replica_groups=mesh['row'=16,'col'=32] {'row'}, dimensions={0} | all-to-all | bytes 786432 | tf_op jit(solution)/shard_map/all_to_all | solution.py:24
  88.3 0.1 reduce_sum.30
  88.4 32.2 %all_gather.3 = bf16[1792,128]{1,0:T(8,128)(2,1)S(1)} all-gather(bf16[112,128]{1,0:T(8,128)(2,1)S(1)} %pad_maximum_fusion.1), channel_id=1, replica_groups=mesh['row'=16,'col'=32] {'row'}, dimensions={0}, use_global_device_ids=true | all-gather | bytes 487424 | tf_op jit(solution)/shard_map/all_gather | solution.py:323
  120.6 0.3 convolution_bitcast_fusion
  121.0 0.1 convert_reduce_fusion.1
  121.1 0.6 fusion.4
  121.7 13.1 %all_to_all.49.blocks_ref = f32[32,24,128]{2,1,0:T(8,128)S(1)} all-to-all(f32[32,24,128]{2,1,0:T(8,128)S(1)} %pad_maximum_fusion), channel_id=1, replica_groups=mesh['row'=16,'col'=32] {'col'}, dimensions={0} | all-to-all | bytes 786432 | tf_op jit(solution)/shard_map/all_to_all | solution.py:24
  134.8 0.8 sum_spread.4
  135.6 5.6 %all-to-all-start.5 = ((f32[32,24,128]{2,1,0:T(8,128)}), f32[32,24,128]{2,1,0:T(8,128)S(1)}, u32[]{:S(2)}, u32[]{:S(2)}) async-start(f32[32,24,128]{2,1,0:T(8,128)} %sum_spread.4), calls=%async_computation.5 | async-start | bytes 786432 | tf_op jit(solution)/shard_map/all_to_all | solution.py:24
  141.2 9.3 %inverse_factor.1.sketch_factor_ref = f32[128,128]{1,0:T(8,128)S(1)} custom-call(f32[128,128]{1,0:T(8,128)S(1)} %bitcast.40), custom_call_target="tpu_custom_call" | custom-call | flops 4000000000 | bytes 30000000 | tf_op jit(solution)/shard_map/inverse_factor/pallas_call | solution.py:161
  150.5 0.0 all-to-all-done.5.gathered_ref
  150.5 1.1 product.1
  151.6 4.8 %all-to-all-start.6 = ((f32[16,16,128]{2,1,0:T(8,128)}), f32[16,16,128]{2,1,0:T(8,128)S(1)}, u32[]{:S(2)}, u32[]{:S(2)}) async-start(f32[16,16,128]{2,1,0:T(8,128)} %get-tuple-element.29), calls=%async_computation.6 | async-start | bytes 262144 | tf_op jit(solution)/shard_map/all_to_all | solution.py:24
  156.4 12.8 %back_factor.1 = (f32[128,128]{1,0:T(8,128)S(1)}, f32[1536,128]{1,0:T(8,128)}, f32[512,128]{1,0:T(8,128)S(1)}) custom-call(f32[128,128]{1,0:T(8,128)S(1)} %bitcast.39, f32[128,128]{1,0:T(8,128)S(1)} %inverse_factor.1.sketch_factor_ref, bf16[1536,128]{1,0:T(8,128)(2,1)S(1)} %bitcast.37, f32[512,128]{1,0:T(8,128)S(1)} %get-tuple-element.31.product_ref), custom_call_target="tpu_custom_call" | custom-call | flops 4000000000 | bytes 30000000 | tf_op jit(solution)/shard_map/back_factor/pallas_call | solution.py:161
  169.3 1.9 all-to-all-done.6.blocks_ref
  171.2 9.7 %all_to_all.50 = f32[8,16,128]{2,1,0:T(8,128)S(1)} all-to-all(f32[8,16,128]{2,1,0:T(8,128)S(1)} %sum_spread.5), channel_id=1, replica_groups={{0,1,2,3,4,5,6,7},{8,9,10,11,12,13,14,15},{16,17,18,19,20,21,22,23},{24..., dimensions={0} | all-to-all | bytes 131072 | tf_op jit(solution)/shard_map/all_to_all | solution.py:24
  180.9 11.1 %second.1 = (f32[16,128]{1,0:T(8,128)}, bf16[512,128]{1,0:T(8,128)(2,1)S(1)}) custom-call(s32[1]{0:T(128)} %bitcast.col_ref, f32[128,128]{1,0:T(8,128)S(1)} %bitcast.38, f32[128,128]{1,0:T(8,128)S(1)} %get-tuple-element.34.factor_ref, f32[512,128]{1,0:T(8,128)S(1)} %get-tuple-element.35.product_ref), custom_call_target="tpu_custom_call" | custom-call | flops 10000000 | bytes 4000000 | tf_op jit(solution)/shard_map/second/pallas_call | solution.py:161
  192.0 0.4 fusion
  192.4 33.4 %all_to_all.51 = bf16[16,8,1536]{2,1,0:T(8,128)(2,1)S(1)} all-to-all(bf16[16,8,1536]{2,1,0:T(8,128)(2,1)S(1)} %fusion), channel_id=1, replica_groups=mesh['row'=16,'col'=32] {'row'}, dimensions={0} | all-to-all | bytes 786432 | tf_op jit(solution)/shard_map/all_to_all | solution.py:24
  225.7 0.7 convert_reduce_fusion
  (11 shorter events, 0.2 us)
Async XLA Ops:
  0.6 33.0 %copy-start = (bf16[1536,128]{1,0:T(8,128)(2,1)S(1)}, bf16[1536,128]{1,0:T(8,128)(2,1)}, u32[]{:S(2)}) copy-start(bf16[1536,128]{1,0:T(8,128)(2,1)} %param.7) | copy-start | bytes 1179652
  1.4 1.0 copy-start.1
  135.6 14.9 %all-to-all-start.5 = ((f32[32,24,128]{2,1,0:T(8,128)}), f32[32,24,128]{2,1,0:T(8,128)S(1)}, u32[]{:S(2)}, u32[]{:S(2)}) async-start(f32[32,24,128]{2,1,0:T(8,128)} %sum_spread.4), calls=%async_computation.5 | async-start | bytes 786432 | tf_op jit(solution)/shard_map/all_to_all | solution.py:24
  151.6 19.6 %all-to-all-start.6 = ((f32[16,16,128]{2,1,0:T(8,128)}), f32[16,16,128]{2,1,0:T(8,128)S(1)}, u32[]{:S(2)}, u32[]{:S(2)}) async-start(f32[16,16,128]{2,1,0:T(8,128)} %get-tuple-element.29), calls=%async_computation.6 | async-start | bytes 262144 | tf_op jit(solution)/shard_map/all_to_all | solution.py:24
